TPU v7x, 32 devices: a whole 2x2x4 slice. The times are simulated.
32 devices in a mesh: ulysses: 4 (over x, core), blk: 8 (over z, y).
Axes of the slice: x: 2, y: 2, z: 4, core: 2. Of those that a mesh axis runs over, the one named last changes fastest.
Arguments:
- tokens: bfloat16 [2048, 2, 2048], P(('ulysses', 'blk')), may hold values from -6 to 6
- w_query: bfloat16 [2048, 2048], P(('ulysses', 'blk')), may hold values from -0.125 to 0.125
- w_key: bfloat16 [2048, 2048], P(('ulysses', 'blk')), may hold values from -0.125 to 0.125
- w_value: bfloat16 [2048, 2048], P(('ulysses', 'blk')), may hold values from -0.125 to 0.125
- w_out: bfloat16 [2048, 2048], P(('ulysses', 'blk')), may hold values from -0.75 to 0.75
- attn_gain: bfloat16 [2048], P(('ulysses', 'blk')), may hold values from 0.5 to 1.5
- ffn_gain: bfloat16 [2048], P(('ulysses', 'blk')), may hold values from 0.5 to 1.5
- qk_gain: bfloat16 [2, 128], P(None, ('ulysses', 'blk')), may hold values from 1.1953125 to 1.796875
- expert_gate: bfloat16 [64, 2048, 1024], P('blk', None, 'ulysses'), may hold values from -0.125 to 0.125
- expert_up: bfloat16 [64, 2048, 1024], P('blk', None, 'ulysses'), may hold values from -0.125 to 0.125
- expert_down: bfloat16 [64, 1024, 2048], P('blk', 'ulysses'), may hold values from -0.1875 to 0.1875
- routes: int32 [2048, 2, 8], P(('ulysses', 'blk')), may hold values from 0 to 63, all different within a row
- gates: float32 [2048, 2, 8], P(('ulysses', 'blk')), may hold values from 0.2 to 0.6
- order: int32 [32, 1024], P(('ulysses', 'blk')), may hold values from 0 to 1023, each once within a row
- cotangent: bfloat16 [2048, 2, 2048], P(('ulysses', 'blk')), may hold values from -6 to 6
Outputs:
- mixed: bfloat16 [2048, 2, 2048], P(('ulysses', 'blk'))
- input_grad: float32 [2048, 2, 2048], P(('ulysses', 'blk'))
- query_grad: float32 [2048, 2048], P(('ulysses', 'blk'))
- key_grad: float32 [2048, 2048], P(('ulysses', 'blk'))
- value_grad: float32 [2048, 2048], P(('ulysses', 'blk'))
- out_grad: float32 [2048, 2048], P(('ulysses', 'blk'))
- attn_gain_grad: float32 [2048], P(('ulysses', 'blk'))
- ffn_gain_grad: float32 [2048], P(('ulysses', 'blk'))
- qk_gain_grad: float32 [2, 128], P(None, ('ulysses', 'blk'))
- gate_grad: float32 [64, 2048, 1024], P('blk', None, 'ulysses')
- up_grad: float32 [64, 2048, 1024], P('blk', None, 'ulysses')
- down_grad: float32 [64, 1024, 2048], P('blk', 'ulysses')
Inputs may be any that keep to these rules, and one draw needn't show every extreme that they name: `routes`: each token names 8 different experts, and every expert is named by some token. `order`: each row holds every number of its range once.
All inputs are finite; a program needn't handle non-finite values.
Results may differ from a plain program's by a relative error of at most 0.02.
Values may be sent and summed in bfloat16 or wider, within the bound.
A program may use at most 576 MiB of HBM per device.

v0:
```python
import math

import jax
import jax.numpy as jnp
from jax import lax
from jax.sharding import PartitionSpec as P

HD = 128
CAP = 18


EPSILON = 1e-06
ROPE_BASE = 10000.0


def shifted(value, axis, by):
    devices = lax.axis_size(axis)
    return lax.ppermute(value, axis, [(i, (i + by) % devices) for i in range(devices)])


def rms_norm(values, gains):
    return values * lax.rsqrt(jnp.mean(values * values, axis=-1, keepdims=True) + EPSILON) * gains


def rotate(values, positions):
    half_size = values.shape[-1] // 2
    inverse = ROPE_BASE ** (-2.0 * jnp.arange(half_size).astype(jnp.float32) / values.shape[-1])
    angles = positions[:, None] * inverse[None, :]
    cosine = jnp.cos(angles)[:, None, None, :]
    sine = jnp.sin(angles)[:, None, None, :]
    first_half = values[..., :half_size]
    second_half = values[..., half_size:]
    return jnp.concatenate(
        [first_half * cosine - second_half * sine, second_half * cosine + first_half * sine],
        axis=-1,
    )


def body(
    tokens,
    w_query,
    w_key,
    w_value,
    w_out,
    attn_gain,
    ffn_gain,
    qk_gain,
    expert_gate,
    expert_up,
    expert_down,
    routes,
    gates,
    order,
    cotangent,
):
    seq_rows, seq_count, width = tokens.shape
    uly_count = lax.axis_size("ulysses")
    blk_count = lax.axis_size("blk")
    head_count = w_query.shape[1] // HD
    local_heads = head_count // uly_count
    head_shape = (seq_rows, seq_count, head_count, HD)
    score_scale = 1.0 / math.sqrt(HD)
    flat_index = lax.axis_index("ulysses") * blk_count + lax.axis_index("blk")
    positions = (flat_index * seq_rows + jnp.arange(seq_rows, dtype=jnp.int32)).astype(jnp.float32)

    def gather_weights():
        return (
            lax.all_gather(w_query, ("ulysses", "blk"), axis=0, tiled=True),
            lax.all_gather(w_key, ("ulysses", "blk"), axis=0, tiled=True),
            lax.all_gather(w_value, ("ulysses", "blk"), axis=0, tiled=True),
            lax.all_gather(w_out, ("ulysses", "blk"), axis=0, tiled=True),
            lax.all_gather(attn_gain, ("ulysses", "blk"), axis=0, tiled=True),
            lax.all_gather(ffn_gain, ("ulysses", "blk"), axis=0, tiled=True),
            lax.all_gather(qk_gain, ("ulysses", "blk"), axis=1, tiled=True),
        )

    gathered = gather_weights()
    query_w, key_w, value_w, out_w = (gathered[0], gathered[1], gathered[2], gathered[3])
    token_float = tokens.astype(jnp.float32)
    hidden_full, attn_norm_back = jax.vjp(rms_norm, token_float, gathered[4].astype(jnp.float32))
    hidden = hidden_full.astype(jnp.bfloat16).reshape(-1, width)
    query_raw = jnp.dot(hidden, query_w, preferred_element_type=jnp.float32).reshape(head_shape)
    key_raw = jnp.dot(hidden, key_w, preferred_element_type=jnp.float32).reshape(head_shape)
    value_heads = (
        jnp.dot(hidden, value_w, preferred_element_type=jnp.float32)
        .astype(jnp.bfloat16)
        .reshape(head_shape)
    )

    def head_norms(query_in, key_in, head_gains):
        return (
            rotate(rms_norm(query_in, head_gains[0]), positions),
            rotate(rms_norm(key_in, head_gains[1]), positions),
        )

    rotated, heads_back = jax.vjp(head_norms, query_raw, key_raw, gathered[6].astype(jnp.float32))
    query_grp, key_grp, value_grp = (
        lax.all_to_all(
            rotated[0].astype(jnp.bfloat16), "ulysses", split_axis=2, concat_axis=0, tiled=True
        ),
        lax.all_to_all(
            rotated[1].astype(jnp.bfloat16), "ulysses", split_axis=2, concat_axis=0, tiled=True
        ),
        lax.all_to_all(value_heads, "ulysses", split_axis=2, concat_axis=0, tiled=True),
    )
    query_rows = query_grp.shape[0]

    def attend_block(state, key_part, value_part):
        running_max, running_sum, accum = state
        scores = (
            jnp.einsum("qshd,kshd->qshk", query_grp, key_part, preferred_element_type=jnp.float32)
            * score_scale
        )
        new_max = jnp.maximum(running_max, jnp.max(scores, axis=-1))
        shrink = jnp.exp(running_max - new_max)
        weights = jnp.exp(scores - new_max[..., None])
        running_sum = running_sum * shrink + jnp.sum(weights, axis=-1)
        accum = accum * shrink[..., None] + jnp.einsum(
            "qshk,kshd->qshd",
            weights.astype(jnp.bfloat16),
            value_part,
            preferred_element_type=jnp.float32,
        )
        return (new_max, running_sum, accum)

    start_state = (
        jnp.full((query_rows, seq_count, local_heads), -1e30, jnp.float32),
        jnp.zeros((query_rows, seq_count, local_heads), jnp.float32),
        jnp.zeros((query_rows, seq_count, local_heads, HD), jnp.float32),
    )
    state = start_state
    key_part = lax.all_gather(key_grp, "blk", axis=0, tiled=True)
    value_part = lax.all_gather(value_grp, "blk", axis=0, tiled=True)
    row_count = key_part.shape[0]

    def inner_step(carry, parts):
        return (attend_block(carry, parts[0], parts[1]), None)

    new_shape = (row_count // 512, 512) + key_part.shape[1:]
    state, unused = lax.scan(
        inner_step, state, (key_part.reshape(new_shape), value_part.reshape(new_shape))
    )
    final_max, final_sum, final_acc = state
    attended_float = final_acc / final_sum[..., None]
    attended_heads = attended_float.astype(jnp.bfloat16)
    log_total = final_max + jnp.log(final_sum)
    attended_tokens = lax.all_to_all(
        attended_heads, "ulysses", split_axis=0, concat_axis=2, tiled=True
    )
    attended_rows = attended_tokens.reshape(-1, head_count * HD)
    residual = token_float.reshape(-1, width) + jnp.dot(
        attended_rows, out_w, preferred_element_type=jnp.float32
    )
    normed_full, ffn_norm_back = jax.vjp(rms_norm, residual, gathered[5].astype(jnp.float32))
    normed = normed_full.astype(jnp.bfloat16)
    top_count = routes.shape[-1]
    exp_local = expert_gate.shape[0]
    expert_total = exp_local * blk_count
    route_flat = routes.reshape(-1)
    prio_flat = order.reshape(-1)
    pair_total = route_flat.shape[0]
    same_expert = route_flat[:, None] == route_flat[None, :]
    earlier = prio_flat[None, :] < prio_flat[:, None]
    ranks = jnp.sum((same_expert & earlier).astype(jnp.int32), axis=1)
    kept = ranks < CAP
    slots = jnp.where(kept, route_flat * CAP + ranks, expert_total * CAP)
    token_of = jnp.arange(pair_total, dtype=jnp.int32) // top_count
    weight_of = jnp.where(kept, gates.reshape(-1), 0.0)

    def slot_buffer(pair_rows):
        buffer = (
            jnp.zeros((expert_total * CAP, width), pair_rows.dtype)
            .at[slots]
            .set(pair_rows, mode="drop")
        )
        return buffer.reshape(blk_count, exp_local, CAP, width)

    def spread(pair_rows):
        buffer = slot_buffer(pair_rows).reshape(1, blk_count, exp_local, CAP, width)
        return jnp.broadcast_to(buffer, (uly_count, blk_count, exp_local, CAP, width)).reshape(
            uly_count * blk_count, exp_local, CAP, width
        )

    received = lax.all_to_all(
        spread(normed[token_of]), ("ulysses", "blk"), split_axis=0, concat_axis=0, tiled=True
    )
    gate_act = jnp.einsum(
        "necd,edf->necf", received, expert_gate, preferred_element_type=jnp.float32
    )
    up_act = jnp.einsum("necd,edf->necf", received, expert_up, preferred_element_type=jnp.float32)
    sigma = jax.nn.sigmoid(gate_act)
    inner = (gate_act * sigma * up_act).astype(jnp.bfloat16)
    partial_value = jnp.einsum(
        "necf,efd->necd", inner, expert_down, preferred_element_type=jnp.float32
    ).astype(jnp.bfloat16)
    returned = lax.all_to_all(
        partial_value, ("ulysses", "blk"), split_axis=0, concat_axis=0, tiled=True
    )
    combined = jnp.sum(
        returned.reshape(uly_count, expert_total * CAP, width).astype(jnp.float32), axis=0
    )
    picked = jnp.take(combined, slots, axis=0, mode="fill", fill_value=0.0)
    expert_sum = jnp.sum((picked * weight_of[:, None]).reshape(-1, top_count, width), axis=1)
    mixed = (residual + expert_sum).reshape(seq_rows, seq_count, width).astype(jnp.bfloat16)
    grad_out = cotangent.astype(jnp.float32).reshape(-1, width)
    pair_grad = (grad_out[token_of] * weight_of[:, None]).astype(jnp.bfloat16)
    grad_sent = lax.all_to_all(
        spread(pair_grad), ("ulysses", "blk"), split_axis=0, concat_axis=0, tiled=True
    )
    inner_grad = jnp.einsum(
        "necd,efd->necf", grad_sent, expert_down, preferred_element_type=jnp.float32
    )
    gate_act_grad = (inner_grad * up_act * sigma * (1.0 + gate_act * (1.0 - sigma))).astype(
        jnp.bfloat16
    )
    up_act_grad = (inner_grad * gate_act * sigma).astype(jnp.bfloat16)
    row_grads = jnp.einsum(
        "necf,edf->necd", gate_act_grad, expert_gate, preferred_element_type=jnp.float32
    ) + jnp.einsum("necf,edf->necd", up_act_grad, expert_up, preferred_element_type=jnp.float32)
    gate_grad = jnp.einsum(
        "necd,necf->edf", received, gate_act_grad, preferred_element_type=jnp.float32
    )
    up_grad = jnp.einsum(
        "necd,necf->edf", received, up_act_grad, preferred_element_type=jnp.float32
    )
    down_grad = jnp.einsum("necf,necd->efd", inner, grad_sent, preferred_element_type=jnp.float32)
    back_rows = lax.all_to_all(
        row_grads.astype(jnp.bfloat16), ("ulysses", "blk"), split_axis=0, concat_axis=0, tiled=True
    ).astype(row_grads.dtype)
    grad_buffer = jnp.sum(back_rows.reshape(uly_count, expert_total * CAP, width), axis=0)
    normed_grad = jnp.sum(
        jnp.take(grad_buffer, slots, axis=0, mode="fill", fill_value=0.0).reshape(
            -1, top_count, width
        ),
        axis=1,
    )
    residual_norm_grad, ffn_gain_part = ffn_norm_back(normed_grad)
    residual_grad = grad_out + residual_norm_grad
    attn_out_grad = residual_grad.astype(jnp.bfloat16)
    regathered = gather_weights()
    query_w, key_w, value_w, out_w = (regathered[0], regathered[1], regathered[2], regathered[3])
    out_part = jnp.einsum(
        "th,td->hd", attended_rows, attn_out_grad, preferred_element_type=jnp.float32
    )
    attended_grad = (
        jnp.einsum("td,hd->th", attn_out_grad, out_w, preferred_element_type=jnp.float32)
        .astype(jnp.bfloat16)
        .reshape(head_shape)
    )
    grad_heads = lax.all_to_all(attended_grad, "ulysses", split_axis=2, concat_axis=0, tiled=True)
    delta = jnp.sum(grad_heads.astype(jnp.float32) * attended_float, axis=-1)

    def cycle_turn(counter, carry):
        key_now, value_now, key_acc, value_acc, query_acc = carry
        scores = (
            jnp.einsum("qshd,kshd->qshk", query_grp, key_now, preferred_element_type=jnp.float32)
            * score_scale
        )
        probs = jnp.exp(scores - log_total[..., None])
        value_acc = value_acc + jnp.einsum(
            "qshk,qshd->kshd",
            probs.astype(jnp.bfloat16),
            grad_heads,
            preferred_element_type=jnp.float32,
        )
        prob_grad = jnp.einsum(
            "qshd,kshd->qshk", grad_heads, value_now, preferred_element_type=jnp.float32
        )
        score_grad = (probs * (prob_grad - delta[..., None])).astype(jnp.bfloat16)
        query_acc = (
            query_acc
            + jnp.einsum("qshk,kshd->qshd", score_grad, key_now, preferred_element_type=jnp.float32)
            * score_scale
        )
        key_acc = (
            key_acc
            + jnp.einsum(
                "qshk,qshd->kshd", score_grad, query_grp, preferred_element_type=jnp.float32
            )
            * score_scale
        )
        key_now, value_now = shifted((key_now, value_now), "blk", 1)
        key_acc, value_acc = (
            shifted(key_acc.astype(jnp.bfloat16), "blk", 1).astype(key_acc.dtype),
            shifted(value_acc.astype(jnp.bfloat16), "blk", 1).astype(value_acc.dtype),
        )
        return (key_now, value_now, key_acc, value_acc, query_acc)

    cycle_start = (
        key_grp,
        value_grp,
        jnp.zeros(key_grp.shape, jnp.float32),
        jnp.zeros(value_grp.shape, jnp.float32),
        jnp.zeros(query_grp.shape, jnp.float32),
    )
    cycle_end = lax.fori_loop(0, blk_count, cycle_turn, cycle_start)
    back_query, back_key, back_value = (
        lax.all_to_all(
            cycle_end[4].astype(jnp.bfloat16), "ulysses", split_axis=0, concat_axis=2, tiled=True
        ),
        lax.all_to_all(
            cycle_end[2].astype(jnp.bfloat16), "ulysses", split_axis=0, concat_axis=2, tiled=True
        ),
        lax.all_to_all(
            cycle_end[3].astype(jnp.bfloat16), "ulysses", split_axis=0, concat_axis=2, tiled=True
        ),
    )
    query_raw_grad, key_raw_grad, qk_gain_part = heads_back(
        (back_query.astype(jnp.float32), back_key.astype(jnp.float32))
    )
    query_raw_low = query_raw_grad.astype(jnp.bfloat16).reshape(-1, head_count * HD)
    key_raw_low = key_raw_grad.astype(jnp.bfloat16).reshape(-1, head_count * HD)
    value_low = back_value.reshape(-1, head_count * HD)
    query_part = jnp.einsum("tc,th->ch", hidden, query_raw_low, preferred_element_type=jnp.float32)
    key_part_grad = jnp.einsum("tc,th->ch", hidden, key_raw_low, preferred_element_type=jnp.float32)
    value_part_grad = jnp.einsum("tc,th->ch", hidden, value_low, preferred_element_type=jnp.float32)
    hidden_grad = jnp.einsum(
        "th,ch->tc", query_raw_low, query_w, preferred_element_type=jnp.float32
    )
    hidden_grad = hidden_grad + jnp.einsum(
        "th,ch->tc", key_raw_low, key_w, preferred_element_type=jnp.float32
    )
    hidden_grad = hidden_grad + jnp.einsum(
        "th,ch->tc", value_low, value_w, preferred_element_type=jnp.float32
    )
    token_norm_grad, attn_gain_part = attn_norm_back(
        hidden_grad.reshape(seq_rows, seq_count, width)
    )
    input_grad = residual_grad.reshape(seq_rows, seq_count, width) + token_norm_grad
    summed = (
        lax.psum_scatter(query_part, ("ulysses", "blk"), scatter_dimension=0, tiled=True),
        lax.psum_scatter(key_part_grad, ("ulysses", "blk"), scatter_dimension=0, tiled=True),
        lax.psum_scatter(value_part_grad, ("ulysses", "blk"), scatter_dimension=0, tiled=True),
        lax.psum_scatter(out_part, ("ulysses", "blk"), scatter_dimension=0, tiled=True),
        lax.psum_scatter(attn_gain_part, ("ulysses", "blk"), scatter_dimension=0, tiled=True),
        lax.psum_scatter(ffn_gain_part, ("ulysses", "blk"), scatter_dimension=0, tiled=True),
        lax.psum_scatter(qk_gain_part, ("ulysses", "blk"), scatter_dimension=1, tiled=True),
    )
    return (
        mixed,
        input_grad,
        summed[0],
        summed[1],
        summed[2],
        summed[3],
        summed[4],
        summed[5],
        summed[6],
        gate_grad,
        up_grad,
        down_grad,
    )


def solution(mesh):
    in_specs = (
        P(("ulysses", "blk"), None, None),
        P(("ulysses", "blk"), None),
        P(("ulysses", "blk"), None),
        P(("ulysses", "blk"), None),
        P(("ulysses", "blk"), None),
        P(("ulysses", "blk")),
        P(("ulysses", "blk")),
        P(None, ("ulysses", "blk")),
        P("blk", None, "ulysses"),
        P("blk", None, "ulysses"),
        P("blk", "ulysses", None),
        P(("ulysses", "blk"), None, None),
        P(("ulysses", "blk"), None, None),
        P(("ulysses", "blk"), None),
        P(("ulysses", "blk"), None, None),
    )
    out_specs = (
        P(("ulysses", "blk"), None, None),
        P(("ulysses", "blk"), None, None),
        P(("ulysses", "blk"), None),
        P(("ulysses", "blk"), None),
        P(("ulysses", "blk"), None),
        P(("ulysses", "blk"), None),
        P(("ulysses", "blk")),
        P(("ulysses", "blk")),
        P(None, ("ulysses", "blk")),
        P("blk", None, "ulysses"),
        P("blk", None, "ulysses"),
        P("blk", "ulysses", None),
    )
    return jax.shard_map(body, mesh=mesh, in_specs=in_specs, out_specs=out_specs, check_vma=False)
```

profile of v0, /device:TPU:0, one launch (start us, length us, event | category | flops | bytes accessed | tf_op | source)
XLA Modules:
  0.0 4310.8 jit_solution(8557945832038193487)
XLA Ops:
  11.2 43.3 %all-reduce.12 = (bf16[2048]{0:T(1024)(128)(2,1)S(1)}, bf16[2048]{0:T(1024)(128)(2,1)S(1)}) all-reduce(bf16[2048]{0:T(1024)(128)(2,1)S(1)} %dynamic-update-slice, bf16[2048]{0:T(1024)(128)(2,1)S(1)} %dynamic-update-slice.1), channel_id=1, replica_groups=mesh['ulysses'=4,'blk'=8] {'ulysses','blk'}, use_global_device_ids=true, to_apply=%add.6 | all-reduce | flops 4096 | bytes 16384
  56.4 65.9 %all-gather = bf16[32,4,2]{1,2,0:T(2,128)(2,1)S(1)} all-gather(bf16[1,4,2]{1,2,0:T(2,128)(2,1)} %bitcast.350), channel_id=1, replica_groups=mesh['ulysses'=4,'blk'=8] {'ulysses','blk'}, dimensions={0}, use_global_device_ids=true | all-gather | bytes 528 | tf_op jit(solution)/shard_map/all_gather | solution.py:74
  136.8 33.6 all-gather.8.cloned.1.call-done
  194.2 16.9 all_to_all.140
  213.3 41.1 all-gather.14.cloned.1.call-done
  288.2 40.2 all-gather.10.cloned.1.call-done
  328.4 73.7 %all-gather.16.cloned.1.call-done = bf16[2048,2,4,128]{3,0,2,1:T(8,128)(2,1)} async-done(((bf16[256,2,4,128]{3,0,2,1:T(8,128)(2,1)}), bf16[2048,2,4,128]{3,0,2,1:T(8,128)(2,1)}) %all-gather.16.cloned.1.call-update) | async-done | bytes 4194320 | tf_op jit(solution)/shard_map/all_gather | solution.py:133
  402.1 43.1 while.34
  451.2 22.6 scatter_custom_fusion.1
  502.9 367.4 %all-gather.18.cloned.1.call-done = bf16[2048,2048]{1,0:T(8,128)(2,1)} async-done(((bf16[64,2048]{1,0:T(8,128)(2,1)}), bf16[2048,2048]{1,0:T(8,128)(2,1)}) %all-gather.18.cloned.1.call-update) | async-done | bytes 8388624 | tf_op jit(solution)/shard_map/all_gather | solution.py:71
  876.1 23.0 scatter_custom_fusion
  914.9 46.6 %all-to-all-done.6 = bf16[32,8,18,2048]{3,1,2,0:T(8,128)(2,1)} async-done(((bf16[32,8,18,2048]{3,1,2,0:T(8,128)(2,1)}), bf16[32,8,18,2048]{3,1,2,0:T(8,128)(2,1)}, u32[]{:S(2)}, u32[]{:S(2)}) %all-to-all-start.6) | async-done | bytes 18874400 | tf_op jit(solution)/shard_map/all_to_all | solution.py:207
  973.7 22.4 fusion.40
  996.1 398.8 %all-to-all-done.4 = bf16[32,8,18,2048]{3,1,2,0:T(8,128)(2,1)} async-done(((bf16[32,8,18,2048]{3,1,2,0:T(8,128)(2,1)}), bf16[32,8,18,2048]{3,1,2,0:T(8,128)(2,1)}, u32[]{:S(2)}, u32[]{:S(2)}) %all-to-all-start.4) | async-done | bytes 18874400 | tf_op jit(solution)/shard_map/all_to_all | solution.py:184
  1394.9 22.7 fusion.48
  1417.6 25.4 fusion.71
  1443.1 18.4 fusion.52
  1461.4 23.9 fusion.37
  1485.3 20.8 copy.287
  1522.4 20.7 copy.282
  1543.1 388.1 %all-to-all-done.7 = bf16[32,8,18,2048]{3,1,2,0:T(8,128)(2,1)} async-done(((bf16[32,8,18,2048]{3,1,2,0:T(8,128)(2,1)}), bf16[32,8,18,2048]{3,1,2,0:T(8,128)(2,1)}, u32[]{:S(2)}, u32[]{:S(2)}) %all-to-all-start.7) | async-done | bytes 18874400 | tf_op jit(solution)/shard_map/all_to_all | solution.py:227
  1935.8 25.8 copy.288
  1961.6 40.3 reshape.375
  2002.0 354.4 %all-to-all-done.5 = bf16[32,8,18,2048]{3,1,2,0:T(8,128)(2,1)} async-done(((bf16[32,8,18,2048]{3,1,2,0:T(8,128)(2,1)}), bf16[32,8,18,2048]{3,1,2,0:T(8,128)(2,1)}, u32[]{:S(2)}, u32[]{:S(2)}) %all-to-all-start.5) | async-done | bytes 18874400 | tf_op jit(solution)/shard_map/all_to_all | solution.py:196
  2356.4 25.4 copy.283
  2381.8 40.3 reshape.371
  2422.1 18.0 reduce_sum.184
  2440.1 18.0 reduce_sum.182
  2528.2 586.6 %while.35 = (s32[]{:T(128)}, bf16[256,2,4,128]{3,0,2,1:T(8,128)(2,1)}, bf16[256,2,4,128]{3,0,2,1:T(8,128)(2,1)}, f32[256,2,4,128]{3,0,2,1:T(8,128)}, f32[256,2,4...) while((s32[]{:T(128)}, ...), condition=%wide.region_18.20_spmd.clone, body=%wide.region_17.19_spmd.clone.sunk | while | flops 678428672 | bytes 32006432 | solution.py:296
  2542.7 16.9 collective-permute-done.2
  2582.0 15.1 collective-permute-done.1
  2674.1 13.6 collective-permute-start.1
  2712.5 18.8 collective-permute-done.1
  2746.4 13.6 collective-permute-start.1
  2814.7 16.6 collective-permute-done.2
  2853.8 18.9 collective-permute-done.1
  2929.5 24.9 collective-permute-done.1
  2996.1 15.1 collective-permute-done
  3011.2 23.2 collective-permute-done.1
  3076.2 15.0 collective-permute-done
  3091.2 23.6 collective-permute-done.1
  3188.0 35.9 fusion.57
  3223.8 36.2 fusion.60
  3260.0 37.2 fusion.63
  3320.5 52.9 %all-reduce.11 = (f32[2048]{0:T(1024)S(1)}, f32[2048]{0:T(1024)S(1)}, f32[2,128]{1,0:T(2,128)S(1)}) all-reduce(f32[2048]{0:T(1024)S(1)} %get-tuple-element.274, f32[2048]{0:T(1024)S(1)} %copy-done.53, f32[2,128]{1,0:T(2,128)S(1)} %pad_add_fusion.2), channel_id=6, replica_groups=mesh['ulysses'=4,'blk'=8] {'ulysses','blk'}, use_global_device_ids=true, to_apply=%region_27.29.clone | all-reduce | flops 4352 | bytes 34816
  3377.2 206.1 %reduce-scatter.6.cloned.1.call-done = f32[64,2048]{1,0:T(8,128)} async-done(((f32[2048,2048]{1,0:T(8,128)}), f32[64,2048]{1,0:T(8,128)}) %reduce-scatter.6.cloned.1.call-update) | async-done | bytes 524304 | tf_op jit(solution)/shard_map/reduce_scatter | solution.py:331
  3583.3 360.2 %reduce-scatter.8.cloned.1.call-done = f32[64,2048]{1,0:T(8,128)} async-done(((f32[2048,2048]{1,0:T(8,128)}), f32[64,2048]{1,0:T(8,128)}) %reduce-scatter.8.cloned.1.call-update) | async-done | bytes 524304 | tf_op jit(solution)/shard_map/reduce_scatter | solution.py:332
  3943.5 360.1 %reduce-scatter.10.cloned.1.call-done = f32[64,2048]{1,0:T(8,128)} async-done(((f32[2048,2048]{1,0:T(8,128)}), f32[64,2048]{1,0:T(8,128)}) %reduce-scatter.10.cloned.1.call-update) | async-done | bytes 524304 | tf_op jit(solution)/shard_map/reduce_scatter | solution.py:333
  (455 shorter events, 752.6 us)
Async XLA Ops:
  7.2 117.4 %all-gather.12.cloned.1.call-start = ((), (), s32[]{:S(2)}) async-start(), calls=%async_computation.18 | async-start | bytes 8650752 | tf_op jit(solution)/shard_map/all_gather | solution.py:68
  7.9 162.5 %all-gather.8.cloned.1.call-start = ((), (), s32[]{:S(2)}) async-start(), calls=%async_computation.16 | async-start | bytes 8650752 | tf_op jit(solution)/shard_map/all_gather | solution.py:69
  8.7 245.7 %all-gather.14.cloned.1.call-start = ((), (), s32[]{:S(2)}) async-start(), calls=%async_computation.19 | async-start | bytes 8650752 | tf_op jit(solution)/shard_map/all_gather | solution.py:70
  9.4 319.0 %all-gather.10.cloned.1.call-start = ((), (), s32[]{:S(2)}) async-start(), calls=%async_computation.17 | async-start | bytes 4718592 | tf_op jit(solution)/shard_map/all_gather | solution.py:132
  212.1 190.0 %all-gather.16.cloned.1.call-start = ((), (), s32[]{:S(2)}) async-start(), calls=%async_computation.20 | async-start | bytes 4718592 | tf_op jit(solution)/shard_map/all_gather | solution.py:133
  447.4 41.9 all-to-all-start.3
  497.6 463.9 %all-to-all-start.6 = ((bf16[32,8,18,2048]{3,1,2,0:T(8,128)(2,1)}), bf16[32,8,18,2048]{3,1,2,0:T(8,128)(2,1)}, u32[]{:S(2)}, u32[]{:S(2)}) async-start(bf16[32,8,18,2048]{3,1,2,0:T(8,128)(2,1)} %bitcast.309), calls=%async_computation.6 | async-start | bytes 37748736 | tf_op jit(solution)/shard_map/all_to_all | solution.py:207
  501.5 368.7 %all-gather.18.cloned.1.call-start = ((), (), s32[]{:S(2)}) async-start(), calls=%async_computation.21 | async-start | bytes 8650752 | tf_op jit(solution)/shard_map/all_gather | solution.py:71
  969.8 425.1 %all-to-all-start.4 = ((bf16[32,8,18,2048]{3,1,2,0:T(8,128)(2,1)}), bf16[32,8,18,2048]{3,1,2,0:T(8,128)(2,1)}, u32[]{:S(2)}, u32[]{:S(2)}) async-start(bf16[32,8,18,2048]{3,1,2,0:T(8,128)(2,1)} %bitcast.310), calls=%async_computation.4 | async-start | bytes 37748736 | tf_op jit(solution)/shard_map/all_to_all | solution.py:184
  1506.1 425.2 %all-to-all-start.7 = ((bf16[32,8,18,2048]{3,1,2,0:T(8,128)(2,1)}), bf16[32,8,18,2048]{3,1,2,0:T(8,128)(2,1)}, u32[]{:S(2)}, u32[]{:S(2)}) async-start(bf16[32,8,18,2048]{3,1,2,0:T(8,128)(2,1)} %copy.287), calls=%async_computation.7 | async-start | bytes 37748736 | tf_op jit(solution)/shard_map/all_to_all | solution.py:227
  1931.2 425.2 %all-to-all-start.5 = ((bf16[32,8,18,2048]{3,1,2,0:T(8,128)(2,1)}), bf16[32,8,18,2048]{3,1,2,0:T(8,128)(2,1)}, u32[]{:S(2)}, u32[]{:S(2)}) async-start(bf16[32,8,18,2048]{3,1,2,0:T(8,128)(2,1)} %copy.282), calls=%async_computation.5 | async-start | bytes 37748736 | tf_op jit(solution)/shard_map/all_to_all | solution.py:196
  1935.2 1442.0 %reduce-scatter.12.cloned.1.call-start = ((), (), s32[]{:S(2)}) async-start(), calls=%async_computation.25 | async-start | bytes 17301504 | tf_op jit(solution)/shard_map/reduce_scatter | solution.py:334
  2512.8 12.3 all-to-all-start.8
  2537.7 21.8 collective-permute-start.2
  2540.1 30.6 collective-permute-start.3
  2540.1 41.9 collective-permute-start
  2540.1 57.0 %collective-permute-start.1 = (bf16[256,2,4,128]{3,0,2,1:T(8,128)(2,1)}, bf16[256,2,4,128]{3,0,2,1:T(8,128)(2,1)}, u32[]{:S(2)}, u32[]{:S(2)}) collective-permute-start(bf16[256,2,4,128]{3,0,2,1:T(8,128)(2,1)} %copy.403), channel_id=1, source_target_pairs={{0,1},{1,2},{2,3},{3,4},{4,5},{5,6},{6,7},{7,0},{8,9},{9,10},{10,1... | collective-permute-start | bytes 1572872 | tf_op jit(solution)/shard_map/while/body/eval_jaxpr/ppermute | solution.py:18
  2607.1 18.7 collective-permute-start.2
  2612.2 24.6 collective-permute-start.3
  2612.2 36.0 collective-permute-start
  2612.3 45.5 %collective-permute-start.1 = (bf16[256,2,4,128]{3,0,2,1:T(8,128)(2,1)}, bf16[256,2,4,128]{3,0,2,1:T(8,128)(2,1)}, u32[]{:S(2)}, u32[]{:S(2)}) collective-permute-start(bf16[256,2,4,128]{3,0,2,1:T(8,128)(2,1)} %copy.403), channel_id=1, source_target_pairs={{0,1},{1,2},{2,3},{3,4},{4,5},{5,6},{6,7},{7,0},{8,9},{9,10},{10,1... | collective-permute-start | bytes 1572872 | tf_op jit(solution)/shard_map/while/body/eval_jaxpr/ppermute | solution.py:18
  2667.6 23.0 collective-permute-start.2
  2672.7 28.6 collective-permute-start.3
  2672.7 39.8 collective-permute-start
  2674.1 57.2 %collective-permute-start.1 = (bf16[256,2,4,128]{3,0,2,1:T(8,128)(2,1)}, bf16[256,2,4,128]{3,0,2,1:T(8,128)(2,1)}, u32[]{:S(2)}, u32[]{:S(2)}) collective-permute-start(bf16[256,2,4,128]{3,0,2,1:T(8,128)(2,1)} %copy.403), channel_id=1, source_target_pairs={{0,1},{1,2},{2,3},{3,4},{4,5},{5,6},{6,7},{7,0},{8,9},{9,10},{10,1... | collective-permute-start | bytes 1572872 | tf_op jit(solution)/shard_map/while/body/eval_jaxpr/ppermute | solution.py:18
  2741.2 21.7 collective-permute-start.2
  2746.3 24.6 collective-permute-start.3
  2746.3 35.9 collective-permute-start
  2746.4 49.0 %collective-permute-start.1 = (bf16[256,2,4,128]{3,0,2,1:T(8,128)(2,1)}, bf16[256,2,4,128]{3,0,2,1:T(8,128)(2,1)}, u32[]{:S(2)}, u32[]{:S(2)}) collective-permute-start(bf16[256,2,4,128]{3,0,2,1:T(8,128)(2,1)} %copy.403), channel_id=1, source_target_pairs={{0,1},{1,2},{2,3},{3,4},{4,5},{5,6},{6,7},{7,0},{8,9},{9,10},{10,1... | collective-permute-start | bytes 1572872 | tf_op jit(solution)/shard_map/while/body/eval_jaxpr/ppermute | solution.py:18
  2805.2 26.1 collective-permute-start.2
  2809.1 33.3 collective-permute-start.3
  2809.3 44.5 %collective-permute-start = (bf16[256,2,4,128]{3,0,2,1:T(8,128)(2,1)}, bf16[256,2,4,128]{3,0,2,1:T(8,128)(2,1)}, u32[]{:S(2)}, u32[]{:S(2)}) collective-permute-start(bf16[256,2,4,128]{3,0,2,1:T(8,128)(2,1)} %copy.402), channel_id=1, source_target_pairs={{0,1},{1,2},{2,3},{3,4},{4,5},{5,6},{6,7},{7,0},{8,9},{9,10},{10,1... | collective-permute-start | bytes 1572872 | tf_op jit(solution)/shard_map/while/body/eval_jaxpr/ppermute | solution.py:18
  2811.8 60.9 %collective-permute-start.1 = (bf16[256,2,4,128]{3,0,2,1:T(8,128)(2,1)}, bf16[256,2,4,128]{3,0,2,1:T(8,128)(2,1)}, u32[]{:S(2)}, u32[]{:S(2)}) collective-permute-start(bf16[256,2,4,128]{3,0,2,1:T(8,128)(2,1)} %copy.403), channel_id=1, source_target_pairs={{0,1},{1,2},{2,3},{3,4},{4,5},{5,6},{6,7},{7,0},{8,9},{9,10},{10,1... | collective-permute-start | bytes 1572872 | tf_op jit(solution)/shard_map/while/body/eval_jaxpr/ppermute | solution.py:18
  2882.5 22.0 collective-permute-start.2
  2890.6 25.0 collective-permute-start.3
  2890.6 39.0 collective-permute-start
  2890.6 63.8 %collective-permute-start.1 = (bf16[256,2,4,128]{3,0,2,1:T(8,128)(2,1)}, bf16[256,2,4,128]{3,0,2,1:T(8,128)(2,1)}, u32[]{:S(2)}, u32[]{:S(2)}) collective-permute-start(bf16[256,2,4,128]{3,0,2,1:T(8,128)(2,1)} %copy.403), channel_id=1, source_target_pairs={{0,1},{1,2},{2,3},{3,4},{4,5},{5,6},{6,7},{7,0},{8,9},{9,10},{10,1... | collective-permute-start | bytes 1572872 | tf_op jit(solution)/shard_map/while/body/eval_jaxpr/ppermute | solution.py:18
  2964.3 18.7 collective-permute-start.2
  2969.8 25.2 collective-permute-start.3
  2969.8 41.4 collective-permute-start
  2969.8 64.6 %collective-permute-start.1 = (bf16[256,2,4,128]{3,0,2,1:T(8,128)(2,1)}, bf16[256,2,4,128]{3,0,2,1:T(8,128)(2,1)}, u32[]{:S(2)}, u32[]{:S(2)}) collective-permute-start(bf16[256,2,4,128]{3,0,2,1:T(8,128)(2,1)} %copy.403), channel_id=1, source_target_pairs={{0,1},{1,2},{2,3},{3,4},{4,5},{5,6},{6,7},{7,0},{8,9},{9,10},{10,1... | collective-permute-start | bytes 1572872 | tf_op jit(solution)/shard_map/while/body/eval_jaxpr/ppermute | solution.py:18
  3044.3 17.9 collective-permute-start.2
  3049.8 25.4 collective-permute-start.3
  3049.8 41.4 collective-permute-start
  3049.8 65.0 %collective-permute-start.1 = (bf16[256,2,4,128]{3,0,2,1:T(8,128)(2,1)}, bf16[256,2,4,128]{3,0,2,1:T(8,128)(2,1)}, u32[]{:S(2)}, u32[]{:S(2)}) collective-permute-start(bf16[256,2,4,128]{3,0,2,1:T(8,128)(2,1)} %copy.403), channel_id=1, source_target_pairs={{0,1},{1,2},{2,3},{3,4},{4,5},{5,6},{6,7},{7,0},{8,9},{9,10},{10,1... | collective-permute-start | bytes 1572872 | tf_op jit(solution)/shard_map/while/body/eval_jaxpr/ppermute | solution.py:18
  3133.4 450.0 %reduce-scatter.6.cloned.1.call-start = ((), (), s32[]{:S(2)}) async-start(), calls=%async_computation.22 | async-start | bytes 17301504 | tf_op jit(solution)/shard_map/reduce_scatter | solution.py:331
  3157.5 786.0 %reduce-scatter.8.cloned.1.call-start = ((), (), s32[]{:S(2)}) async-start(), calls=%async_computation.23 | async-start | bytes 17301504 | tf_op jit(solution)/shard_map/reduce_scatter | solution.py:332
  3166.1 1137.5 %reduce-scatter.10.cloned.1.call-start = ((), (), s32[]{:S(2)}) async-start(), calls=%async_computation.24 | async-start | bytes 17301504 | tf_op jit(solution)/shard_map/reduce_scatter | solution.py:333
  (75 other events, 3923.5 us)
Sparse Core Ops, SparseCore 0:
  11.0 80.4 all-gather.11
  94.4 75.9 all-gather.7
  173.4 80.8 all-gather.13
  256.4 71.9 all-gather.9
  330.4 71.6 all-gather.15
  505.0 365.1 all-gather.17
  2504.7 716.6 reduce-scatter.11
  3224.3 359.0 reduce-scatter.5
  3586.2 357.2 reduce-scatter.7
  3946.3 357.3 reduce-scatter.9
where the time goes:
time: 4330 us; the launch traced here: 4310 us
  waiting for transfers between devices  3090 us (71%)
  matrix products  433 us (10%)
  local copies, waits for them, and re-layouts  355 us (8%)
  blocking collectives  202 us (5%)
  other arithmetic  129 us (3%)
  starting transfers between devices  90.4 us (2%)
    all_to_all x1, waiting for transfers between devices, body(): lax.all_to_all(spread(normed[token_of]), ('ulysses', 'blk'), split_axis=0...  399 us
    all_to_all x1, waiting for transfers between devices, body(): lax.all_to_all(row_grads.astype(jnp.bfloat16), ('ulysses', 'blk'), split_...  388 us
    ppermute x32, waiting for transfers between devices, shifted(): lax.ppermute(value, axis, [(i, (i + by) % devices) for i in range(devices)])  383 us
    all_gather x1, waiting for transfers between devices, gather_weights(): lax.all_gather(w_out, ('ulysses', 'blk'), axis=0, tiled=True)  367 us
    reduce_scatter x1, waiting for transfers between devices, body(): lax.psum_scatter(key_part_grad, ('ulysses', 'blk'), scatter_dimension=0,...  360 us
    reduce_scatter x1, waiting for transfers between devices, body(): lax.psum_scatter(value_part_grad, ('ulysses', 'blk'), scatter_dimension=0...  360 us
    all_to_all x1, waiting for transfers between devices, body(): lax.all_to_all(partial_value, ('ulysses', 'blk'), split_axis=0, concat_ax...  354 us
    reduce_scatter x1, waiting for transfers between devices, body(): lax.psum_scatter(query_part, ('ulysses', 'blk'), scatter_dimension=0, til...  206 us
  transfers between devices with their start and end apart: 51, of which 46 were waited for; matrix products, arithmetic and copies ran while one was open for 14% of the time, Pallas kernels for 0%

commit v1 on v0

v1 whole, which is shorter than its diff:
```python
import functools
import math

import jax
import jax.numpy as jnp
import numpy as np
from jax import lax
from jax.experimental import pallas as pl
from jax.experimental.pallas import tpu as pltpu
from jax.sharding import PartitionSpec as P

HD = 128
CAP = 18
EPSILON = 1e-06
ROPE_BASE = 10000.0
AXES = ("ulysses", "blk")
MESH = pl.DeviceIdType.MESH


class Place:
    def __init__(self, U, B):
        self.U, self.B = U, B
        self.X, self.Y = U // 2, 2
        self.Z = B // self.Y
        u, b = lax.axis_index("ulysses"), lax.axis_index("blk")
        self.c, self.x = lax.rem(u, 2), lax.div(u, 2)
        self.y, self.z = lax.rem(b, self.Y), lax.div(b, self.Y)
        self.core_peer = self.dev(self.x, self.y, self.z, 1 - self.c)

    def dev(self, x, y, z, c):
        return (x * 2 + c, z * self.Y + y)

    def block(self, x, y, z, c):
        return (x * 2 + c) * self.B + z * self.Y + y

    def others(self, axis):
        n = {"x": self.X, "y": self.Y, "z": self.Z}[axis]
        i = {"x": self.x, "y": self.y, "z": self.z}[axis]
        return [lax.rem(i + o, n) for o in range(1, n)]

    def barrier(self, chain):
        sem = pltpu.get_barrier_semaphore()

        def greet(d):
            pl.semaphore_signal(sem, inc=1, device_id=d, device_id_type=MESH)

        greet(self.core_peer)
        for k in self.others("x"):
            greet(self.dev(k, self.y, self.z, self.c))
        for k in self.others("y"):
            greet(self.dev(self.x, k, self.z, self.c))
        count = self.X + self.Y - 1
        if chain:
            below, above = self.z > 0, self.z < self.Z - 1

            @pl.when(below)
            def _():
                greet(self.dev(self.x, self.y, self.z - 1, self.c))

            @pl.when(above)
            def _():
                greet(self.dev(self.x, self.y, self.z + 1, self.c))

            count = count + jnp.where(below, 1, 0) + jnp.where(above, 1, 0)
        else:
            for k in self.others("z"):
                greet(self.dev(self.x, self.y, k, self.c))
            count += self.Z - 1
        pl.semaphore_wait(sem, count)


def gather_kernel(U, B, by_seq, src, out, send_sem, recv_sem, local_sem):
    p = Place(U, B)
    Z = p.Z
    p.barrier(True)
    started = []
    always = p.z >= 0

    def where(half, x, y, z):
        if by_seq:
            f = p.block(x, y, z, half)
            return out.at[f], (0, f)
        f = p.block(x, y, z, p.c)
        return out.at[f, half], (half, f)

    def send(cond, src_ref, dst_ref, ix, way, dev):
        cp = pltpu.make_async_remote_copy(
            src_ref=src_ref, dst_ref=dst_ref, send_sem=send_sem.at[(way,) + ix], recv_sem=recv_sem.at[ix],
            device_id=dev, device_id_type=MESH)

        @pl.when(cond)
        def _():
            cp.start()

        started.append((cond, cp))

    def wait(ref, ix):
        pltpu.make_async_remote_copy(
            src_ref=ref, dst_ref=ref, send_sem=send_sem.at[(0,) + ix], recv_sem=recv_sem.at[ix],
            device_id=p.core_peer, device_id_type=MESH).wait_recv()

    def along(cond, half, x, y, z, axes):
        ref, ix = where(half, x, y, z)
        for ax in axes:
            if ax == "core":
                if not by_seq:
                    send(cond, ref, ref, ix, 0, p.core_peer)
            elif ax == "up":
                send(cond & (p.z < Z - 1), ref, ref, ix, 1, p.dev(p.x, p.y, p.z + 1, p.c))
            elif ax == "down":
                send(cond & (p.z > 0), ref, ref, ix, 2, p.dev(p.x, p.y, p.z - 1, p.c))
            elif ax == "y":
                for i, k in enumerate(p.others("y")):
                    send(cond, ref, ref, ix, 3 + i, p.dev(p.x, k, p.z, p.c))
            else:
                for i, k in enumerate(p.others("x")):
                    send(cond, ref, ref, ix, 2 + p.Y + i, p.dev(k, p.y, p.z, p.c))

    me = p.block(p.x, p.y, p.z, p.c)
    sib = p.block(p.x, p.y, p.z, 1 - p.c)
    if by_seq:
        cp = pltpu.make_async_copy(src.at[p.c], out.at[me], local_sem.at[0])
        cp.start()
        send(always, src.at[1 - p.c], out.at[me], (0, me), 0, p.core_peer)
        cp.wait()
        wait(out.at[sib], (0, sib))
    else:
        cp = pltpu.make_async_copy(src, out.at[me], local_sem.at[0])
        cp.start()
        cp.wait()
    for half in (0, 1):
        along(always, half, p.x, p.y, p.z, ("up", "down", "y", "x"))
    for half in (0, 1):
        along(always, half, p.x, p.y, p.z, ("core",))

    def zs(step):
        if step == 0:
            return [(always, p.z, ())]
        return [(p.z - step >= 0, p.z - step, ("up",)), (p.z + step < Z, p.z + step, ("down",))]

    def arrive(cond, half, x, y, z, axes):
        ref, ix = where(half, x, y, z)

        @pl.when(cond)
        def _():
            wait(ref, ix)

        along(cond, half, x, y, z, axes)

    for step in range(1, Z + 2):
        if step < Z:
            for half in (0, 1):
                for cond, k, on in zs(step):
                    arrive(cond, half, p.x, p.y, k, on + ("y", "x", "core"))
        if 1 <= step <= Z:
            for cond, k, _ in zs(step - 1):
                for j in p.others("y"):
                    arrive(cond, 0, p.x, j, k, ("x", "core"))
                for j in p.others("x"):
                    arrive(cond, 1, j, p.y, k, ("y", "core"))
        if step >= 2:
            for cond, k, _ in zs(step - 2):
                for j in p.others("x"):
                    arrive(cond, 0, j, p.y, k, ("core",))
                for i in p.others("y"):
                    arrive(cond, 1, p.x, i, k, ("core",))
                for j in p.others("x"):
                    for i in p.others("y"):
                        arrive(cond, 0, j, i, k, ("core",))
                        arrive(cond, 1, j, i, k, ("core",))
    if not by_seq:
        for k in range(Z):
            for j in range(p.X):
                for i in range(p.Y):
                    for half in (0, 1):
                        f = p.block(j, i, k, 1 - p.c)
                        wait(out.at[f, half], (half, f))
    for cond, cp in started:
        @pl.when(cond)
        def _(cp=cp):
            cp.wait_send()


def gather_blocks(v, U, B, by_seq, cid):
    F = U * B
    shape = (F,) + (v.shape[1:] if by_seq else v.shape)
    n = 1 if by_seq else 2
    return pl.pallas_call(
        functools.partial(gather_kernel, U, B, by_seq),
        out_shape=jax.ShapeDtypeStruct(shape, v.dtype),
        in_specs=[pl.BlockSpec(memory_space=pl.ANY)],
        out_specs=pl.BlockSpec(memory_space=pl.ANY),
        scratch_shapes=[
            pltpu.SemaphoreType.DMA((2 + 2 + U // 2 - 1 + 0, n, F)),
            pltpu.SemaphoreType.DMA((n, F)),
            pltpu.SemaphoreType.DMA((1,)),
        ],
        compiler_params=pltpu.CompilerParams(collective_id=cid, has_side_effects=True),
    )(v)


def scatter_kernel(U, B, by_seq, src, out, acc, rc, rx0, rx1, ry0, ry1, rz, fin,
                   loc, scs, rcs, sxs, rxs, sys_, rys, szs, rzs, fs):
    p = Place(U, B)
    X, Y, Z = p.X, p.Y, p.Z
    rows = acc.shape[2]
    p.barrier(False)
    f32 = jnp.float32
    started = []

    def chip(x, y, z):
        return x * B + z * Y + y

    def remote(a, b, ss, rs, dev):
        return pltpu.make_async_remote_copy(
            src_ref=a, dst_ref=b, send_sem=ss, recv_sem=rs, device_id=dev, device_id_type=MESH)

    def start(*a):
        cp = remote(*a)
        cp.start()
        started.append(cp)

    def got(ref, rs):
        remote(ref, ref, fs.at[1], rs, p.core_peer).wait_recv()

    order = p.others("z") + [p.z]
    ox, oy = p.others("x"), p.others("y")

    def first_pieces(k):
        return [(0, j, i, k) for j in ox for i in range(Y)] + [(1, j, i, k) for i in oy for j in range(X)]

    def second_pieces(k):
        return [(0, p.x, i, k) for i in oy] + [(1, j, p.y, k) for j in ox]

    def third_pieces(k):
        return [(0, p.x, p.y, k), (1, p.x, p.y, k)]

    def load(h, j, i, k):
        q = chip(j, i, k)
        if by_seq:
            pltpu.make_async_copy(src.at[p.block(j, i, k, h)], acc.at[q, h], loc.at[q, h]).start()
        else:
            start(src.at[p.block(j, i, k, 1 - p.c), h], rc.at[q, h], scs.at[q, h], rcs.at[q, h], p.core_peer)
            pltpu.make_async_copy(src.at[p.block(j, i, k, p.c), h], acc.at[q, h], loc.at[q, h]).start()

    def ready(h, j, i, k):
        q = chip(j, i, k)
        pltpu.make_async_copy(acc.at[q, h], acc.at[q, h], loc.at[q, h]).wait()
        if by_seq:
            return []
        got(rc.at[q, h], rcs.at[q, h])
        return [rc.at[q, h]]

    step = 16

    def add(dst, srcs, f32_out=None):
        if not srcs and f32_out is None:
            return

        def one(n, _):
            r = pl.ds(pl.multiple_of(n * step, step), step)
            t = dst[r, :].astype(f32)
            for s in srcs:
                t = t + s[r, :].astype(f32)
            if f32_out is None:
                dst[r, :] = t.astype(dst.dtype)
            else:
                f32_out[r, :] = t
            return 0

        lax.fori_loop(0, rows // step, one, 0)

    def phase1(k):
        for h, j, i, kk in first_pieces(k):
            q = chip(j, i, k)
            add(acc.at[q, h], ready(h, j, i, k))
            if h == 0:
                s = k * Y + i
                start(acc.at[q, 0], rx0.at[p.x, s], sxs.at[0, j, s], rxs.at[0, p.x, s], p.dev(j, p.y, p.z, p.c))
            else:
                s = k * X + j
                start(acc.at[q, 1], ry1.at[p.y, s], sys_.at[1, i, s], rys.at[1, p.y, s], p.dev(p.x, i, p.z, p.c))

    def phase2(k):
        for h, j, i, kk in second_pieces(k):
            q = chip(j, i, k)
            extra = ready(h, j, i, k)
            if h == 0:
                s = k * Y + i
                for a in ox:
                    got(rx0.at[a, s], rxs.at[0, a, s])
                    extra.append(rx0.at[a, s])
                add(acc.at[q, 0], extra)
                start(acc.at[q, 0], ry0.at[p.y, k], sys_.at[0, i, k], rys.at[0, p.y, k], p.dev(p.x, i, p.z, p.c))
            else:
                s = k * X + j
                for a in oy:
                    got(ry1.at[a, s], rys.at[1, a, s])
                    extra.append(ry1.at[a, s])
                add(acc.at[q, 1], extra)
                start(acc.at[q, 1], rx1.at[p.x, k], sxs.at[1, j, k], rxs.at[1, p.x, k], p.dev(j, p.y, p.z, p.c))

    def phase3(n, k):
        for h, j, i, kk in third_pieces(k):
            q = chip(j, i, k)
            extra = ready(h, j, i, k)
            if h == 0:
                s = k * Y + i
                for a in ox:
                    got(rx0.at[a, s], rxs.at[0, a, s])
                    extra.append(rx0.at[a, s])
                for a in oy:
                    got(ry0.at[a, k], rys.at[0, a, k])
                    extra.append(ry0.at[a, k])
            else:
                s = k * X + j
                for a in oy:
                    got(ry1.at[a, s], rys.at[1, a, s])
                    extra.append(ry1.at[a, s])
                for a in ox:
                    got(rx1.at[a, k], rxs.at[1, a, k])
                    extra.append(rx1.at[a, k])
            if n < Z - 1:
                add(acc.at[q, h], extra)
                start(acc.at[q, h], rz.at[h, p.z], szs.at[h, k], rzs.at[h, p.z], p.dev(p.x, p.y, k, p.c))
            else:
                for a in p.others("z"):
                    got(rz.at[h, a], rzs.at[h, a])
                    extra.append(rz.at[h, a])
                add(acc.at[q, h], extra, fin.at[h])

    for k in order:
        for piece in first_pieces(k) + second_pieces(k) + third_pieces(k):
            load(*piece)
    for n in range(Z + 2):
        if n < Z:
            phase1(order[n])
        if 1 <= n <= Z:
            phase2(order[n - 1])
        if n >= 2:
            phase3(n - 2, order[n - 2])
    if by_seq:
        start(fin.at[1 - p.c], out.at[p.c], fs.at[2], fs.at[0], p.core_peer)
        cp = pltpu.make_async_copy(fin.at[p.c], out.at[p.c], fs.at[1])
        cp.start()
        cp.wait()
        got(out.at[1 - p.c], fs.at[0])
    else:
        cp = pltpu.make_async_copy(fin, out, fs.at[1])
        cp.start()
        cp.wait()
    for cp in started:
        cp.wait_send()


def scatter_blocks(v, U, B, by_seq, cid):
    F, Q = U * B, U * B // 2
    X, Y, Z = U // 2, 2, B // 2
    rows, D = v.shape[-2:]
    parts = max(1, F // 32)
    if parts > 1:
        w = D // parts
        return jnp.concatenate(
            [_scatter(v[..., n * w:(n + 1) * w], U, B, by_seq, cid) for n in range(parts)], axis=-1)
    return _scatter(v, U, B, by_seq, cid)


def _scatter(v, U, B, by_seq, cid):
    F, Q = U * B, U * B // 2
    X, Y, Z = U // 2, 2, B // 2
    rows, D = v.shape[-2:]
    t = v.dtype
    dma = pltpu.SemaphoreType.DMA
    big = max(Z * Y, Z * X)
    return pl.pallas_call(
        functools.partial(scatter_kernel, U, B, by_seq),
        out_shape=jax.ShapeDtypeStruct((2, rows, D), jnp.float32),
        in_specs=[pl.BlockSpec(memory_space=pl.ANY)],
        out_specs=pl.BlockSpec(memory_space=pl.ANY),
        scratch_shapes=[
            pltpu.VMEM((Q, 2, rows, D), t),
            pltpu.VMEM((1, 1, 16, 128) if by_seq else (Q, 2, rows, D), t),
            pltpu.VMEM((X, Z * Y, rows, D), t),
            pltpu.VMEM((X, Z, rows, D), t),
            pltpu.VMEM((Y, Z, rows, D), t),
            pltpu.VMEM((Y, Z * X, rows, D), t),
            pltpu.VMEM((2, Z, rows, D), t),
            pltpu.VMEM((2, rows, D), jnp.float32),
            dma((Q, 2)),
            dma((Q, 2)),
            dma((Q, 2)),
            dma((2, X, big)),
            dma((2, X, big)),
            dma((2, Y, big)),
            dma((2, Y, big)),
            dma((2, Z)),
            dma((2, Z)),
            dma((3,)),
        ],
        compiler_params=pltpu.CompilerParams(
            collective_id=cid, has_side_effects=True, vmem_limit_bytes=58 * 2**20),
    )(v)


def rms_norm(values, gains):
    return values * lax.rsqrt(jnp.mean(values * values, axis=-1, keepdims=True) + EPSILON) * gains


def rotate(values):
    half = values.shape[-1] // 2
    inverse = ROPE_BASE ** (-2.0 * jnp.arange(half).astype(jnp.float32) / values.shape[-1])
    angles = jnp.arange(values.shape[0]).astype(jnp.float32)[:, None] * inverse[None, :]
    cosine, sine = jnp.cos(angles), jnp.sin(angles)
    a, b = values[:, :half], values[:, half:]
    return jnp.concatenate([a * cosine - b * sine, b * cosine + a * sine], axis=-1)


def dot(a, b, ca, cb):
    return lax.dot_general(a, b, (((ca,), (cb,)), ((), ())), preferred_element_type=jnp.float32)


def attend_kernel(scale, q_ref, k_ref, vt_ref, o_ref, lse_ref):
    s = dot(k_ref[...], q_ref[...], 1, 1) * scale
    top = jnp.max(s, axis=0, keepdims=True)
    e = jnp.exp(s - top)
    total = jnp.sum(e, axis=0, keepdims=True)
    o = dot(vt_ref[...], e.astype(jnp.bfloat16), 1, 0) / total
    o_ref[...] = o.T.astype(o_ref.dtype)
    lse_ref[...] = top + jnp.log(total)


def attend(q, k, vt):
    n = q.shape[0]
    bq = 256 if n <= 2048 else 128
    return pl.pallas_call(
        functools.partial(attend_kernel, 1.0 / math.sqrt(HD)),
        grid=(n // bq,),
        in_specs=[
            pl.BlockSpec((bq, HD), lambda i: (i, 0)),
            pl.BlockSpec((n, HD), lambda i: (0, 0)),
            pl.BlockSpec((HD, n), lambda i: (0, 0)),
        ],
        out_specs=[pl.BlockSpec((bq, HD), lambda i: (i, 0)), pl.BlockSpec((1, bq), lambda i: (0, i))],
        out_shape=[jax.ShapeDtypeStruct((n, HD), jnp.bfloat16), jax.ShapeDtypeStruct((1, n), jnp.float32)],
        compiler_params=pltpu.CompilerParams(vmem_limit_bytes=58 * 2**20),
    )(q, k, vt)


def attend_back_kernel(scale, q_ref, do_ref, lse_ref, k_ref, kt_ref, v_ref, dq_ref, dk_ref, dv_ref):
    @pl.when(pl.program_id(0) == 0)
    def _():
        dk_ref[...] = jnp.zeros_like(dk_ref)
        dv_ref[...] = jnp.zeros_like(dv_ref)

    p = jnp.exp(dot(k_ref[...], q_ref[...], 1, 1) * scale - lse_ref[...])
    dp = dot(v_ref[...], do_ref[...], 1, 1)
    delta = jnp.sum(p * dp, axis=0, keepdims=True)
    ds = (p * (dp - delta)).astype(jnp.bfloat16)
    dv_ref[...] += dot(p.astype(jnp.bfloat16), do_ref[...], 1, 0)
    dk_ref[...] += dot(ds, q_ref[...], 1, 0) * scale
    dq_ref[...] = (dot(kt_ref[...], ds, 1, 0) * scale).T


def attend_back(q, do, lse, k, kt, v):
    n = q.shape[0]
    bq = 256 if n <= 2048 else 128
    row = lambda i: (i, 0)
    whole = lambda i: (0, 0)
    f32 = jax.ShapeDtypeStruct((n, HD), jnp.float32)
    return pl.pallas_call(
        functools.partial(attend_back_kernel, 1.0 / math.sqrt(HD)),
        grid=(n // bq,),
        in_specs=[
            pl.BlockSpec((bq, HD), row),
            pl.BlockSpec((bq, HD), row),
            pl.BlockSpec((1, bq), lambda i: (0, i)),
            pl.BlockSpec((n, HD), whole),
            pl.BlockSpec((HD, n), whole),
            pl.BlockSpec((n, HD), whole),
        ],
        out_specs=[pl.BlockSpec((bq, HD), row), pl.BlockSpec((n, HD), whole), pl.BlockSpec((n, HD), whole)],
        out_shape=[f32, f32, f32],
        compiler_params=pltpu.CompilerParams(vmem_limit_bytes=58 * 2**20),
    )(q, do, lse, k, kt, v)


def to_all(v):
    return lax.all_to_all(v, AXES, split_axis=0, concat_axis=0, tiled=True)


def body(tokens, w_query, w_key, w_value, w_out, attn_gain, ffn_gain, qk_gain,
         expert_gate, expert_up, expert_down, routes, gates, order, cotangent):
    f32, bf16 = jnp.float32, jnp.bfloat16
    positions, seqs, D = tokens.shape
    U, B = lax.axis_size("ulysses"), lax.axis_size("blk")
    F = U * B
    u, b = lax.axis_index("ulysses"), lax.axis_index("blk")
    H = w_query.shape[1] // HD
    W = w_query.shape[0]
    L = F * positions
    T = seqs * positions
    top_count = routes.shape[-1]
    local_experts = expert_gate.shape[0]
    E = local_experts * B
    chips = F // 2
    R = chips // H
    chip_of = np.array([(d // B // 2) * B + d % B for d in range(F)])
    head_of, seq_of = chip_of // R, np.array([(d // B) % 2 for d in range(F)])
    first_copy = lax.rem((u // 2) * B + b, R) == 0

    tok = tokens.transpose(1, 0, 2)
    cot = cotangent.transpose(1, 0, 2)
    rows_f = tok.reshape(T, D).astype(f32)

    gains_all = lax.all_gather(
        jnp.concatenate([attn_gain, ffn_gain, qk_gain[0], qk_gain[1]]), AXES, axis=0).astype(f32)
    nq = qk_gain.shape[1]
    attn_g = gains_all[:, :W].reshape(-1)
    ffn_g = gains_all[:, W:2 * W].reshape(-1)
    qk_g = jnp.stack([gains_all[:, 2 * W:2 * W + nq].reshape(-1), gains_all[:, 2 * W + nq:].reshape(-1)])
    seq_tok = gather_blocks(tok, U, B, True, 1).reshape(L, D)
    heads_w = jnp.stack([w_query, w_key, w_value]).reshape(3, W, H, HD).transpose(2, 1, 0, 3).reshape(H, W, 3 * HD)
    head_w = to_all(heads_w[head_of]).reshape(D, 3 * HD)
    out_w = lax.all_gather(w_out, AXES, axis=0, tiled=True)

    expert_of = routes.transpose(1, 0, 2).reshape(-1)
    prio = order.reshape(positions, seqs, top_count).transpose(1, 0, 2).reshape(-1)
    same = expert_of[:, None] == expert_of[None, :]
    ranks = jnp.sum((same & (prio[None, :] < prio[:, None])).astype(jnp.int32), axis=1)
    slot = jnp.where(ranks < CAP, expert_of * CAP + ranks, -1).astype(f32)
    gate_flat = gates.transpose(1, 0, 2).reshape(-1)
    table = lax.all_gather(jnp.stack([slot, gate_flat]), AXES, axis=0)
    GB = 4
    G = F // GB
    KB = GB * T
    RB = -(-GB * CAP // 16) * 16
    span = E * CAP
    slot_all = table[:, 0].astype(jnp.int32).reshape(G, GB, T, top_count)
    code = jnp.where(slot_all >= 0, slot_all + jnp.arange(GB, dtype=jnp.int32)[None, :, None, None] * span, -1)
    code = code.reshape(G, KB, top_count)
    gate_all = table[:, 1].reshape(G, KB, top_count)
    r_ix = np.arange(RB)
    r_code = np.where(r_ix < GB * CAP, (r_ix // CAP) * span + r_ix % CAP, -(1 << 24)).astype(np.int32)
    want = (b * local_experts + jnp.arange(local_experts, dtype=jnp.int32))[:, None] * CAP + r_code[None, :]
    onehot = jnp.zeros((G, local_experts, RB, KB), jnp.bool_)
    row_gate = jnp.zeros((G, local_experts, RB), f32)
    for j in range(top_count):
        hit = code[:, None, None, :, j] == want[None, :, :, None]
        onehot = onehot | hit
        row_gate = row_gate + jnp.sum(jnp.where(hit, gate_all[:, None, None, :, j], 0.0), axis=-1)
    onehot = onehot.astype(bf16)
    row_gate = row_gate.transpose(1, 0, 2).reshape(local_experts, G * RB, 1)

    def first_norm(v):
        return rms_norm(v, attn_g)

    hidden = first_norm(seq_tok.astype(f32)).astype(bf16)
    raw = jnp.dot(hidden, head_w, preferred_element_type=f32)

    def head_norms(query_in, key_in, gains):
        return rotate(rms_norm(query_in, gains[0])), rotate(rms_norm(key_in, gains[1]))

    (rot_q, rot_k), heads_back = jax.vjp(head_norms, raw[:, :HD], raw[:, HD:2 * HD], qk_g)
    q, k, v = rot_q.astype(bf16), rot_k.astype(bf16), raw[:, 2 * HD:].astype(bf16)
    att, lse = attend(q, k, v.T)
    att_rows = to_all(att.reshape(F, positions, HD))

    def from_heads(m):
        m = m.reshape(U // 2, 2, B, positions, HD).transpose(1, 3, 0, 2, 4)
        return m.reshape(2, positions, H, R, HD)[:, :, :, 0].reshape(T, H * HD)

    attended = from_heads(att_rows)
    residual = rows_f + jnp.dot(attended, out_w, preferred_element_type=f32)
    normed_full, ffn_back = jax.vjp(rms_norm, residual, ffn_g)
    normed = normed_full.astype(bf16).reshape(2, positions, D)

    normed_all = gather_blocks(normed, U, B, False, 2).reshape(G, KB, D)
    cot_all = gather_blocks(cot, U, B, False, 2).reshape(G, KB, D)

    def dispatch(m):
        x = jnp.einsum("gert,gtd->egrd", onehot, m, preferred_element_type=f32)
        return x.reshape(local_experts, G * RB, D)

    def combine(m):
        m = m.reshape(local_experts, G, RB, D)
        return jnp.einsum("gert,egrd->gtd", onehot, m, preferred_element_type=f32).astype(bf16).reshape(F, 2, positions, D)

    x = dispatch(normed_all).astype(bf16)
    pair_grad = (dispatch(cot_all) * row_gate).astype(bf16)
    gate_act = jnp.einsum("erd,edf->erf", x, expert_gate, preferred_element_type=f32)
    up_act = jnp.einsum("erd,edf->erf", x, expert_up, preferred_element_type=f32)
    sigma = jax.nn.sigmoid(gate_act)
    inner = (gate_act * sigma * up_act).astype(bf16)
    part = jnp.einsum("erf,efd->erd", inner, expert_down, preferred_element_type=f32)
    mixed_part = combine((part * row_gate).astype(bf16))
    mixed = residual + scatter_blocks(mixed_part, U, B, False, 3).reshape(T, D)
    mixed = mixed.reshape(2, positions, D).transpose(1, 0, 2).astype(bf16)
    inner_grad = jnp.einsum("erd,efd->erf", pair_grad, expert_down, preferred_element_type=f32)
    gate_act_grad = (inner_grad * up_act * sigma * (1.0 + gate_act * (1.0 - sigma))).astype(bf16)
    up_act_grad = (inner_grad * gate_act * sigma).astype(bf16)
    row_grads = (
        jnp.einsum("erf,edf->erd", gate_act_grad, expert_gate, preferred_element_type=f32)
        + jnp.einsum("erf,edf->erd", up_act_grad, expert_up, preferred_element_type=f32)
    )
    gate_grad = jnp.einsum("erd,erf->edf", x, gate_act_grad, preferred_element_type=f32)
    up_grad = jnp.einsum("erd,erf->edf", x, up_act_grad, preferred_element_type=f32)
    down_grad = jnp.einsum("erf,erd->efd", inner, pair_grad, preferred_element_type=f32)
    normed_grad = scatter_blocks(combine(row_grads.astype(bf16)), U, B, False, 3).reshape(T, D)

    residual_norm_grad, ffn_gain_part = ffn_back(normed_grad)
    residual_grad = cot.reshape(T, D).astype(f32) + residual_norm_grad
    attn_out_grad = residual_grad.astype(bf16)
    att_grad = dot(attn_out_grad, out_w, 1, 1).astype(bf16)
    att_grad = att_grad.reshape(2, positions, H, HD)
    to_heads = jnp.stack([att_grad[seq_of[d], :, head_of[d]] for d in range(F)])
    do = to_all(to_heads).reshape(L, HD)
    out_part = dot(attended, attn_out_grad, 0, 0).astype(bf16)
    out_part = out_part.reshape(F, W, 2, D // 2).transpose(0, 2, 1, 3)
    out_grad = scatter_blocks(out_part, U, B, False, 5).transpose(1, 0, 2).reshape(W, D)
    dq, dk, dv = attend_back(q, do, lse, k, k.T, v)
    query_raw_grad, key_raw_grad, qk_part = heads_back(
        (dq.astype(bf16).astype(f32), dk.astype(bf16).astype(f32)))
    head_grad = jnp.concatenate(
        [query_raw_grad.astype(bf16), key_raw_grad.astype(bf16), dv.astype(bf16)], axis=-1)
    head_grad = jnp.where(first_copy, head_grad, jnp.zeros_like(head_grad))
    qk_part = jnp.where(first_copy, qk_part, 0.0)
    weight_part = to_all(dot(hidden, head_grad, 0, 0).astype(bf16).reshape(F, W, 3 * HD))
    weight_grad = jnp.sum(weight_part.reshape(U // 2, 2, B, W, 3 * HD).astype(f32), axis=1)
    weight_grad = weight_grad.reshape(H, R, W, 3 * HD).sum(axis=1).transpose(1, 0, 2).reshape(W, H, 3, HD)
    query_grad, key_grad, value_grad = (weight_grad[:, :, n].reshape(W, H * HD) for n in range(3))
    hidden_part = dot(head_grad, head_w, 1, 1).astype(bf16).reshape(F, positions, D)
    hidden_grad = scatter_blocks(hidden_part, U, B, True, 4).reshape(T, D)
    _, attn_back = jax.vjp(rms_norm, rows_f, attn_g)
    token_grad, attn_gain_part = attn_back(hidden_grad)
    input_grad = (residual_grad + token_grad).reshape(2, positions, D).transpose(1, 0, 2)
    small = jnp.concatenate(
        [attn_gain_part.reshape(F, W), ffn_gain_part.reshape(F, W),
         qk_part[0].reshape(F, nq), qk_part[1].reshape(F, nq)], axis=1)
    small = jnp.sum(to_all(small), axis=0)
    return (
        mixed, input_grad, query_grad, key_grad, value_grad, out_grad,
        small[:W], small[W:2 * W], small[2 * W:].reshape(2, nq),
        gate_grad, up_grad, down_grad,
    )


def solution(mesh):
    rows = P(AXES, None, None)
    flat = P(AXES, None)
    by_expert = (P("blk", None, "ulysses"), P("blk", None, "ulysses"), P("blk", "ulysses", None))
    in_specs = (rows, flat, flat, flat, flat, P(AXES), P(AXES), P(None, AXES)) + by_expert + (rows, rows, flat, rows)
    out_specs = (rows, rows, flat, flat, flat, flat, P(AXES), P(AXES), P(None, AXES)) + by_expert
    return jax.shard_map(body, mesh=mesh, in_specs=in_specs, out_specs=out_specs, check_vma=False)
```

time: 4330 us -> 1360 us (0.31)
  waiting for transfers between devices: 3090 us -> 8.41 us
  Pallas kernels: 0 us -> 622 us
  local copies, waits for them, and re-layouts: 355 us -> 159 us
  matrix products: 433 us -> 302 us
  starting transfers between devices: 90.4 us -> 24 us
  blocking collectives: 202 us -> 138 us
  other arithmetic: 129 us -> 82.8 us
    all_to_all x9 -> x5, waiting for transfers between devices: 1220 us -> 7.71 us  [to_all(): return lax.all_to_all(v, AXES, split_axis=0, concat_axis=0, tiled=True)]
    reduce_scatter x4 -> x0, waiting for transfers between devices: 926 us -> none  [the longest x1 360 us: body(): lax.psum_scatter(key_part_grad, ('ulysses', 'blk'), scatter_dimension=0,...]
    pallas_call x0 -> x9, Pallas kernels: none -> 622 us  [the longest x4 324 us: _scatter(): pl.pallas_call(functools.partial(scatter_kernel, U, B, by_seq), out_shape...]
    all_gather x6 -> x1, waiting for transfers between devices: 556 us -> 0.02 us  [body(): out_w = lax.all_gather(w_out, AXES, axis=0, tiled=True)]
    ppermute x32 -> x0, waiting for transfers between devices: 383 us -> none  [shifted(): lax.ppermute(value, axis, [(i, (i + by) % devices) for i in range(devices)])]
    dot_general x69 -> x19, matrix products: 433 us -> 302 us  [the longest x2 55.9 us: combine(): jnp.einsum('gert,egrd->gtd', onehot, m, preferred_element_type=f32)]
    convert_element_type x11 -> x4, local copies, waits for them, and re-layouts: 110 us -> 20.4 us  [the longest x1 17.9 us: body(): x = dispatch(normed_all).astype(bf16)]
    unnamed x2 -> x1, blocking collectives: 96.2 us -> 37 us
  transfers between devices with their start and end apart: 51 -> 6, of which waited for: 46 -> 1; matrix products, arithmetic and copies ran while one was open for 14% -> 17% of each run, Pallas kernels for 0% -> 18%
where the time goes in v1:
time: 1360 us; the launch traced here: 1350 us
  Pallas kernels  622 us (46%)
  matrix products  302 us (22%)
  local copies, waits for them, and re-layouts  159 us (12%)
  blocking collectives  138 us (10%)
  other arithmetic  82.8 us (6%)
  starting transfers between devices  24 us (2%)
  between operations  15.5 us (1%)
    pallas_call x4, Pallas kernels, _scatter(): pl.pallas_call(functools.partial(scatter_kernel, U, B, by_seq), out_shape...  324 us
    pallas_call x3, Pallas kernels, gather_blocks(): pl.pallas_call(functools.partial(gather_kernel, U, B, by_seq), out_shape=...  268 us
    all_gather x1, blocking collectives, body(): table = lax.all_gather(jnp.stack([slot, gate_flat]), AXES, axis=0)  101 us
    dot_general x2, matrix products, combine(): jnp.einsum('gert,egrd->gtd', onehot, m, preferred_element_type=f32)  55.9 us
    dot_general x2, matrix products, dispatch(): x = jnp.einsum('gert,gtd->egrd', onehot, m, preferred_element_type=f32)  52.1 us
    unnamed x1, blocking collectives  37 us
    unnamed x167, local copies, waits for them, and re-layouts  33.6 us
    dot_general x4, matrix products, dot(): lax.dot_general(a, b, (((ca,), (cb,)), ((), ())), preferred_element_type=...  30.3 us
  transfers between devices with their start and end apart: 6, of which 1 were waited for; matrix products, arithmetic and copies ran while one was open for 17% of the time, Pallas kernels for 18%

profile of v1, /device:TPU:0, one launch (start us, length us, event | category | flops | bytes accessed | tf_op | source)
XLA Modules:
  0.0 1352.2 jit_solution(12227449684744690255)
XLA Ops:
  16.2 7.4 all-to-all-start
  27.5 101.1 %all-gather.2 = f32[32,2,1024]{2,1,0:T(2,128)S(1)} all-gather(f32[1,2,1024]{2,1,0:T(2,128)S(1)} %maximum_bitcast_fusion.1), channel_id=3, replica_groups=mesh['ulysses'=4,'blk'=8] {'ulysses','blk'}, dimensions={0}, use_global_device_ids=true | all-gather | bytes 270336 | tf_op jit(solution)/shard_map/all_gather | solution.py:532
  130.9 8.6 slice_reduce_fusion.14
  140.7 8.3 slice_reduce_fusion.6
  149.1 9.8 fusion.12
  160.0 92.8 %shard_map.269 = bf16[32,2,64,2048]{3,2,1,0:T(8,128)(2,1)} custom-call(bf16[2,64,2048]{2,1,0:T(8,128)(2,1)} %bitcast.328), custom_call_target="tpu_custom_call" | custom-call | tf_op jit(solution)/shard_map/pallas_call | solution.py:188
  252.9 27.9 %convolution_bitcast_fusion = f32[8,8,80,2048]{3,2,0,1:T(8,128)} fusion(bf16[8,512,2048,1]{2,1,3,0:T(8,128)(2,1)} %bitcast.321, s32[8,512]{1,0:T(8,128)S(1)} %get-tuple-element.36, s32[8,512]{1,0:T(8,128)S(1)} %get-tuple-element.37, s32[8,512]{1,0:T(8,128)S(1)} %get-tuple-element.38, s32[8,512]{1,0:T(8,128)S(1)} %get-tuple-element.39, ...), kind=kOutput, calls=%fused_computation.17 | convolution fusion | flops 10776739840 | bytes 58853888 | tf_op jit(solution)/shard_map/gert,gtd->egrd/dot_general | solution.py:581
  280.8 29.0 %copy.349 = f32[8,8,80,2048]{3,2,1,0:T(8,128)} copy(f32[8,8,80,2048]{3,2,0,1:T(8,128)} %convolution_bitcast_fusion) | data formatting | bytes 83886080 | tf_op jit(solution)/shard_map/gert,gtd->egrd/transpose | solution.py:581
  310.1 37.0 %all-reduce.6 = bf16[4352]{0:T(1024)(128)(2,1)S(1)} all-reduce(bf16[4352]{0:T(1024)(128)(2,1)S(1)} %dynamic-update-slice), channel_id=2, replica_groups=mesh['ulysses'=4,'blk'=8] {'ulysses','blk'}, use_global_device_ids=true, to_apply=%add.6 | all-reduce | flops 4352 | bytes 17408
  348.4 82.5 %shard_map.265 = bf16[32,64,2048]{2,1,0:T(8,128)(2,1)} custom-call(bf16[2,64,2048]{2,1,0:T(8,128)(2,1)} %get-tuple-element.116.src), custom_call_target="tpu_custom_call" | custom-call | tf_op jit(solution)/shard_map/pallas_call | solution.py:188
  431.3 5.1 multiply_reduce_fusion
  438.0 8.8 multiply_convert_fusion.1
  446.8 21.6 %fusion = bf16[8,640,2048]{2,1,0:T(8,128)(2,1)} fusion(f32[8,8,80,2048]{3,2,1,0:T(8,128)} %copy.349, f32[8,640]{1,0:T(8,128)S(1)} %mul.531), kind=kLoop, calls=%fused_computation.2 | loop fusion | flops 20971520 | bytes 62935040 | tf_op jit(solution)/shard_map/convert_element_type | solution.py:589
  468.4 6.4 fusion.78
  483.1 12.6 shard_map.266
  495.7 4.0 all-to-all-start.1
  499.7 8.6 fusion.6
  508.4 7.7 all-to-all-done.1
  516.7 4.9 multiply_reduce_fusion.6
  523.6 92.4 %shard_map.267 = bf16[32,2,64,2048]{3,2,1,0:T(8,128)(2,1)} custom-call(bf16[2,64,2048]{2,1,0:T(8,128)(2,1)} %bitcast.337), custom_call_target="tpu_custom_call" | custom-call | tf_op jit(solution)/shard_map/pallas_call | solution.py:188
  616.0 24.2 %convert_bitcast_fusion = bf16[8,8,80,2048]{3,2,0,1:T(8,128)(2,1)} fusion(bf16[8,512,2048,1]{2,1,3,0:T(8,128)(2,1)} %bitcast.319, s32[8,512]{1,0:T(8,128)S(1)} %get-tuple-element.36, s32[8,512]{1,0:T(8,128)S(1)} %get-tuple-element.37, s32[8,512]{1,0:T(8,128)S(1)} %get-tuple-element.38, s32[8,512]{1,0:T(8,128)S(1)} %get-tuple-element.39, ...), kind=kOutput, calls=%fused_computation.11 | convolution fusion | flops 10787225600 | bytes 37882368 | tf_op jit(solution)/shard_map/gert,gtd->egrd/dot_general | solution.py:581
  640.1 17.9 %copy.344 = bf16[8,8,80,2048]{3,2,1,0:T(8,128)(2,1)} copy(bf16[8,8,80,2048]{3,2,0,1:T(8,128)(2,1)} %convert_bitcast_fusion) | data formatting | bytes 41943040 | tf_op jit(solution)/shard_map/convert_element_type | solution.py:588
  658.0 13.9 %fusion.79 = f32[8,640,256]{2,1,0:T(8,128)} fusion(bf16[8,640,2048]{2,1,0:T(8,128)(2,1)} %bitcast.311, bf16[8,2048,256]{2,1,0:T(8,128)(2,1)} %param.26), kind=kOutput, calls=%fused_computation.267 | convolution fusion | flops 5368709120 | bytes 34603008 | tf_op jit(solution)/shard_map/erd,edf->erf/dot_general | solution.py:590
  671.9 12.3 fusion.80
  684.2 18.8 %multiply_convert_fusion.2 = (bf16[8,640,256]{2,1,0:T(8,128)(2,1)}, bf16[8,640,256]{2,1,0:T(8,128)(2,1)}, bf16[8,640,256]{2,1,0:T(8,128)(2,1)S(1)}) fusion(f32[8,640,256]{2,1,0:T(8,128)} %fusion.79, f32[8,640,256]{2,1,0:T(8,128)} %fusion.80, bf16[8,640,2048]{2,1,0:T(8,128)(2,1)} %fusion, bf16[8,256,2048]{2,1,0:T(8,128)(2,1)} %param.28), kind=kOutput, calls=%fused_computation.44 | convolution fusion | flops 5389680640 | bytes 47710208 | tf_op jit(solution)/shard_map/erd,efd->erf/dot_general | solution.py:598
  703.0 13.4 multiply_convert_fusion
  716.3 27.8 %bitcast_convert_fusion.1 = bf16[8,512,2048]{2,1,0:T(8,128)(2,1)} fusion(bf16[8,8,80,2048]{3,2,1,0:T(8,128)(2,1)} %bitcast.317, s32[8,512]{1,0:T(8,128)S(1)} %get-tuple-element.36, s32[8,512]{1,0:T(8,128)S(1)} %get-tuple-element.37, s32[8,512]{1,0:T(8,128)S(1)} %get-tuple-element.38, s32[8,512]{1,0:T(8,128)S(1)} %get-tuple-element.39, ...), kind=kOutput, calls=%fused_computation.6 | convolution fusion | flops 10785128448 | bytes 37882368 | tf_op jit(solution)/shard_map/gert,egrd->gtd/dot_general | solution.py:586
  744.2 90.6 %shard_map.268 = f32[2,64,2048]{2,1,0:T(8,128)} custom-call(bf16[32,2,64,2048]{3,2,1,0:T(8,128)(2,1)} %bitcast.320), custom_call_target="tpu_custom_call" | custom-call | tf_op jit(solution)/shard_map/pallas_call | solution.py:375
  834.8 18.8 %fusion.81 = f32[8,640,2048]{2,1,0:T(8,128)} fusion(bf16[8,640,256]{2,1,0:T(8,128)(2,1)} %get-tuple-element.64, bf16[8,2048,256]{2,1,0:T(8,128)(2,1)} %param.26), kind=kOutput, calls=%fused_computation.269 | convolution fusion | flops 5368709120 | bytes 52953088 | tf_op jit(solution)/shard_map/erf,edf->erd/dot_general | solution.py:602
  853.6 25.9 %add_convert_fusion = bf16[8,640,2048]{2,1,0:T(8,128)(2,1)} fusion(f32[8,640,2048]{2,1,0:T(8,128)} %fusion.81, bf16[8,640,256]{2,1,0:T(8,128)(2,1)} %get-tuple-element.63, bf16[8,2048,256]{2,1,0:T(8,128)(2,1)} %param.27), kind=kOutput, calls=%fused_computation.3 | convolution fusion | flops 5389680640 | bytes 73924608 | tf_op jit(solution)/shard_map/erf,edf->erd/dot_general | solution.py:603
  879.5 28.0 %bitcast_convert_fusion = bf16[8,512,2048]{2,1,0:T(8,128)(2,1)} fusion(bf16[8,8,80,2048]{3,2,1,0:T(8,128)(2,1)} %bitcast.316, s32[8,512]{1,0:T(8,128)S(1)} %get-tuple-element.36, s32[8,512]{1,0:T(8,128)S(1)} %get-tuple-element.37, s32[8,512]{1,0:T(8,128)S(1)} %get-tuple-element.38, s32[8,512]{1,0:T(8,128)S(1)} %get-tuple-element.39, ...), kind=kOutput, calls=%fused_computation.5 | convolution fusion | flops 10785128448 | bytes 37882368 | tf_op jit(solution)/shard_map/gert,egrd->gtd/dot_general | solution.py:586
  907.6 90.4 %shard_map.270 = f32[2,64,2048]{2,1,0:T(8,128)} custom-call(bf16[32,2,64,2048]{3,2,1,0:T(8,128)(2,1)} %bitcast.318), custom_call_target="tpu_custom_call" | custom-call | tf_op jit(solution)/shard_map/pallas_call | solution.py:375
  1002.0 6.7 fusion.19
  1010.5 15.8 %fusion.82 = f32[8,2048,256]{2,1,0:T(8,128)} fusion(bf16[8,640,2048]{2,1,0:T(8,128)(2,1)} %bitcast.313, bf16[8,640,256]{2,1,0:T(8,128)(2,1)} %get-tuple-element.64), kind=kOutput, calls=%fused_computation.270 | convolution fusion | flops 5368709120 | bytes 40370176 | tf_op jit(solution)/shard_map/erd,erf->edf/dot_general | solution.py:605
  1051.8 17.5 %fusion.84 = f32[8,256,2048]{2,1,0:T(8,128)} fusion(bf16[8,640,256]{2,1,0:T(8,128)(2,1)S(1)} %get-tuple-element.65, bf16[8,640,2048]{2,1,0:T(8,128)(2,1)} %fusion), kind=kOutput, calls=%fused_computation.272 | convolution fusion | flops 5368709120 | bytes 40370176 | tf_op jit(solution)/shard_map/erf,erd->efd/dot_general | solution.py:607
  1070.1 17.6 %shard_map.271 = (f32[2048,128]{1,0:T(8,128)}, f32[2048,128]{1,0:T(8,128)}, f32[2048,128]{1,0:T(8,128)}) custom-call(bf16[2048,128]{1,0:T(8,128)(2,1)} %copy.336.q_ref, bf16[2048,128]{1,0:T(8,128)(2,1)} %bitcast.335, f32[1,2048]{1,0:T(1,128)} %get-tuple-element.18.lse_ref, bf16[2048,128]{1,0:T(8,128)(2,1)} %copy.337.k_ref, ...), custom_call_target="tpu_custom_call" | custom-call | tf_op jit(solution)/shard_map/pallas_call | solution.py:470
  1095.7 3.8 fusion.55
  1105.7 8.6 convolution_convert_fusion
  1114.4 91.1 %shard_map.272 = f32[2,64,2048]{2,1,0:T(8,128)} custom-call(bf16[32,64,2048]{2,1,0:T(8,128)(2,1)} %bitcast.324), custom_call_target="tpu_custom_call" | custom-call | tf_op jit(solution)/shard_map/pallas_call | solution.py:375
  1207.9 3.7 all-to-all-start.4
  1211.7 9.3 convolution_convert_fusion.2
  1220.9 5.9 all-to-all-start.3
  1226.9 5.8 convolution_convert_fusion.1
  1232.7 14.4 %reshape.406 = bf16[32,64,2,1024]{3,2,1,0:T(2,128)(2,1)} reshape(bf16[2048,2048]{1,0:T(8,128)(2,1)} %convolution_convert_fusion.1) | data formatting | bytes 16777216 | tf_op jit(solution)/shard_map/reshape | solution.py:618
  1247.1 9.7 copy.567
  1256.8 52.0 %shard_map.273 = f32[2,64,1024]{2,1,0:T(8,128)} custom-call(bf16[32,2,64,1024]{3,2,1,0:T(8,128)(2,1)} %bitcast.315), custom_call_target="tpu_custom_call" | custom-call | tf_op jit(solution)/shard_map/pallas_call | solution.py:375
  1312.0 16.0 %fusion.83 = f32[8,2048,256]{2,1,0:T(8,128)} fusion(bf16[8,640,2048]{2,1,0:T(8,128)(2,1)} %bitcast.314, bf16[8,640,256]{2,1,0:T(8,128)(2,1)} %get-tuple-element.63), kind=kOutput, calls=%fused_computation.271 | convolution fusion | flops 5368709120 | bytes 40370176 | tf_op jit(solution)/shard_map/erd,erf->edf/dot_general | solution.py:606
  1338.2 4.1 slice_reduce_fusion.16
  (277 shorter events, 96.0 us)
Async XLA Ops:
  11.7 13.2 copy-start.49
  11.7 14.1 %copy-start.40 = (s32[64,2,8]{0,2,1:T(8,128)S(1)}, s32[64,2,8]{0,2,1:T(8,128)}, u32[]{:S(2)}) copy-start(s32[64,2,8]{0,2,1:T(8,128)} %param.29) | copy-start | bytes 12292
  11.7 14.5 %copy-start.41 = (f32[64,2,8]{0,2,1:T(8,128)S(1)}, f32[64,2,8]{0,2,1:T(8,128)}, u32[]{:S(2)}) copy-start(f32[64,2,8]{0,2,1:T(8,128)} %param.30) | copy-start | bytes 12292
  16.2 452.2 %all-to-all-start = ((bf16[32,64,384]{2,1,0:T(8,128)(2,1)}), bf16[32,64,384]{2,1,0:T(8,128)(2,1)}, u32[]{:S(2)}, u32[]{:S(2)}) async-start(bf16[32,64,384]{2,1,0:T(8,128)(2,1)} %gather_fusion), calls=%async_computation | async-start | bytes 3145728 | tf_op jit(solution)/shard_map/all_to_all | solution.py:488
  23.6 493.1 %all-gather.5.cloned.1.call-start = ((), (), s32[]{:S(2)}) async-start(), calls=%async_computation.5 | async-start | bytes 8650752 | tf_op jit(solution)/shard_map/all_gather | solution.py:524
  140.7 18.4 %copy-start.25 = (bf16[64,2,2048]{2,1,0:T(2,128)(2,1)S(1)}, bf16[64,2,2048]{2,1,0:T(2,128)(2,1)}, u32[]{:S(2)}) copy-start(bf16[64,2,2048]{2,1,0:T(2,128)(2,1)} %param.32) | copy-start | bytes 1572868
  280.7 29.0 %copy-start.50 = (bf16[2,4]{1,0:T(2,128)(2,1)S(1)}, bf16[2,4]{1,0:T(2,128)(2,1)}, u32[]{:S(2)}) copy-start(bf16[2,4]{1,0:T(2,128)(2,1)} %param.25) | copy-start | bytes 52
  280.7 29.0 %copy-start.55 = (bf16[64]{0:T(256)(128)(2,1)S(1)}, bf16[64]{0:T(256)(128)(2,1)}, u32[]{:S(2)}) copy-start(bf16[64]{0:T(256)(128)(2,1)} %param.24) | copy-start | bytes 388
  280.7 29.0 %copy-start.56 = (bf16[64]{0:T(256)(128)(2,1)S(1)}, bf16[64]{0:T(256)(128)(2,1)}, u32[]{:S(2)}) copy-start(bf16[64]{0:T(256)(128)(2,1)} %param.23) | copy-start | bytes 388
  280.8 66.6 %copy-start.9 = (bf16[64,2,2048]{2,1,0:T(2,128)(2,1)S(1)}, bf16[64,2,2048]{2,1,0:T(2,128)(2,1)}, u32[]{:S(2)}) copy-start(bf16[64,2,2048]{2,1,0:T(2,128)(2,1)} %param.18) | copy-start | bytes 1572868
  347.4 152.3 %copy-start.26 = (f32[2048]{0:T(1024)}, f32[2048]{0:T(1024)S(1)}, u32[]{:S(2)}) copy-start(f32[2048]{0:T(1024)S(1)} %mul.492) | copy-start | bytes 24580
  431.1 44.7 %copy-start.42 = (f32[128]{0:T(128)}, f32[128]{0:T(128)S(1)}, u32[]{:S(2)}) copy-start(f32[128]{0:T(128)S(1)} %mul.498) | copy-start | bytes 1540
  431.2 44.6 %copy-start.44 = (f32[128]{0:T(128)}, f32[128]{0:T(128)S(1)}, u32[]{:S(2)}) copy-start(f32[128]{0:T(128)S(1)} %mul.511) | copy-start | bytes 1540
  431.3 90.4 %copy-start.28 = (f32[2048]{0:T(1024)}, f32[2048]{0:T(1024)S(1)}, u32[]{:S(2)}) copy-start(f32[2048]{0:T(1024)S(1)} %mul.526) | copy-start | bytes 24580
  438.0 38.5 %copy-start.51 = (f32[64]{0:T(128)}, f32[64]{0:T(128)S(1)}, u32[]{:S(2)}) copy-start(f32[64]{0:T(128)S(1)} %multiply_power_fusion) | copy-start | bytes 772
  438.0 38.5 %copy-start.34 = (f32[2048]{0:T(1024)}, f32[2048]{0:T(1024)S(1)}, u32[]{:S(2)}) copy-start(f32[2048]{0:T(1024)S(1)} %iota_convert_fusion) | copy-start | bytes 24580
  482.1 26.2 %copy-start.12 = (bf16[2048,128]{1,0:T(8,128)(2,1)}, bf16[2048,128]{1,0:T(8,128)(2,1)S(1)}, u32[]{:S(2)}) copy-start(bf16[2048,128]{1,0:T(8,128)(2,1)S(1)} %copy.434.v_ref) | copy-start | bytes 1572868
  495.7 20.4 %all-to-all-start.1 = ((bf16[32,64,128]{2,1,0:T(8,128)(2,1)}), bf16[32,64,128]{2,1,0:T(8,128)(2,1)S(1)}, u32[]{:S(2)}, u32[]{:S(2)}) async-start(bf16[32,64,128]{2,1,0:T(8,128)(2,1)} %bitcast.352), calls=%async_computation.1 | async-start | bytes 1048576 | tf_op jit(solution)/shard_map/all_to_all | solution.py:488
  521.6 94.3 %copy-start.53 = (f32[128]{0:T(128)}, f32[128]{0:T(128)S(1)}, u32[]{:S(2)}) copy-start(f32[128]{0:T(128)S(1)} %get-tuple-element.134) | copy-start | bytes 1540
  521.7 94.3 %copy-start.46 = (f32[128]{0:T(128)}, f32[128]{0:T(128)S(1)}, u32[]{:S(2)}) copy-start(f32[128]{0:T(128)S(1)} %fusion.65) | copy-start | bytes 1540
  640.1 31.7 %slice-start = ((s8[8388608]{0:T(1024)(128)(4,1)}), s8[4194304]{0:T(1024)(128)(4,1)S(1)}, s32[]{:S(2)}) async-start(s8[8388608]{0:T(1024)(128)(4,1)} %bitcast.322), calls=%async_computation.6 | async-start | bytes 8388608
  658.0 13.9 %slice-start.1 = ((s8[8388608]{0:T(1024)(128)(4,1)}), s8[4194304]{0:T(1024)(128)(4,1)S(1)}, s32[]{:S(2)}) async-start(s8[8388608]{0:T(1024)(128)(4,1)} %bitcast.322), calls=%async_computation.7 | async-start | bytes 8388608
  907.6 90.5 %copy-start.5 = (f32[128,2048]{1,0:T(8,128)S(1)}, f32[128,2048]{1,0:T(8,128)}, u32[]{:S(2)}) copy-start(f32[128,2048]{1,0:T(8,128)} %copy-done.4) | copy-start | bytes 3145732
  907.6 90.5 %copy-start.29 = (f32[2048]{0:T(1024)S(1)}, f32[2048]{0:T(1024)}, u32[]{:S(2)}) copy-start(f32[2048]{0:T(1024)} %copy-done.28) | copy-start | bytes 24580
  907.6 90.5 %copy-start.47 = (f32[128]{0:T(128)S(1)}, f32[128]{0:T(128)}, u32[]{:S(2)}) copy-start(f32[128]{0:T(128)} %copy-done.46) | copy-start | bytes 1540
  907.6 92.0 %copy-start.54 = (f32[128]{0:T(128)S(1)}, f32[128]{0:T(128)}, u32[]{:S(2)}) copy-start(f32[128]{0:T(128)} %copy-done.53) | copy-start | bytes 1540
  907.6 92.0 %copy-start.11 = (bf16[64,2,2048]{2,0,1:T(8,128)(2,1)S(1)}, bf16[64,2,2048]{2,0,1:T(8,128)(2,1)}, u32[]{:S(2)}) copy-start(bf16[64,2,2048]{2,0,1:T(8,128)(2,1)} %copy.574) | copy-start | bytes 1572868
  907.6 92.0 %copy-start.17 = (f32[2,64,2048]{2,1,0:T(8,128)S(1)}, f32[2,64,2048]{2,1,0:T(8,128)}, u32[]{:S(2)}) copy-start(f32[2,64,2048]{2,1,0:T(8,128)} %shard_map.268) | copy-start | bytes 3145732
  1048.8 20.5 %all-to-all-start.2 = ((bf16[32,64,128]{2,1,0:T(8,128)(2,1)}), bf16[32,64,128]{2,1,0:T(8,128)(2,1)S(1)}, u32[]{:S(2)}, u32[]{:S(2)}) async-start(bf16[32,64,128]{2,1,0:T(8,128)(2,1)} %constant_dynamic-update-slice_fusion), calls=%async_computation.2 | async-start | bytes 1048576 | tf_op jit(solution)/shard_map/all_to_all | solution.py:488
  1069.3 26.3 %copy-start.35 = (f32[2048]{0:T(1024)S(1)}, f32[2048]{0:T(1024)}, u32[]{:S(2)}) copy-start(f32[2048]{0:T(1024)} %copy-done.34) | copy-start | bytes 24580
  1069.3 26.3 %copy-start.52 = (f32[64]{0:T(128)S(1)}, f32[64]{0:T(128)}, u32[]{:S(2)}) copy-start(f32[64]{0:T(128)} %copy-done.51) | copy-start | bytes 772
  1087.7 12.5 copy-start.1
  1087.7 12.5 copy-start.31
  1087.7 12.5 copy-start.33
  1087.7 12.5 copy-start.43
  1087.7 12.5 copy-start.45
  1114.3 91.2 %copy-start.10 = (bf16[64,2,2048]{2,1,0:T(2,128)(2,1)S(1)}, bf16[64,2,2048]{2,1,0:T(2,128)(2,1)}, u32[]{:S(2)}) copy-start(bf16[64,2,2048]{2,1,0:T(2,128)(2,1)} %param.18) | copy-start | bytes 1572868
  1114.4 91.2 %copy-start.27 = (f32[2048]{0:T(1024)S(1)}, f32[2048]{0:T(1024)}, u32[]{:S(2)}) copy-start(f32[2048]{0:T(1024)} %copy-done.26) | copy-start | bytes 24580
  1114.4 91.2 %copy-start.48 = (f32[2,64]{1,0:T(2,128)S(1)}, f32[2,64]{1,0:T(2,128)}, u32[]{:S(2)}) copy-start(f32[2,64]{1,0:T(2,128)} %get-tuple-element.129) | copy-start | bytes 1540
  1114.4 97.3 %copy-start.21 = (bf16[2048,128]{0,1:T(8,128)(2,1)S(1)}, bf16[2048,128]{0,1:T(8,128)(2,1)}, u32[]{:S(2)}) copy-start(bf16[2048,128]{0,1:T(8,128)(2,1)} %copy.387) | copy-start | bytes 1572868
  1114.4 97.3 %copy-start.23 = (bf16[2048,128]{0,1:T(8,128)(2,1)S(1)}, bf16[2048,128]{0,1:T(8,128)(2,1)}, u32[]{:S(2)}) copy-start(bf16[2048,128]{0,1:T(8,128)(2,1)} %copy-done.22) | copy-start | bytes 1572868
  1207.9 13.0 all-to-all-start.4
  1211.6 15.3 %copy-start.3 = (f32[128,2048]{1,0:T(8,128)S(1)}, f32[128,2048]{1,0:T(8,128)}, u32[]{:S(2)}) copy-start(f32[128,2048]{1,0:T(8,128)} %copy-done.2) | copy-start | bytes 3145732
  1211.7 15.3 %copy-start.8 = (bf16[128,2048]{1,0:T(8,128)(2,1)S(1)}, bf16[128,2048]{1,0:T(8,128)(2,1)}, u32[]{:S(2)}) copy-start(bf16[128,2048]{1,0:T(8,128)(2,1)} %copy-done.7) | copy-start | bytes 1572868
  1220.9 110.8 %all-to-all-start.3 = ((bf16[32,64,384]{2,1,0:T(8,128)(2,1)}), bf16[32,64,384]{2,1,0:T(8,128)(2,1)}, u32[]{:S(2)}, u32[]{:S(2)}) async-start(bf16[32,64,384]{2,1,0:T(8,128)(2,1)} %bitcast.342), calls=%async_computation.3 | async-start | bytes 3145728 | tf_op jit(solution)/shard_map/all_to_all | solution.py:488
  1256.8 53.9 %copy-start.18 = (bf16[128,2048]{1,0:T(8,128)(2,1)S(1)}, bf16[128,2048]{1,0:T(8,128)(2,1)}, u32[]{:S(2)}) copy-start(bf16[128,2048]{1,0:T(8,128)(2,1)} %get-tuple-element.79) | copy-start | bytes 1572868
  1312.0 16.1 %copy-start.59 = (f32[128]{0:T(128)S(1)}, f32[128]{0:T(128)}, u32[]{:S(2)}) copy-start(f32[128]{0:T(128)} %add.221) | copy-start | bytes 1540
  1312.0 16.1 %copy-start.6 = (f32[2,64,2048]{2,1,0:T(8,128)S(1)}, f32[2,64,2048]{2,1,0:T(8,128)}, u32[]{:S(2)}) copy-start(f32[2,64,2048]{2,1,0:T(8,128)} %shard_map.272) | copy-start | bytes 3145732
  (20 other events, 77.0 us)
Sparse Core Ops, SparseCore 0:
  27.4 88.5 all-gather.4

commit v2 on v1

v2 whole, which is shorter than its diff:
```python
import functools
import math

import jax
import jax.numpy as jnp
import numpy as np
from jax import lax
from jax.experimental import pallas as pl
from jax.experimental.pallas import tpu as pltpu
from jax.sharding import PartitionSpec as P

HD = 128
CAP = 18
EPSILON = 1e-06
ROPE_BASE = 10000.0
AXES = ("ulysses", "blk")
MESH = pl.DeviceIdType.MESH


class Place:
    def __init__(self, U, B):
        self.U, self.B = U, B
        self.X, self.Y = U // 2, 2
        self.Z = B // self.Y
        self.Q, self.F = self.X * B, U * B
        u, b = lax.axis_index("ulysses"), lax.axis_index("blk")
        self.c, self.x = lax.rem(u, 2), lax.div(u, 2)
        self.y, self.z = lax.rem(b, self.Y), lax.div(b, self.Y)
        self.q = self.x * B + b
        self.me, self.sib = self.at(self.q, self.c), self.at(self.q, 1 - self.c)
        self.core_peer = self.dev(self.x, self.y, self.z, 1 - self.c)

    def dev(self, x, y, z, c):
        return (x * 2 + c, z * self.Y + y)

    def block(self, x, y, z, c):
        return (x * 2 + c) * self.B + z * self.Y + y

    def chip(self, x, y, z):
        return x * self.B + z * self.Y + y

    def at(self, q, c):
        return (lax.div(q, self.B) * 2 + c) * self.B + lax.rem(q, self.B)

    def chip_dev(self, q):
        return (lax.div(q, self.B) * 2 + self.c, lax.rem(q, self.B))

    def flat_dev(self, f):
        return (lax.div(f, self.B), lax.rem(f, self.B))

    def others(self, axis):
        n = {"x": self.X, "y": self.Y, "z": self.Z}[axis]
        i = {"x": self.x, "y": self.y, "z": self.z}[axis]
        return [lax.rem(i + o, n) for o in range(1, n)]

    def barrier(self, reach):
        sem = pltpu.get_barrier_semaphore()

        def greet(d):
            pl.semaphore_signal(sem, inc=1, device_id=d, device_id_type=MESH)

        if reach == "every":
            @pl.loop(1, self.F)
            def _(o):
                greet(self.flat_dev(lax.rem(self.me + o, self.F)))

            pl.semaphore_wait(sem, self.F - 1)
            return
        greet(self.core_peer)
        if reach == "all":
            @pl.loop(1, self.Q)
            def _(o):
                greet(self.chip_dev(lax.rem(self.q + o, self.Q)))

            pl.semaphore_wait(sem, self.Q)
            return
        for k in self.others("x"):
            greet(self.dev(k, self.y, self.z, self.c))
        for k in self.others("y"):
            greet(self.dev(self.x, k, self.z, self.c))
        count = self.X + self.Y - 1
        if reach == "chain":
            below, above = self.z > 0, self.z < self.Z - 1

            @pl.when(below)
            def _():
                greet(self.dev(self.x, self.y, self.z - 1, self.c))

            @pl.when(above)
            def _():
                greet(self.dev(self.x, self.y, self.z + 1, self.c))

            count = count + jnp.where(below, 1, 0) + jnp.where(above, 1, 0)
        else:
            for k in self.others("z"):
                greet(self.dev(self.x, self.y, k, self.c))
            count += self.Z - 1
        pl.semaphore_wait(sem, count)


def remote(src, dst, send, recv, dev):
    return pltpu.make_async_remote_copy(
        src_ref=src, dst_ref=dst, send_sem=send, recv_sem=recv, device_id=dev, device_id_type=MESH)


class Gather:
    def __init__(self, p, by_seq, src, out, send_sem, recv_sem, local_sem):
        self.p, self.by_seq, self.src, self.out = p, by_seq, src, out
        self.send_sem, self.recv_sem, self.local_sem = send_sem, recv_sem, local_sem
        self.steps = p.Z + 2
        self.started = []
        self.always = p.z >= 0

    @staticmethod
    def semaphores(U, B, by_seq):
        n = 1 if by_seq else 2
        dma = pltpu.SemaphoreType.DMA
        return [dma((4 + U // 2 - 1 + 1, n, U * B)), dma((n, U * B)), dma((1,))]

    def where(self, half, x, y, z):
        p = self.p
        if self.by_seq:
            f = p.block(x, y, z, half)
            return self.out.at[f], (0, f)
        f = p.block(x, y, z, p.c)
        return self.out.at[f, half], (half, f)

    def send(self, cond, src_ref, dst_ref, ix, way, dev):
        cp = remote(src_ref, dst_ref, self.send_sem.at[(way,) + ix], self.recv_sem.at[ix], dev)

        @pl.when(cond)
        def _():
            cp.start()

        self.started.append((cond, cp))

    def wait(self, ref, ix):
        remote(ref, ref, self.send_sem.at[(0,) + ix], self.recv_sem.at[ix], self.p.core_peer).wait_recv()

    def along(self, cond, half, x, y, z, axes):
        p = self.p
        ref, ix = self.where(half, x, y, z)
        for ax in axes:
            if ax == "core":
                if not self.by_seq:
                    self.send(cond, ref, ref, ix, 0, p.core_peer)
            elif ax == "up":
                self.send(cond & (p.z < p.Z - 1), ref, ref, ix, 1, p.dev(p.x, p.y, p.z + 1, p.c))
            elif ax == "down":
                self.send(cond & (p.z > 0), ref, ref, ix, 2, p.dev(p.x, p.y, p.z - 1, p.c))
            elif ax == "y":
                for i, k in enumerate(p.others("y")):
                    self.send(cond, ref, ref, ix, 3 + i, p.dev(p.x, k, p.z, p.c))
            else:
                for i, k in enumerate(p.others("x")):
                    self.send(cond, ref, ref, ix, 2 + p.Y + i, p.dev(k, p.y, p.z, p.c))

    def zs(self, step):
        p = self.p
        if step == 0:
            return [(self.always, p.z, ())]
        return [(p.z - step >= 0, p.z - step, ("up",)), (p.z + step < p.Z, p.z + step, ("down",))]

    def arrive(self, cond, half, x, y, z, axes):
        ref, ix = self.where(half, x, y, z)

        @pl.when(cond)
        def _():
            self.wait(ref, ix)

        self.along(cond, half, x, y, z, axes)

    def step(self, n):
        p = self.p
        if n == 0:
            if self.by_seq:
                cp = pltpu.make_async_copy(self.src.at[p.c], self.out.at[p.me], self.local_sem.at[0])
                cp.start()
                self.send(self.always, self.src.at[1 - p.c], self.out.at[p.me], (0, p.me), 0, p.core_peer)
                cp.wait()
                self.wait(self.out.at[p.sib], (0, p.sib))
            else:
                cp = pltpu.make_async_copy(self.src, self.out.at[p.me], self.local_sem.at[0])
                cp.start()
                cp.wait()
            for half in (0, 1):
                self.along(self.always, half, p.x, p.y, p.z, ("up", "down", "y", "x"))
            for half in (0, 1):
                self.along(self.always, half, p.x, p.y, p.z, ("core",))
            return
        if n < p.Z:
            for half in (0, 1):
                for cond, k, on in self.zs(n):
                    self.arrive(cond, half, p.x, p.y, k, on + ("y", "x", "core"))
        if n <= p.Z:
            for cond, k, _ in self.zs(n - 1):
                for j in p.others("y"):
                    self.arrive(cond, 0, p.x, j, k, ("x", "core"))
                for j in p.others("x"):
                    self.arrive(cond, 1, j, p.y, k, ("y", "core"))
        if n >= 2:
            for cond, k, _ in self.zs(n - 2):
                for j in p.others("x"):
                    self.arrive(cond, 0, j, p.y, k, ("core",))
                for i in p.others("y"):
                    self.arrive(cond, 1, p.x, i, k, ("core",))
                for j in p.others("x"):
                    for i in p.others("y"):
                        self.arrive(cond, 0, j, i, k, ("core",))
                        self.arrive(cond, 1, j, i, k, ("core",))

    def from_core(self, cond, x, y, z):
        f = self.p.block(x, y, z, 1 - self.p.c)

        @pl.when(cond)
        def _():
            for half in (0, 1):
                self.wait(self.out.at[f, half], (half, f))

    def end(self):
        p = self.p
        if not self.by_seq:
            for k in range(p.Z):
                for j in range(p.X):
                    for i in range(p.Y):
                        self.from_core(self.always, j, i, k)
        self.sent()

    def sent(self):
        for cond, cp in self.started:
            @pl.when(cond)
            def _(cp=cp):
                cp.wait_send()


class Spread:
    def __init__(self, p, same, src, out, send_sem, recv_sem):
        self.p, self.same, self.src, self.out = p, same, src, out
        self.send_sem, self.recv_sem = send_sem, recv_sem

    @staticmethod
    def semaphores(U, B):
        dma = pltpu.SemaphoreType.DMA
        return [dma((2, U * B // 2)), dma((U * B,))]

    def part(self, q):
        return self.src if self.same else self.src.at[q]

    def out_to(self, o):
        p = self.p
        q = lax.rem(p.q + o, p.Q)
        return remote(self.part(q), self.out.at[p.me], self.send_sem.at[0, q], self.recv_sem.at[p.me], p.chip_dev(q))

    def across(self, q):
        f = self.p.at(q, self.p.c)
        return remote(self.out.at[f], self.out.at[f], self.send_sem.at[1, q], self.recv_sem.at[f], self.p.core_peer)

    def arrive(self, f):
        remote(self.out.at[f], self.out.at[f], self.send_sem.at[0, 0], self.recv_sem.at[f], self.p.core_peer).wait_recv()

    def begin(self):
        p = self.p

        @pl.loop(1, p.Q)
        def _(o):
            self.out_to(o).start()

        cp = pltpu.make_async_copy(self.part(p.q), self.out.at[p.me], self.send_sem.at[0, p.q])
        cp.start()
        cp.wait()
        self.across(p.q).start()

    def middle(self):
        p = self.p

        @pl.loop(1, p.Q)
        def _(o):
            q = lax.rem(p.q + o, p.Q)
            self.arrive(p.at(q, p.c))
            self.across(q).start()

    def end(self):
        p = self.p

        @pl.loop(0, p.Q)
        def _(q):
            self.arrive(p.at(q, 1 - p.c))
            self.across(q).wait_send()

        @pl.loop(1, p.Q)
        def _(o):
            self.out_to(o).wait_send()


def any_specs(n):
    return [pl.BlockSpec(memory_space=pl.ANY)] * n


def gather_kernel(U, B, by_seq, src, out, *sems):
    p = Place(U, B)
    p.barrier("chain")
    g = Gather(p, by_seq, src, out, *sems)
    for n in range(g.steps):
        g.step(n)
    g.end()


def gather_blocks(v, U, B, by_seq, cid):
    shape = (U * B,) + (v.shape[1:] if by_seq else v.shape)
    return pl.pallas_call(
        functools.partial(gather_kernel, U, B, by_seq),
        out_shape=jax.ShapeDtypeStruct(shape, v.dtype),
        in_specs=any_specs(1),
        out_specs=any_specs(1)[0],
        scratch_shapes=Gather.semaphores(U, B, by_seq),
        compiler_params=pltpu.CompilerParams(collective_id=cid, has_side_effects=True),
    )(v)


def front_kernel(U, B, tok, small, weights, tok_out, small_out, weights_out, *sems):
    p = Place(U, B)
    p.barrier("all")
    g = Gather(p, True, tok, tok_out, *sems[:3])
    s = Spread(p, True, small, small_out, *sems[3:5])
    w = Spread(p, False, weights, weights_out, *sems[5:7])
    s.begin()
    g.step(0)
    w.begin()
    for n in range(1, g.steps):
        g.step(n)
        if n == 1:
            s.middle()
        if n == 2:
            w.middle()
    s.end()
    w.end()
    g.end()


def front(tok, small, weights, U, B, cid):
    F = U * B
    return pl.pallas_call(
        functools.partial(front_kernel, U, B),
        out_shape=[
            jax.ShapeDtypeStruct((F,) + tok.shape[1:], tok.dtype),
            jax.ShapeDtypeStruct((F,) + small.shape, small.dtype),
            jax.ShapeDtypeStruct((F,) + weights.shape[1:], weights.dtype),
        ],
        in_specs=any_specs(3),
        out_specs=any_specs(3),
        scratch_shapes=Gather.semaphores(U, B, True) + Spread.semaphores(U, B) * 2,
        compiler_params=pltpu.CompilerParams(collective_id=cid, has_side_effects=True),
    )(tok, small, weights)


def exchange_kernel(U, B, src, out, send_sem, recv_sem):
    p = Place(U, B)
    p.barrier("every")

    def copy(o):
        f = lax.rem(p.me + o, p.F)
        return f, remote(src.at[f], out.at[p.me], send_sem.at[f], recv_sem.at[p.me], p.flat_dev(f))

    @pl.loop(1, p.F)
    def _(o):
        copy(o)[1].start()

    cp = pltpu.make_async_copy(src.at[p.me], out.at[p.me], recv_sem.at[p.me])
    cp.start()
    cp.wait()

    @pl.loop(1, p.F)
    def _(o):
        f, cp = copy(o)
        remote(out.at[f], out.at[f], send_sem.at[f], recv_sem.at[f], p.flat_dev(f)).wait_recv()
        cp.wait_send()


def exchange(v, U, B, cid):
    return pl.pallas_call(
        functools.partial(exchange_kernel, U, B),
        out_shape=jax.ShapeDtypeStruct(v.shape, v.dtype),
        in_specs=any_specs(1),
        out_specs=any_specs(1)[0],
        scratch_shapes=[pltpu.SemaphoreType.DMA((U * B,))] * 2,
        compiler_params=pltpu.CompilerParams(collective_id=cid, has_side_effects=True),
    )(v)


class Scatter:
    def __init__(self, p, by_seq, acc, rc, rx0, rx1, ry0, ry1, rz, fin, loc, cs, cr, xs, xr, ys, yr, zs, zr):
        self.p, self.by_seq = p, by_seq
        self.acc, self.rc, self.rx, self.ry, self.rz, self.fin = acc, rc, (rx0, rx1), (ry0, ry1), rz, fin
        self.loc, self.cs, self.cr = loc, cs, cr
        self.xs, self.xr, self.ys, self.yr, self.zs, self.zr = xs, xr, ys, yr, zs, zr
        self.order = p.others("z") + [p.z]
        self.steps = p.Z + 2
        self.started = []
        self.local = True

    @staticmethod
    def scratch(U, B, by_seq, rows, D, t):
        X, Y, Z, Q = U // 2, 2, B // 2, U * B // 2
        dma = pltpu.SemaphoreType.DMA
        x, y = max(X - 1, 1), Y - 1
        return [
            pltpu.VMEM((Q, 2, rows, D), t),
            pltpu.VMEM((1, 1, 16, 128) if by_seq else (Q, 2, rows, D), t),
            pltpu.VMEM((x, Z * Y, rows, D), t),
            pltpu.VMEM((x, Z, rows, D), t),
            pltpu.VMEM((y, Z, rows, D), t),
            pltpu.VMEM((y, Z * X, rows, D), t),
            pltpu.VMEM((2, Z, rows, D), t),
            pltpu.VMEM((2, rows, D), jnp.float32),
            dma((Q, 2)),
            dma((Q, 2)),
            dma((Q, 2)),
            dma((2, x, Z * Y)),
            dma((2, x, Z * Y)),
            dma((2, y, Z * X)),
            dma((2, y, Z * X)),
            dma((2, Z)),
            dma((2, Z)),
        ]

    SCRATCH = 17

    def start(self, *a):
        cp = remote(*a)
        cp.start()
        self.started.append(cp)

    def got(self, ref, sem):
        remote(ref, ref, sem, sem, self.p.core_peer).wait_recv()

    def pieces(self, k):
        p = self.p
        ox, oy = p.others("x"), p.others("y")
        return (
            [(0, j, i, k) for j in ox for i in range(p.Y)] + [(1, j, i, k) for i in oy for j in range(p.X)],
            [(0, p.x, i, k) for i in oy] + [(1, j, p.y, k) for j in ox],
            [(0, p.x, p.y, k), (1, p.x, p.y, k)],
        )

    def load(self, src):
        p = self.p
        for k in self.order:
            for some in self.pieces(k):
                for h, j, i, _ in some:
                    q = p.chip(j, i, k)
                    if self.by_seq:
                        mine = src.at[p.block(j, i, k, h)]
                    else:
                        self.across(src.at[p.block(j, i, k, 1 - p.c), h], q, h)
                        mine = src.at[p.block(j, i, k, p.c), h]
                    pltpu.make_async_copy(mine, self.acc.at[q, h], self.loc.at[q, h]).start()

    def across(self, src, q, h):
        self.start(src, self.rc.at[q, h], self.cs.at[q, h], self.cr.at[q, h], self.p.core_peer)

    def ready(self, h, j, i, k):
        q = self.p.chip(j, i, k)
        if self.local:
            pltpu.make_async_copy(self.acc.at[q, h], self.acc.at[q, h], self.loc.at[q, h]).wait()
        if self.by_seq:
            return []
        self.got(self.rc.at[q, h], self.cr.at[q, h])
        return [self.rc.at[q, h]]

    def add(self, dst, srcs, f32_out=None):
        if not srcs and f32_out is None:
            return
        step = 16

        def one(n, _):
            r = pl.ds(pl.multiple_of(n * step, step), step)
            t = dst[r, :].astype(jnp.float32)
            for s in srcs:
                t = t + s[r, :].astype(jnp.float32)
            if f32_out is None:
                dst[r, :] = t.astype(dst.dtype)
            else:
                f32_out[r, :] = t
            return 0

        lax.fori_loop(0, dst.shape[0] // step, one, 0)

    def send_x(self, h, q, j, s):
        p = self.p
        o = lax.rem(j - p.x + p.X, p.X) - 1
        self.start(self.acc.at[q, h], self.rx[h].at[o, s], self.xs.at[h, o, s], self.xr.at[h, o, s],
                   p.dev(j, p.y, p.z, p.c))

    def send_y(self, h, q, i, s):
        p = self.p
        o = lax.rem(i - p.y + p.Y, p.Y) - 1
        self.start(self.acc.at[q, h], self.ry[h].at[o, s], self.ys.at[h, o, s], self.yr.at[h, o, s],
                   p.dev(p.x, i, p.z, p.c))

    def from_x(self, h, s):
        out = []
        for o in range(self.p.X - 1):
            self.got(self.rx[h].at[o, s], self.xr.at[h, o, s])
            out.append(self.rx[h].at[o, s])
        return out

    def from_y(self, h, s):
        out = []
        for o in range(self.p.Y - 1):
            self.got(self.ry[h].at[o, s], self.yr.at[h, o, s])
            out.append(self.ry[h].at[o, s])
        return out

    def step(self, n):
        p = self.p
        X, Y, Z = p.X, p.Y, p.Z
        if n < Z:
            k = self.order[n]
            for h, j, i, _ in self.pieces(k)[0]:
                q = p.chip(j, i, k)
                self.add(self.acc.at[q, h], self.ready(h, j, i, k))
                if h == 0:
                    self.send_x(0, q, j, k * Y + i)
                else:
                    self.send_y(1, q, i, k * X + j)
        if 1 <= n <= Z:
            k = self.order[n - 1]
            for h, j, i, _ in self.pieces(k)[1]:
                q = p.chip(j, i, k)
                extra = self.ready(h, j, i, k)
                if h == 0:
                    self.add(self.acc.at[q, 0], extra + self.from_x(0, k * Y + i))
                    self.send_y(0, q, i, k)
                else:
                    self.add(self.acc.at[q, 1], extra + self.from_y(1, k * X + j))
                    self.send_x(1, q, j, k)
        if n >= 2:
            k = self.order[n - 2]
            for h, j, i, _ in self.pieces(k)[2]:
                q = p.chip(j, i, k)
                extra = self.ready(h, j, i, k)
                if h == 0:
                    extra = extra + self.from_x(0, k * Y + i) + self.from_y(0, k)
                else:
                    extra = extra + self.from_y(1, k * X + j) + self.from_x(1, k)
                if n - 2 < Z - 1:
                    self.add(self.acc.at[q, h], extra)
                    self.start(self.acc.at[q, h], self.rz.at[h, p.z], self.zs.at[h, k], self.zr.at[h, p.z],
                               p.dev(p.x, p.y, k, p.c))
                else:
                    for a in p.others("z"):
                        self.got(self.rz.at[h, a], self.zr.at[h, a])
                        extra.append(self.rz.at[h, a])
                    self.add(self.acc.at[q, h], extra, self.fin.at[h])

    def sent(self):
        for cp in self.started:
            cp.wait_send()


def give(p, by_seq, fin, out, sems):
    if by_seq:
        away = remote(fin.at[1 - p.c], out.at[p.c], sems.at[0], sems.at[1], p.core_peer)
        away.start()
        cp = pltpu.make_async_copy(fin.at[p.c], out.at[p.c], sems.at[2])
        cp.start()
        cp.wait()
        remote(out.at[1 - p.c], out.at[1 - p.c], sems.at[0], sems.at[1], p.core_peer).wait_recv()
        away.wait_send()
    else:
        cp = pltpu.make_async_copy(fin, out, sems.at[2])
        cp.start()
        cp.wait()


def scatter_kernel(U, B, by_seq, src, out, *scratch):
    p = Place(U, B)
    p.barrier("lines")
    s = Scatter(p, by_seq, *scratch[:Scatter.SCRATCH])
    s.load(src)
    for n in range(s.steps):
        s.step(n)
    give(p, by_seq, s.fin, out, scratch[-1])
    s.sent()


def in_parts(call, v, F, D):
    parts = max(1, F * D // 65536)
    w = D // parts
    return jnp.concatenate([call(v[..., n * w:(n + 1) * w]) for n in range(parts)], axis=-1)


def scatter_blocks(v, U, B, by_seq, cid):
    def call(m):
        rows, D = m.shape[-2:]
        return pl.pallas_call(
            functools.partial(scatter_kernel, U, B, by_seq),
            out_shape=jax.ShapeDtypeStruct((2, rows, D), jnp.float32),
            in_specs=any_specs(1),
            out_specs=any_specs(1)[0],
            scratch_shapes=Scatter.scratch(U, B, by_seq, rows, D, m.dtype) + [pltpu.SemaphoreType.DMA((3,))],
            compiler_params=pltpu.CompilerParams(
                collective_id=cid, has_side_effects=True, vmem_limit_bytes=58 * 2**20),
        )(m)

    return in_parts(call, v, U * B, v.shape[-1])


def pair_kernel(U, B, n, *refs):
    p = Place(U, B)
    p.barrier("lines")
    srcs, outs, scratch = refs[:n], refs[n:2 * n], refs[2 * n:]
    work = [Scatter(p, False, *scratch[Scatter.SCRATCH * i:Scatter.SCRATCH * (i + 1)]) for i in range(n)]
    for s, src in zip(work, srcs):
        s.load(src)
    for k in range(work[0].steps):
        for s in work:
            s.step(k)
    for i, s in enumerate(work):
        give(p, False, s.fin, outs[i], scratch[-1])
        s.sent()


def scatter_pair(a, b, U, B, cid):
    def call(v, w):
        rows, D = v.shape[-2:]
        return pl.pallas_call(
            functools.partial(pair_kernel, U, B, 2),
            out_shape=[jax.ShapeDtypeStruct((2, rows, D), jnp.float32)] * 2,
            in_specs=any_specs(2),
            out_specs=any_specs(2),
            scratch_shapes=Scatter.scratch(U, B, False, rows, D, v.dtype) * 2 + [pltpu.SemaphoreType.DMA((3,))],
            compiler_params=pltpu.CompilerParams(
                collective_id=cid, has_side_effects=True, vmem_limit_bytes=60 * 2**20),
        )(v, w)

    parts = max(1, U * B // 32)
    w = a.shape[-1] // parts
    got = [call(a[..., n * w:(n + 1) * w], b[..., n * w:(n + 1) * w]) for n in range(parts)]
    return tuple(jnp.concatenate([g[i] for g in got], axis=-1) for i in range(2))


class PairExchange:
    def __init__(self, p, src, out, acc, rc, local, send, recv):
        self.p, self.src, self.out, self.acc, self.rc = p, src, out, acc, rc
        self.local, self.send, self.recv = local, send, recv

    @staticmethod
    def scratch(U, B, rows, w, t):
        X, Q = U // 2, U * B // 2
        dma = pltpu.SemaphoreType.DMA
        return [pltpu.VMEM((Q, rows, w), t), pltpu.VMEM((Q, rows, w), t),
                dma((X,)), dma((X + Q,)), dma((X + Q,))]

    SCRATCH = 5

    def across(self, j):
        p = self.p
        part = self.rc.at[pl.ds(j * p.B, p.B)]
        return remote(self.src.at[j, 1 - p.c], part, self.send.at[j], self.recv.at[j], p.core_peer)

    def own(self, j):
        p = self.p
        return pltpu.make_async_copy(self.src.at[j, p.c], self.acc.at[pl.ds(j * p.B, p.B)], self.local.at[j])

    def away(self, o):
        p = self.p
        q = lax.rem(p.q + o, p.Q)
        return remote(self.acc.at[q], self.out.at[p.q], self.send.at[p.X + q], self.recv.at[p.X + p.q], p.chip_dev(q))

    def begin(self):
        for j in range(self.p.X):
            self.across(j).start()
            self.own(j).start()

    def middle(self):
        p = self.p
        for j in range(p.X):
            self.own(j).wait()
            self.across(j).wait_recv()

        @pl.loop(0, p.Q)
        def _(q):
            t = self.acc[q].astype(jnp.float32) + self.rc[q].astype(jnp.float32)
            self.acc[q] = t.astype(self.acc.dtype)

        @pl.loop(1, p.Q)
        def _(o):
            self.away(o).start()

        cp = pltpu.make_async_copy(self.acc.at[p.q], self.out.at[p.q], self.local.at[0])
        cp.start()
        cp.wait()

    def end(self):
        p = self.p
        for j in range(p.X):
            self.across(j).wait_send()

        @pl.loop(1, p.Q)
        def _(o):
            q = lax.rem(p.q + o, p.Q)
            part = self.out.at[q]
            remote(part, part, self.send.at[0], self.recv.at[p.X + q], p.core_peer).wait_recv()
            self.away(o).wait_send()


def finish_kernel(U, B, more, *refs):
    p = Place(U, B)
    p.barrier("all")
    n = 4 if more else 3
    srcs, outs, scratch = refs[:n], refs[n:2 * n], refs[2 * n:]
    k = Scatter.SCRATCH
    work = [Scatter(p, True, *scratch[:k])]
    if more:
        work.append(Scatter(p, False, *scratch[k:2 * k]))
    ex, at = [], k * len(work)
    for i in range(2):
        ex.append(PairExchange(p, srcs[i], outs[i], *scratch[at:at + PairExchange.SCRATCH]))
        at += PairExchange.SCRATCH
    for e in ex:
        e.begin()
    for s, src in zip(work, srcs[2:]):
        s.load(src)
    work[0].step(0)
    for e in ex:
        e.middle()
    for s in work[1:]:
        s.step(0)
    for j in range(1, p.Z + 2):
        for s in work:
            s.step(j)
    for s, out, by_seq in zip(work, outs[2:], (True, False)):
        give(p, by_seq, s.fin, out, scratch[-1])
    for s in work:
        s.sent()
    for e in ex:
        e.end()


def finish(weights, small, hidden, out, U, B, cid):
    X, F, Q = U // 2, U * B, U * B // 2
    parts = max(1, F // 32)
    rows, D = hidden.shape[-2:]
    D = D // parts
    sds, f32 = jax.ShapeDtypeStruct, jnp.float32

    def call(w, s, h, o):
        args = [w.reshape((X, 2, B) + w.shape[1:]), s.reshape((X, 2, B) + s.shape[1:]), h]
        shapes = [sds((Q,) + w.shape[1:], w.dtype), sds((Q,) + s.shape[1:], s.dtype), sds((2,) + h.shape[1:], f32)]
        scratch = Scatter.scratch(U, B, True, h.shape[1], h.shape[2], h.dtype)
        if o is not None:
            args.append(o)
            shapes.append(sds(o.shape[1:], f32))
            scratch += Scatter.scratch(U, B, False, o.shape[2], o.shape[3], o.dtype)
        for m in (w, s):
            scratch += PairExchange.scratch(U, B, m.shape[1], m.shape[2], m.dtype)
        return pl.pallas_call(
            functools.partial(finish_kernel, U, B, o is not None),
            out_shape=shapes,
            in_specs=any_specs(len(args)),
            out_specs=any_specs(len(args)),
            scratch_shapes=scratch + [pltpu.SemaphoreType.DMA((3,))],
            compiler_params=pltpu.CompilerParams(
                collective_id=cid, has_side_effects=True, vmem_limit_bytes=60 * 2**20),
        )(*args)

    if parts == 1:
        return call(weights, small, hidden, out)
    w, s, h = call(weights, small, hidden[..., :D], None)
    rest = [scatter_blocks(hidden[..., n * D:(n + 1) * D], U, B, True, cid + 1) for n in range(1, parts)]
    return w, s, jnp.concatenate([h] + rest, axis=-1), scatter_by_permutes(out, U, B)


def scatter_by_permutes(v, U, B):
    X, Y, Z = U // 2, 2, B // 2
    f32 = jnp.float32
    u, b = lax.axis_index("ulysses"), lax.axis_index("blk")
    c, x, y, z = lax.rem(u, 2), lax.div(u, 2), lax.rem(b, Y), lax.div(b, Y)
    where = {"c": c, "x": x, "y": y, "z": z}
    size = {"c": 2, "x": X, "y": Y, "z": Z}

    def pairs(axis, by):
        out = []
        for f in range(U * B):
            at = {"x": f // B // 2, "c": f // B % 2, "z": f % B // Y, "y": f % Y}
            at[axis] = (at[axis] + by) % size[axis]
            out.append((f, (at["x"] * 2 + at["c"]) * B + at["z"] * Y + at["y"]))
        return out

    def fold(m, axis, dim):
        n = size[axis]
        total = lax.dynamic_index_in_dim(m, where[axis], dim, keepdims=False).astype(f32)
        for by in range(1, n):
            part = lax.dynamic_index_in_dim(m, lax.rem(where[axis] + by, n), dim, keepdims=False)
            total = total + lax.ppermute(part, ("ulysses", "blk"), pairs(axis, by)).astype(f32)
        return total

    rows, D = v.shape[-2:]
    m = fold(v.reshape(X, 2, Z, Y, 2, rows, D), "c", 1).astype(v.dtype)
    first = fold(m[:, :, :, 0], "x", 0).astype(v.dtype)
    first = fold(first, "y", 1).astype(v.dtype)
    second = fold(m[:, :, :, 1], "y", 2).astype(v.dtype)
    second = fold(second, "x", 0).astype(v.dtype)
    return fold(jnp.stack([first, second], axis=1), "z", 0)


def rms_norm(values, gains):
    return values * lax.rsqrt(jnp.mean(values * values, axis=-1, keepdims=True) + EPSILON) * gains


def dot(a, b, ca, cb):
    return lax.dot_general(a, b, (((ca,), (cb,)), ((), ())), preferred_element_type=jnp.float32)


def attend_kernel(scale, q_ref, k_ref, vt_ref, o_ref, lse_ref):
    s = dot(k_ref[...], q_ref[...], 1, 1) * scale
    top = jnp.max(s, axis=0, keepdims=True)
    e = jnp.exp(s - top)
    total = jnp.sum(e, axis=0, keepdims=True)
    o = dot(vt_ref[...], e.astype(jnp.bfloat16), 1, 0) / total
    o_ref[...] = o.T.astype(o_ref.dtype)
    lse_ref[...] = top + jnp.log(total)


def attend(q, k, vt):
    n = q.shape[0]
    bq = 256 if n <= 2048 else 128
    return pl.pallas_call(
        functools.partial(attend_kernel, 1.0 / math.sqrt(HD)),
        grid=(n // bq,),
        in_specs=[
            pl.BlockSpec((bq, HD), lambda i: (i, 0)),
            pl.BlockSpec((n, HD), lambda i: (0, 0)),
            pl.BlockSpec((HD, n), lambda i: (0, 0)),
        ],
        out_specs=[pl.BlockSpec((bq, HD), lambda i: (i, 0)), pl.BlockSpec((1, bq), lambda i: (0, i))],
        out_shape=[jax.ShapeDtypeStruct((n, HD), jnp.bfloat16), jax.ShapeDtypeStruct((1, n), jnp.float32)],
        compiler_params=pltpu.CompilerParams(vmem_limit_bytes=58 * 2**20),
    )(q, k, vt)


def attend_back_kernel(scale, q_ref, do_ref, lse_ref, k_ref, kt_ref, v_ref, dq_ref, dk_ref, dv_ref):
    @pl.when(pl.program_id(0) == 0)
    def _():
        dk_ref[...] = jnp.zeros_like(dk_ref)
        dv_ref[...] = jnp.zeros_like(dv_ref)

    p = jnp.exp(dot(k_ref[...], q_ref[...], 1, 1) * scale - lse_ref[...])
    dp = dot(v_ref[...], do_ref[...], 1, 1)
    delta = jnp.sum(p * dp, axis=0, keepdims=True)
    ds = (p * (dp - delta)).astype(jnp.bfloat16)
    dv_ref[...] += dot(p.astype(jnp.bfloat16), do_ref[...], 1, 0)
    dk_ref[...] += dot(ds, q_ref[...], 1, 0) * scale
    dq_ref[...] = (dot(kt_ref[...], ds, 1, 0) * scale).T


def attend_back(q, do, lse, k, kt, v):
    n = q.shape[0]
    bq = 256 if n <= 2048 else 128
    row = lambda i: (i, 0)
    whole = lambda i: (0, 0)
    f32 = jax.ShapeDtypeStruct((n, HD), jnp.float32)
    return pl.pallas_call(
        functools.partial(attend_back_kernel, 1.0 / math.sqrt(HD)),
        grid=(n // bq,),
        in_specs=[
            pl.BlockSpec((bq, HD), row),
            pl.BlockSpec((bq, HD), row),
            pl.BlockSpec((1, bq), lambda i: (0, i)),
            pl.BlockSpec((n, HD), whole),
            pl.BlockSpec((HD, n), whole),
            pl.BlockSpec((n, HD), whole),
        ],
        out_specs=[pl.BlockSpec((bq, HD), row), pl.BlockSpec((n, HD), whole), pl.BlockSpec((n, HD), whole)],
        out_shape=[f32, f32, f32],
        compiler_params=pltpu.CompilerParams(vmem_limit_bytes=58 * 2**20),
    )(q, do, lse, k, kt, v)


def turn(v, cosine, sine):
    return v * cosine + pltpu.roll(v, HD // 2, 1) * sine


def project_kernel(tok_ref, gain_ref, w_ref, qk_ref, cos_ref, sin_ref,
                   q_ref, k_ref, v_ref, kt_ref, vt_ref, rq_ref, rk_ref):
    bf16 = jnp.bfloat16
    raw = dot(rms_norm(tok_ref[...].astype(jnp.float32), gain_ref[...]).astype(bf16), w_ref[...], 1, 0)
    rq, rk, v = raw[:, :HD], raw[:, HD:2 * HD], raw[:, 2 * HD:].astype(bf16)
    rq_ref[...] = rq
    rk_ref[...] = rk
    q_ref[...] = turn(rms_norm(rq, qk_ref[0:1]), cos_ref[...], sin_ref[...]).astype(bf16)
    k = turn(rms_norm(rk, qk_ref[1:2]), cos_ref[...], sin_ref[...])
    k_ref[...] = k.astype(bf16)
    kt_ref[...] = k.T.astype(bf16)
    v_ref[...] = v
    vt_ref[...] = raw[:, 2 * HD:].T.astype(bf16)


def project(tok, gain, w, qk, cosine, sine):
    n, D = tok.shape
    bm = 256
    row, whole = (lambda i: (i, 0)), (lambda i: (0, 0))
    head, across = pl.BlockSpec((bm, HD), row), pl.BlockSpec((HD, bm), lambda i: (0, i))
    sds = jax.ShapeDtypeStruct
    f32, bf16 = jnp.float32, jnp.bfloat16
    return pl.pallas_call(
        project_kernel,
        grid=(n // bm,),
        in_specs=[
            pl.BlockSpec((bm, D), row), pl.BlockSpec((1, D), whole), pl.BlockSpec((D, 3 * HD), whole),
            pl.BlockSpec((2, HD), whole), head, head,
        ],
        out_specs=[head, head, head, across, across, head, head],
        out_shape=[sds((n, HD), bf16)] * 3 + [sds((HD, n), bf16)] * 2 + [sds((n, HD), f32)] * 2,
        compiler_params=pltpu.CompilerParams(vmem_limit_bytes=58 * 2**20),
    )(tok, gain, w, qk, cosine, sine)


def head_back_kernel(dq_ref, dk_ref, dv_ref, rq_ref, rk_ref, cos_ref, sin_ref, qk_ref, tok_ref, gain_ref, w_ref,
                     part_ref, dw_ref, dg_ref, da_ref):
    f32, bf16 = jnp.float32, jnp.bfloat16

    @pl.when(pl.program_id(0) == 0)
    def _():
        dw_ref[...] = jnp.zeros_like(dw_ref)
        dg_ref[...] = jnp.zeros_like(dg_ref)
        da_ref[...] = jnp.zeros_like(da_ref)

    grads = []
    for n, (g_ref, raw_ref) in enumerate(((dq_ref, rq_ref), (dk_ref, rk_ref))):
        w = turn(g_ref[...].astype(bf16).astype(f32), cos_ref[...], -sin_ref[...])
        u = raw_ref[...]
        r = lax.rsqrt(jnp.mean(u * u, axis=-1, keepdims=True) + EPSILON)
        norm = u * r
        dg_ref[n:n + 1, :] += jnp.sum(w * norm, axis=0, keepdims=True)
        m = w * qk_ref[n:n + 1]
        grads.append((r * (m - norm * jnp.mean(m * norm, axis=-1, keepdims=True))).astype(bf16))
    grads.append(dv_ref[...].astype(bf16))
    grad = jnp.concatenate(grads, axis=1)
    tok = tok_ref[...].astype(f32)
    norm = tok * lax.rsqrt(jnp.mean(tok * tok, axis=-1, keepdims=True) + EPSILON)
    hidden = (norm * gain_ref[...]).astype(bf16)
    D = tok.shape[1]
    cut = min(D, 512)
    for n in range(0, D, cut):
        part = dot(grad, w_ref[n:n + cut, :], 1, 1)
        part_ref[:, n:n + cut] = part.astype(bf16)
        da_ref[0:1, n:n + cut] += jnp.sum(part * norm[:, n:n + cut], axis=0, keepdims=True)
        dw_ref[n:n + cut, :] += dot(hidden[:, n:n + cut], grad, 0, 0)


def head_back(dq, dk, dv, rq, rk, cosine, sine, qk, tok, gain, w):
    n, D = tok.shape
    bm = 512
    row, whole = (lambda i: (i, 0)), (lambda i: (0, 0))
    head = pl.BlockSpec((bm, HD), row)
    sds = jax.ShapeDtypeStruct
    return pl.pallas_call(
        head_back_kernel,
        grid=(n // bm,),
        in_specs=[head] * 7 + [
            pl.BlockSpec((2, HD), whole), pl.BlockSpec((bm, D), row), pl.BlockSpec((1, D), whole),
            pl.BlockSpec((D, 3 * HD), whole)],
        out_specs=[
            pl.BlockSpec((bm, D), row), pl.BlockSpec((D, 3 * HD), whole), pl.BlockSpec((8, HD), whole),
            pl.BlockSpec((8, D), whole)],
        out_shape=[sds((n, D), jnp.bfloat16), sds((D, 3 * HD), jnp.float32), sds((8, HD), jnp.float32),
                   sds((8, D), jnp.float32)],
        compiler_params=pltpu.CompilerParams(vmem_limit_bytes=58 * 2**20),
    )(dq, dk, dv, rq, rk, cosine, sine, qk, tok, gain, w)


def dispatch_kernel(val_ref, gate_ref, norm_ref, cot_ref, x_ref, pg_ref, hot_ref, rg_ref, rg_s):
    f32, bf16 = jnp.float32, jnp.bfloat16
    experts, KB = val_ref.shape[1:]
    RB, D = x_ref.shape[1:]
    at = lax.broadcasted_iota(jnp.int32, (RB, KB), 0)
    for e in range(experts):
        hit = at == val_ref[0, e:e + 1, :]
        hot_ref[0, e * RB:(e + 1) * RB, :] = jnp.where(hit, 1.0, 0.0).astype(bf16)
        weight = jnp.sum(jnp.where(hit, gate_ref[0, e:e + 1, :], 0.0), axis=1, keepdims=True)
        rg_s[e * RB:(e + 1) * RB, :] = weight
        rg_ref[e] = jnp.broadcast_to(weight, (RB, rg_ref.shape[2]))
    cut = min(D, 512)
    hot = hot_ref[0]
    norm = norm_ref[...].reshape(KB, D)
    cot = cot_ref[...].reshape(KB, D)
    for n in range(0, D, cut):
        x = dot(hot, norm[:, n:n + cut], 1, 0).astype(bf16)
        x_ref[:, :, n:n + cut] = x.reshape(experts, RB, cut)
        g = (dot(hot, cot[:, n:n + cut], 1, 0) * rg_s[...]).astype(bf16)
        pg_ref[:, :, n:n + cut] = g.reshape(experts, RB, cut)


def group_spec(shape, Z):
    X, two, _, Y, T, D = shape
    return pl.BlockSpec((1, two, 1, Y, T, D), lambda g: (g // Z, 0, g % Z, 0, 0, 0))


def dispatch(val, gate, normed, cot, RB):
    G, experts, KB = val.shape
    D, Z = normed.shape[-1], normed.shape[2]
    one = pl.BlockSpec((1, experts, KB), lambda g: (g, 0, 0))
    out = pl.BlockSpec((experts, RB, D), lambda g: (0, g, 0))
    sds = jax.ShapeDtypeStruct
    return pl.pallas_call(
        dispatch_kernel,
        grid=(G,),
        in_specs=[one, one, group_spec(normed.shape, Z), group_spec(cot.shape, Z)],
        out_specs=[out, out, pl.BlockSpec((1, experts * RB, KB), lambda g: (g, 0, 0)),
                   pl.BlockSpec((experts, RB, 128), lambda g: (0, g, 0))],
        out_shape=[sds((experts, G * RB, D), jnp.bfloat16)] * 2 + [
            sds((G, experts * RB, KB), jnp.bfloat16), sds((experts, G * RB, 128), jnp.float32)],
        scratch_shapes=[pltpu.VMEM((experts * RB, 1), jnp.float32)],
        compiler_params=pltpu.CompilerParams(vmem_limit_bytes=58 * 2**20),
    )(val, gate, normed, cot)


def expert_kernel(x_ref, pg_ref, rg_ref, wg_ref, wu_ref, wd_ref, y_ref, dx_ref, dwg_ref, dwu_ref, dwd_ref):
    bf16 = jnp.bfloat16
    x, pg = x_ref[0], pg_ref[0]
    D = x.shape[1]
    gate, up = dot(x, wg_ref[0], 1, 0), dot(x, wu_ref[0], 1, 0)
    sigma = jax.nn.sigmoid(gate)
    silu = gate * sigma
    inner = (silu * up).astype(bf16)
    back = dot(pg, wd_ref[0], 1, 1)
    dgate = (back * up * sigma * (1.0 + gate * (1.0 - sigma))).astype(bf16)
    dup = (back * silu).astype(bf16)
    cut = min(D, 512)
    weight = rg_ref[0, :, 0:1]
    first = pl.program_id(1) == 0

    def gather_in(ref, ix, value):
        if pl.num_programs(1) == 1:
            ref[ix] = value
        else:
            ref[ix] = value + jnp.where(first, 0.0, ref[ix])

    for n in range(0, D, cut):
        c = slice(n, n + cut)
        y_ref[0, :, c] = (dot(inner, wd_ref[0, :, c], 1, 0) * weight).astype(bf16)
        dx_ref[0, :, c] = (dot(dgate, wg_ref[0, c, :], 1, 1) + dot(dup, wu_ref[0, c, :], 1, 1)).astype(bf16)
        gather_in(dwg_ref, (0, c, slice(None)), dot(x_ref[0, :, c], dgate, 0, 0))
        gather_in(dwu_ref, (0, c, slice(None)), dot(x_ref[0, :, c], dup, 0, 0))
        gather_in(dwd_ref, (0, slice(None), c), dot(inner, pg_ref[0, :, c], 0, 0))


def expert_layer(x, pg, rg, wg, wu, wd):
    rows = x.shape[1]
    step = 640 if rows % 640 == 0 else rows
    some = lambda a: pl.BlockSpec((1, step) + a.shape[2:], lambda e, i: (e, i, 0))
    whole = lambda a: pl.BlockSpec((1,) + a.shape[1:], lambda e, i: (e, 0, 0))
    sds = jax.ShapeDtypeStruct
    return pl.pallas_call(
        expert_kernel,
        grid=(x.shape[0], rows // step),
        in_specs=[some(a) for a in (x, pg, rg)] + [whole(a) for a in (wg, wu, wd)],
        out_specs=[some(a) for a in (x, x)] + [whole(a) for a in (wg, wu, wd)],
        out_shape=[sds(x.shape, x.dtype)] * 2 + [sds(a.shape, jnp.float32) for a in (wg, wu, wd)],
        compiler_params=pltpu.CompilerParams(vmem_limit_bytes=60 * 2**20),
    )(x, pg, rg, wg, wu, wd)


def combine_kernel(hot_ref, y_ref, dx_ref, py_ref, pdx_ref):
    hot = hot_ref[0]
    rows, KB = hot.shape
    D = y_ref.shape[2]
    cut = min(D, 512)
    for src, dst in ((y_ref, py_ref), (dx_ref, pdx_ref)):
        for n in range(0, D, cut):
            t = dot(hot, src[:, :, n:n + cut].reshape(rows, cut), 0, 0)
            dst[:, :, :, :, :, n:n + cut] = t.astype(dst.dtype).reshape(dst.shape[:-1] + (cut,))


def combine(hot, y, dx, shape):
    G, rows, KB = hot.shape
    experts, D = y.shape[0], y.shape[2]
    RB = rows // experts
    part = pl.BlockSpec((experts, RB, D), lambda g: (0, g, 0))
    out = group_spec(shape, shape[2])
    return pl.pallas_call(
        combine_kernel,
        grid=(G,),
        in_specs=[pl.BlockSpec((1, rows, KB), lambda g: (g, 0, 0)), part, part],
        out_specs=[out, out],
        out_shape=[jax.ShapeDtypeStruct(shape, jnp.bfloat16)] * 2,
        compiler_params=pltpu.CompilerParams(vmem_limit_bytes=58 * 2**20),
    )(hot, y, dx)


def body(tokens, w_query, w_key, w_value, w_out, attn_gain, ffn_gain, qk_gain,
         expert_gate, expert_up, expert_down, routes, gates, order, cotangent):
    f32, bf16 = jnp.float32, jnp.bfloat16
    positions, seqs, D = tokens.shape
    U, B = lax.axis_size("ulysses"), lax.axis_size("blk")
    F = U * B
    u, b = lax.axis_index("ulysses"), lax.axis_index("blk")
    H = w_query.shape[1] // HD
    W = w_query.shape[0]
    L = F * positions
    T = seqs * positions
    top_count = routes.shape[-1]
    local_experts = expert_gate.shape[0]
    E = local_experts * B
    chips = F // 2
    R = chips // H
    first_copy = lax.rem((u // 2) * B + b, R) == 0

    tok = tokens.transpose(1, 0, 2)
    cot = cotangent.transpose(1, 0, 2)
    rows_f = tok.reshape(T, D).astype(f32)

    expert_of = routes.transpose(1, 0, 2).reshape(-1)
    prio = order.reshape(positions, seqs, top_count).transpose(1, 0, 2).reshape(-1)
    same = expert_of[:, None] == expert_of[None, :]
    ranks = jnp.sum((same & (prio[None, :] < prio[:, None])).astype(jnp.int32), axis=1)
    slot = jnp.where(ranks < CAP, expert_of * CAP + ranks, -1).astype(f32)
    pairs = slot.shape[0]

    nq = qk_gain.shape[1]
    small = jnp.concatenate(
        [slot, gates.transpose(1, 0, 2).reshape(-1)]
        + [g.astype(f32) for g in (attn_gain, ffn_gain, qk_gain[0], qk_gain[1])])
    small = jnp.pad(small, (0, -small.shape[0] % 1024)).reshape(-1, 128)
    heads_w = jnp.stack([w_query, w_key, w_value]).reshape(3, W, H, HD).transpose(2, 1, 0, 3).reshape(H, W, 3 * HD)
    if R > 1:
        heads_w = heads_w[np.arange(chips) // R]
    seq_tok, table, head_w = front(tok, small, heads_w, U, B, 1)
    seq_tok, head_w = seq_tok.reshape(L, D), head_w.reshape(D, 3 * HD)
    out_w = lax.all_gather(w_out, AXES, axis=0, tiled=True)
    cot_all = lax.all_gather(cot, AXES, axis=0)
    table = table.reshape(F, -1)
    cut = 2 * pairs
    attn_g = table[:, cut:cut + W].reshape(1, D)
    ffn_g = table[:, cut + W:cut + 2 * W].reshape(1, D)
    cut = cut + 2 * W
    qk_g = jnp.stack([table[:, cut:cut + nq].reshape(-1), table[:, cut + nq:cut + 2 * nq].reshape(-1)])

    groups = (U // 2, 2, B // 2, 2)
    GB = 4
    G, KB = F // GB, GB * T
    RB = -(-GB * CAP // 16) * 16
    slot_all = table[:, :pairs].astype(jnp.int32).reshape(F, T, top_count)
    gate_all = table[:, pairs:2 * pairs].reshape(F, T, top_count)
    place = ((np.arange(F) // B % 2) * 2 + np.arange(F) % 2).astype(np.int32)
    base = (b * local_experts + jnp.arange(local_experts, dtype=jnp.int32)) * CAP
    off = slot_all[:, :, :, None] - base
    mine = (off >= 0) & (off < CAP)
    val = jnp.sum(jnp.where(mine, off + 1, 0), axis=2)
    val = jnp.where(val > 0, val - 1 + jnp.asarray(place)[:, None, None] * CAP, -1)
    gate_of = jnp.sum(jnp.where(mine, gate_all[:, :, :, None], 0.0), axis=2)

    def by_group(m):
        return m.reshape(groups + (T, local_experts)).transpose(0, 2, 5, 1, 3, 4).reshape(G, local_experts, KB)

    val, gate_of = by_group(val), by_group(gate_of)

    half = HD // 2
    inverse = ROPE_BASE ** (-2.0 * jnp.arange(half).astype(f32) / HD)
    angles = jnp.arange(L).astype(f32)[:, None] * inverse[None, :]
    cosine = jnp.concatenate([jnp.cos(angles)] * 2, axis=1)
    sine = jnp.concatenate([-jnp.sin(angles), jnp.sin(angles)], axis=1)
    q, k, v, kt, vt, raw_q, raw_k = project(seq_tok, attn_g, head_w, qk_g, cosine, sine)
    att, lse = attend(q, k, vt)
    att_rows = exchange(att.reshape(F, positions, HD), U, B, 6)

    def from_heads(m):
        m = m.reshape(U // 2, 2, B, positions, HD).transpose(1, 3, 0, 2, 4)
        return m.reshape(2, positions, H, R, HD)[:, :, :, 0].reshape(T, H * HD)

    attended = from_heads(att_rows)
    residual = rows_f + jnp.dot(attended, out_w, preferred_element_type=f32)
    normed_full, ffn_back = jax.vjp(rms_norm, residual, ffn_g)
    normed = normed_full.astype(bf16).reshape(2, positions, D)

    normed_all = gather_blocks(normed, U, B, False, 2)
    shape = groups + (T, D)
    x, pair_grad, hot, row_gate = dispatch(val, gate_of, normed_all.reshape(shape), cot_all.reshape(shape), RB)
    y, dx, gate_grad, up_grad, down_grad = expert_layer(x, pair_grad, row_gate, expert_gate, expert_up, expert_down)
    mixed_part, normed_part = combine(hot, y, dx, shape)
    blocks = (F, 2, positions, D)
    mixed_sum, normed_grad = scatter_pair(mixed_part.reshape(blocks), normed_part.reshape(blocks), U, B, 3)
    mixed = (residual + mixed_sum.reshape(T, D)).reshape(2, positions, D).transpose(1, 0, 2).astype(bf16)
    normed_grad = normed_grad.reshape(T, D)

    residual_norm_grad, ffn_gain_part = ffn_back(normed_grad)
    residual_grad = cot.reshape(T, D).astype(f32) + residual_norm_grad
    attn_out_grad = residual_grad.astype(bf16)
    att_grad = dot(attn_out_grad, out_w, 1, 1).astype(bf16)
    att_grad = jnp.repeat(att_grad.reshape(2, positions, H, HD).transpose(2, 0, 1, 3), R, axis=0)
    att_grad = att_grad.reshape(U // 2, B, 2, positions, HD).transpose(0, 2, 1, 3, 4).reshape(F, positions, HD)
    do = exchange(att_grad, U, B, 6).reshape(L, HD)
    out_part = dot(attended, attn_out_grad, 0, 0).astype(bf16)
    out_part = out_part.reshape(F, 2, W // 2, D)
    dq, dk, dv = attend_back(q, do, lse, k, kt, v)
    if R > 1:
        dq, dk, dv = (jnp.where(first_copy, m, 0.0) for m in (dq, dk, dv))
    hidden_part, weight_part, qk_part, attn_gain_part = head_back(
        dq, dk, dv, raw_q, raw_k, cosine, sine, qk_g, seq_tok, attn_g, head_w)
    weight_part = weight_part.astype(bf16).reshape(F, W, 3 * HD)
    small = jnp.concatenate(
        [attn_gain_part[0].reshape(F, W), ffn_gain_part.reshape(F, W),
         qk_part[0].reshape(F, nq), qk_part[1].reshape(F, nq)], axis=1)
    small = jnp.pad(small, ((0, 0), (0, -small.shape[1] % 1024))).reshape(F, -1, 128)
    weight_grad, small, hidden_grad, out_grad = finish(
        weight_part, small, hidden_part.reshape(F, positions, D), out_part, U, B, 4)
    small = jnp.sum(small, axis=0).reshape(-1)
    weight_grad = weight_grad.reshape(H, R, W, 3 * HD).astype(f32).sum(axis=1)
    weight_grad = weight_grad.transpose(1, 0, 2).reshape(W, H, 3, HD)
    query_grad, key_grad, value_grad = (weight_grad[:, :, n].reshape(W, H * HD) for n in range(3))
    hidden_grad, out_grad = hidden_grad.reshape(T, D), out_grad.reshape(W, D)
    inv = lax.rsqrt(jnp.mean(rows_f * rows_f, axis=-1, keepdims=True) + EPSILON)
    norm = rows_f * inv
    m = hidden_grad * attn_g
    token_grad = inv * (m - norm * jnp.mean(m * norm, axis=-1, keepdims=True))
    input_grad = (residual_grad + token_grad).reshape(2, positions, D).transpose(1, 0, 2)
    return (
        mixed, input_grad, query_grad, key_grad, value_grad, out_grad,
        small[:W], small[W:2 * W], small[2 * W:2 * W + 2 * nq].reshape(2, nq),
        gate_grad, up_grad, down_grad,
    )


def solution(mesh):
    rows = P(AXES, None, None)
    flat = P(AXES, None)
    by_expert = (P("blk", None, "ulysses"), P("blk", None, "ulysses"), P("blk", "ulysses", None))
    in_specs = (rows, flat, flat, flat, flat, P(AXES), P(AXES), P(None, AXES)) + by_expert + (rows, rows, flat, rows)
    out_specs = (rows, rows, flat, flat, flat, flat, P(AXES), P(AXES), P(None, AXES)) + by_expert
    return jax.shard_map(body, mesh=mesh, in_specs=in_specs, out_specs=out_specs, check_vma=False)
```

time: 1360 us -> 859 us (0.63)
  matrix products: 302 us -> 13.3 us
  Pallas kernels: 622 us -> 762 us
  blocking collectives: 138 us -> 0 us
  local copies, waits for them, and re-layouts: 159 us -> 38.3 us
  other arithmetic: 82.8 us -> 25.6 us
  starting transfers between devices: 24 us -> 0.08 us
    pallas_call x4 -> x10, Pallas kernels: 324 us -> 635 us  [the longest x1 156 us: call(): pl.pallas_call(functools.partial(pair_kernel, U, B, 2), out_shape=[jax.Sh...]
    dot_general x14 -> x0, matrix products: 267 us -> none  [the longest x2 55.9 us: combine(): jnp.einsum('gert,egrd->gtd', onehot, m, preferred_element_type=f32)]
    pallas_call x3 -> x1, Pallas kernels: 268 us -> 96.5 us  [gather_blocks(): pl.pallas_call(functools.partial(gather_kernel, U, B, by_seq), out_shape=...]
    all_gather x1 -> x0, blocking collectives: 101 us -> none  [body(): table = lax.all_gather(jnp.stack([slot, gate_flat]), AXES, axis=0)]
    convert_element_type x8 -> x3, other arithmetic: 44.8 us -> 3.21 us  [the longest x1 3.2 us: body(): weight_part = weight_part.astype(bf16).reshape(F, W, 3 * HD)]
    unnamed x1 -> x0, blocking collectives: 37 us -> none
    transpose x4 -> x5, local copies, waits for them, and re-layouts: 30.4 us -> 3.12 us  [the longest x2 1.33 us: by_group(): m.reshape(groups + (T, local_experts)).transpose(0, 2, 5, 1, 3, 4)]
    all_to_all x5 -> x0, starting transfers between devices: 23.9 us -> none  [to_all(): return lax.all_to_all(v, AXES, split_axis=0, concat_axis=0, tiled=True)]
  transfers between devices with their start and end apart: 6 -> 2, of which waited for: 1 -> 0; matrix products, arithmetic and copies ran while one was open for 17% -> 4% of each run, Pallas kernels for 18% -> 32%
where the time goes in v2:
time: 859 us; the launch traced here: 855 us
  Pallas kernels  762 us (89%)
  local copies, waits for them, and re-layouts  38.3 us (4%)
  other arithmetic  25.6 us (3%)
  between operations  14.8 us (2%)
  matrix products  13.3 us (2%)
    pallas_call x1, Pallas kernels, call(): pl.pallas_call(functools.partial(pair_kernel, U, B, 2), out_shape=[jax.Sh...  156 us
    pallas_call x1, Pallas kernels, call(): pl.pallas_call(functools.partial(finish_kernel, U, B, o is not None), out...  133 us
    pallas_call x1, Pallas kernels, front(): pl.pallas_call(functools.partial(front_kernel, U, B), out_shape=[jax.Shap...  125 us
    pallas_call x1, Pallas kernels, gather_blocks(): pl.pallas_call(functools.partial(gather_kernel, U, B, by_seq), out_shape=...  96.5 us
    pallas_call x1, Pallas kernels, expert_layer(): pl.pallas_call(expert_kernel, grid=(x.shape[0], rows // step), in_specs=[...  70.6 us
    pallas_call x2, Pallas kernels, exchange(): pl.pallas_call(functools.partial(exchange_kernel, U, B), out_shape=jax.Sh...  44.7 us
    pallas_call x1, Pallas kernels, dispatch(): pl.pallas_call(dispatch_kernel, grid=(G,), in_specs=[one, one, group_spec...  36.6 us
    pallas_call x1, Pallas kernels, combine(): pl.pallas_call(combine_kernel, grid=(G,), in_specs=[pl.BlockSpec((1, rows...  35.2 us
  transfers between devices with their start and end apart: 2, of which 0 were waited for; matrix products, arithmetic and copies ran while one was open for 4% of the time, Pallas kernels for 32%

profile of v2, /device:TPU:0, one launch (start us, length us, event | category | flops | bytes accessed | tf_op | source)
XLA Modules:
  0.0 854.6 jit_solution(4343602964405097645)
XLA Ops:
  8.0 2.0 copy.137
  10.6 1.3 reduce.29
  13.9 1.0 copy.103
  15.4 1.0 copy.104
  17.0 1.0 copy.105
  18.5 1.8 maximum_bitcast_fusion
  20.3 1.6 reshape.237.weights
  21.9 1.0 convert_reduce_fusion
  23.7 1.0 copy_bitcast_fusion.6
  24.7 125.3 %shard_map.247 = (bf16[32,64,2048]{2,1,0:T(8,128)(2,1)}, f32[32,24,128]{2,1,0:T(8,128)}, bf16[32,64,384]{2,1,0:T(8,128)(2,1)}) custom-call(bf16[2,64,2048]{2,1,0:T(8,128)(2,1)} %get-tuple-element.95.tok, f32[24,128]{1,0:T(8,128)} %pad_bitcast_fusion.small, bf16[16,64,384]{2,1,0:T(8,128)(2,1)} %reshape.237.weights), custom_call_target="tpu_custom_call" | custom-call | tf_op jit(solution)/shard_map/pallas_call | solution.py:342
  150.0 1.1 copy.136
  156.2 3.7 fusion.11
  159.9 2.0 pad_maximum_fusion
  161.9 13.1 %shard_map.248 = (bf16[2048,128]{1,0:T(8,128)(2,1)}, bf16[2048,128]{1,0:T(8,128)(2,1)}, bf16[2048,128]{1,0:T(8,128)(2,1)}, bf16[128,2048]{1,0:T(8,128)(2,1)}, bf...) custom-call(bf16[2048,2048]{1,0:T(8,128)(2,1)} %bitcast.147, f32[1,2048]{1,0:T(1,128)} %reshape.240.gain_ref, ...), custom_call_target="tpu_custom_call" | custom-call | tf_op jit(solution)/shard_map/pallas_call | solution.py:907
  175.0 12.6 %shard_map.249 = (bf16[2048,128]{1,0:T(8,128)(2,1)}, f32[1,2048]{1,0:T(1,128)}) custom-call(bf16[2048,128]{1,0:T(8,128)(2,1)} %get-tuple-element.51.q_ref, bf16[2048,128]{1,0:T(8,128)(2,1)} %get-tuple-element.52.k_ref, bf16[128,2048]{1,0:T(8,128)(2,1)} %get-tuple-element.53.vt_ref), custom_call_target="tpu_custom_call" | custom-call | tf_op jit(solution)/shard_map/pallas_call | solution.py:829
  187.6 27.6 %shard_map.250 = bf16[32,64,128]{2,1,0:T(8,128)(2,1)} custom-call(bf16[32,64,128]{2,1,0:T(8,128)(2,1)} %bitcast.186), custom_call_target="tpu_custom_call" | custom-call | tf_op jit(solution)/shard_map/pallas_call | solution.py:380
  215.3 1.4 copy.135
  216.9 4.8 multiply_reduce_fusion.3
  221.7 1.0 multiply_convert_fusion
  222.7 96.5 %shard_map.251 = bf16[32,2,64,2048]{3,2,1,0:T(8,128)(2,1)} custom-call(bf16[2,64,2048]{2,1,0:T(8,128)(2,1)} %bitcast.162), custom_call_target="tpu_custom_call" | custom-call | tf_op jit(solution)/shard_map/pallas_call | solution.py:310
  319.2 36.6 %shard_map.252 = (bf16[8,640,2048]{2,1,0:T(8,128)(2,1)}, bf16[8,640,2048]{2,1,0:T(8,128)(2,1)}, bf16[8,640,512]{2,1,0:T(8,128)(2,1)}, f32[8,640,128]{2,1,0:T(8,128)}) custom-call(s32[8,8,512]{2,1,0:T(8,128)} %bitcast.178, f32[8,8,512]{2,1,0:T(8,128)} %bitcast.177, bf16[2,2,4,2,128,2048]{5,4,3,2,1,0:T(8,128)(2,1)} %bitcast.143, ...), custom_call_target="tpu_custom_call" | custom-call | tf_op jit(solution)/shard_map/pallas_call | solution.py:1007
  355.8 70.6 %shard_map.253 = (bf16[8,640,2048]{2,1,0:T(8,128)(2,1)}, bf16[8,640,2048]{2,1,0:T(8,128)(2,1)}, f32[8,2048,256]{2,1,0:T(8,128)}, f32[8,2048,256]{2,1,0:T(8,128)}, f32[8,256,2048]{2,1,0:T(8,128)}) custom-call(bf16[8,640,2048]{2,1,0:T(8,128)(2,1)} %get-tuple-element.56.x_ref, bf16[8,640,2048]{2,1,0:T(8,128)(2,1)} %get-tuple-element.57.pg_ref, ...), custom_call_target="tpu_custom_call" | custom-call | tf_op jit(solution)/shard_map/pallas_call | solution.py:1056
  426.4 35.2 %shard_map.254 = (bf16[2,2,4,2,128,2048]{5,4,3,2,1,0:T(8,128)(2,1)}, bf16[2,2,4,2,128,2048]{5,4,3,2,1,0:T(8,128)(2,1)}) custom-call(bf16[8,640,512]{2,1,0:T(8,128)(2,1)} %get-tuple-element.55.hot_ref, bf16[8,640,2048]{2,1,0:T(8,128)(2,1)} %get-tuple-element.59.y_ref, bf16[8,640,2048]{2,1,0:T(8,128)(2,1)} %get-tuple-element.60.dx_ref), custom_call_target="tpu_custom_call" | custom-call | tf_op jit(solution)/shard_map/pallas_call | solution.py:1083
  461.6 156.4 %shard_map.255 = (f32[2,64,2048]{2,1,0:T(8,128)}, f32[2,64,2048]{2,1,0:T(8,128)}) custom-call(bf16[32,2,64,2048]{3,2,1,0:T(8,128)(2,1)} %bitcast.150, bf16[32,2,64,2048]{3,2,1,0:T(8,128)(2,1)} %bitcast.151), custom_call_target="tpu_custom_call" | custom-call | tf_op jit(solution)/shard_map/pallas_call | solution.py:627
  617.9 1.5 fusion.7
  619.4 1.9 fusion.1
  621.3 1.3 copy.134
  622.7 5.6 convolution_convert_fusion
  628.3 2.9 fusion
  631.3 1.0 copy.97
  632.3 17.1 %shard_map.256 = bf16[32,64,128]{2,1,0:T(8,128)(2,1)} custom-call(bf16[32,64,128]{2,1,0:T(8,128)(2,1)} %bitcast.166), custom_call_target="tpu_custom_call" | custom-call | tf_op jit(solution)/shard_map/pallas_call | solution.py:380
  649.4 17.6 %shard_map.257 = (f32[2048,128]{1,0:T(8,128)}, f32[2048,128]{1,0:T(8,128)}, f32[2048,128]{1,0:T(8,128)}) custom-call(bf16[2048,128]{1,0:T(8,128)(2,1)} %get-tuple-element.51.q_ref, bf16[2048,128]{1,0:T(8,128)(2,1)} %bitcast.159, f32[1,2048]{1,0:T(1,128)} %get-tuple-element.65.lse_ref, bf16[2048,128]{1,0:T(8,128)(2,1)} %get-tuple-element.52.k_ref, ...), custom_call_target="tpu_custom_call" | custom-call | tf_op jit(solution)/shard_map/pallas_call | solution.py:864
  667.1 20.5 %shard_map.258 = (bf16[2048,2048]{1,0:T(8,128)(2,1)}, f32[2048,384]{1,0:T(8,128)}, f32[8,128]{1,0:T(8,128)}, f32[8,2048]{1,0:T(8,128)}) custom-call(f32[2048,128]{1,0:T(8,128)} %get-tuple-element.68.dq_ref, f32[2048,128]{1,0:T(8,128)} %get-tuple-element.69.dk_ref, f32[2048,128]{1,0:T(8,128)} %get-tuple-element.70.dv_ref, ...), custom_call_target="tpu_custom_call" | custom-call | tf_op jit(solution)/shard_map/pallas_call | solution.py:959
  687.6 3.2 convert_element_type.121
  691.5 0.9 slice_reduce_fusion.3
  693.5 132.8 %shard_map.259 = (bf16[16,64,384]{2,1,0:T(8,128)(2,1)}, f32[16,8,128]{2,1,0:T(8,128)}, f32[2,64,2048]{2,1,0:T(8,128)}, f32[2,32,2048]{2,1,0:T(8,128)}) custom-call(bf16[2,2,8,64,384]{4,3,2,1,0:T(8,128)(2,1)} %bitcast.153, f32[2,2,8,8,128]{4,3,2,1,0:T(8,128)} %bitcast.179, bf16[32,64,2048]{2,1,0:T(8,128)(2,1)} %bitcast.152, bf16[32,2,32,2048]{3,2,1,0:T(8,128)(2,1)} %bitcast.146), custom_call_target="tpu_custom_call" | custom-call | tf_op jit(solution)/shard_map/pallas_call | solution.py:758
  826.3 1.7 multiply_reduce_fusion
  828.0 1.7 fusion.6
  829.7 1.8 copy.130
  831.5 0.9 reduce_sum.97
  833.6 1.3 convert_bitcast_fusion
  834.9 2.1 copy.99
  837.0 2.7 reshape.271
  839.7 4.1 slice_reduce_fusion
  843.9 1.0 copy.131
  844.8 1.0 copy.132
  845.8 1.0 copy.133
  846.7 0.8 copy.139
  (84 shorter events, 14.3 us)
Async XLA Ops:
  7.2 15.8 %copy-start.4 = (bf16[2,4]{1,0:T(2,128)(2,1)S(1)}, bf16[2,4]{1,0:T(2,128)(2,1)}, u32[]{:S(2)}) copy-start(bf16[2,4]{1,0:T(2,128)(2,1)} %param.23) | copy-start | bytes 52
  7.2 15.8 %copy-start.6 = (bf16[64]{0:T(256)(128)(2,1)S(1)}, bf16[64]{0:T(256)(128)(2,1)}, u32[]{:S(2)}) copy-start(bf16[64]{0:T(256)(128)(2,1)} %param.22) | copy-start | bytes 388
  7.2 15.8 %copy-start.5 = (bf16[64]{0:T(256)(128)(2,1)S(1)}, bf16[64]{0:T(256)(128)(2,1)}, u32[]{:S(2)}) copy-start(bf16[64]{0:T(256)(128)(2,1)} %param.21) | copy-start | bytes 388
  7.2 16.5 %copy-start = (bf16[64,2,2048]{2,1,0:T(2,128)(2,1)S(1)}, bf16[64,2,2048]{2,1,0:T(2,128)(2,1)}, u32[]{:S(2)}) copy-start(bf16[64,2,2048]{2,1,0:T(2,128)(2,1)} %param.16) | copy-start | bytes 1572868
  7.2 209.7 %all-gather.4.cloned.1.call-start = ((), (), s32[]{:S(2)}) async-start(), calls=%async_computation | async-start | bytes 8650752 | tf_op jit(solution)/shard_map/all_gather | solution.py:1132
  8.0 311.3 %all-gather.6.cloned.1.call-start = ((), (), s32[]{:S(2)}) async-start(), calls=%async_computation.1 | async-start | bytes 17301504 | tf_op jit(solution)/shard_map/all_gather | solution.py:1133
  17.0 137.9 %copy-start.3 = (s32[2,2,4,2]{3,2,1,0:T(4,128)S(1)}, s32[2,2,4,2]{3,2,1,0:T(4,128)}, u32[]{:S(2)}) copy-start(s32[2,2,4,2]{3,2,1,0:T(4,128)} %constant.51) | copy-start | bytes 388
  461.6 157.8 %copy-start.1 = (bf16[64,2,2048]{2,0,1:T(8,128)(2,1)S(1)}, bf16[64,2,2048]{2,0,1:T(8,128)(2,1)}, u32[]{:S(2)}) copy-start(bf16[64,2,2048]{2,0,1:T(8,128)(2,1)} %copy.137) | copy-start | bytes 1572868
  621.3 6.9 slice-start
  622.7 5.6 slice-start.1
  829.7 17.0 %copy-start.2 = (f32[2,32,2048]{2,1,0:T(8,128)S(1)}, f32[2,32,2048]{2,1,0:T(8,128)}, u32[]{:S(2)}) copy-start(f32[2,32,2048]{2,1,0:T(8,128)} %get-tuple-element.79) | copy-start | bytes 1572868
Sparse Core Ops, SparseCore 0:
  11.0 114.1 all-gather.3
  128.3 124.3 all-gather.5

commit v3 on v2

--- a/solution.py
+++ b/solution.py
@@ -26,9 +26,10 @@
         u, b = lax.axis_index("ulysses"), lax.axis_index("blk")
         self.c, self.x = lax.rem(u, 2), lax.div(u, 2)
         self.y, self.z = lax.rem(b, self.Y), lax.div(b, self.Y)
-        self.q = self.x * B + b
-        self.me, self.sib = self.at(self.q, self.c), self.at(self.q, 1 - self.c)
+        self.r = self.c * B + b
+        self.me = u * B + b
         self.core_peer = self.dev(self.x, self.y, self.z, 1 - self.c)
+        self.x_peer = self.dev(1 - self.x, self.y, self.z, self.c)
 
     def dev(self, x, y, z, c):
         return (x * 2 + c, z * self.Y + y)
@@ -39,11 +40,11 @@
     def chip(self, x, y, z):
         return x * self.B + z * self.Y + y
 
-    def at(self, q, c):
-        return (lax.div(q, self.B) * 2 + c) * self.B + lax.rem(q, self.B)
-
-    def chip_dev(self, q):
-        return (lax.div(q, self.B) * 2 + self.c, lax.rem(q, self.B))
+    def at(self, r, x):
+        return x * 2 * self.B + r
+
+    def plane_dev(self, r):
+        return (self.x * 2 + lax.div(r, self.B), lax.rem(r, self.B))
 
     def flat_dev(self, f):
         return (lax.div(f, self.B), lax.rem(f, self.B))
@@ -66,14 +67,16 @@
 
             pl.semaphore_wait(sem, self.F - 1)
             return
+        if reach == "plane":
+            greet(self.x_peer)
+
+            @pl.loop(1, 2 * self.B)
+            def _(o):
+                greet(self.plane_dev(lax.rem(self.r + o, 2 * self.B)))
+
+            pl.semaphore_wait(sem, 2 * self.B)
+            return
         greet(self.core_peer)
-        if reach == "all":
-            @pl.loop(1, self.Q)
-            def _(o):
-                greet(self.chip_dev(lax.rem(self.q + o, self.Q)))
-
-            pl.semaphore_wait(sem, self.Q)
-            return
         for k in self.others("x"):
             greet(self.dev(k, self.y, self.z, self.c))
         for k in self.others("y"):
@@ -104,25 +107,20 @@
 
 
 class Gather:
-    def __init__(self, p, by_seq, src, out, send_sem, recv_sem, local_sem):
-        self.p, self.by_seq, self.src, self.out = p, by_seq, src, out
+    def __init__(self, p, src, out, send_sem, recv_sem, local_sem):
+        self.p, self.src, self.out = p, src, out
         self.send_sem, self.recv_sem, self.local_sem = send_sem, recv_sem, local_sem
         self.steps = p.Z + 2
         self.started = []
         self.always = p.z >= 0
 
     @staticmethod
-    def semaphores(U, B, by_seq):
-        n = 1 if by_seq else 2
+    def semaphores(U, B):
         dma = pltpu.SemaphoreType.DMA
-        return [dma((4 + U // 2 - 1 + 1, n, U * B)), dma((n, U * B)), dma((1,))]
+        return [dma((4 + U // 2, 2, U * B)), dma((2, U * B)), dma((1,))]
 
     def where(self, half, x, y, z):
-        p = self.p
-        if self.by_seq:
-            f = p.block(x, y, z, half)
-            return self.out.at[f], (0, f)
-        f = p.block(x, y, z, p.c)
+        f = self.p.block(x, y, z, self.p.c)
         return self.out.at[f, half], (half, f)
 
     def send(self, cond, src_ref, dst_ref, ix, way, dev):
@@ -142,8 +140,7 @@
         ref, ix = self.where(half, x, y, z)
         for ax in axes:
             if ax == "core":
-                if not self.by_seq:
-                    self.send(cond, ref, ref, ix, 0, p.core_peer)
+                self.send(cond, ref, ref, ix, 0, p.core_peer)
             elif ax == "up":
                 self.send(cond & (p.z < p.Z - 1), ref, ref, ix, 1, p.dev(p.x, p.y, p.z + 1, p.c))
             elif ax == "down":
@@ -173,16 +170,9 @@
     def step(self, n):
         p = self.p
         if n == 0:
-            if self.by_seq:
-                cp = pltpu.make_async_copy(self.src.at[p.c], self.out.at[p.me], self.local_sem.at[0])
-                cp.start()
-                self.send(self.always, self.src.at[1 - p.c], self.out.at[p.me], (0, p.me), 0, p.core_peer)
-                cp.wait()
-                self.wait(self.out.at[p.sib], (0, p.sib))
-            else:
-                cp = pltpu.make_async_copy(self.src, self.out.at[p.me], self.local_sem.at[0])
-                cp.start()
-                cp.wait()
+            cp = pltpu.make_async_copy(self.src, self.out.at[p.me], self.local_sem.at[0])
+            cp.start()
+            cp.wait()
             for half in (0, 1):
                 self.along(self.always, half, p.x, p.y, p.z, ("up", "down", "y", "x"))
             for half in (0, 1):
@@ -209,30 +199,66 @@
                         self.arrive(cond, 0, j, i, k, ("core",))
                         self.arrive(cond, 1, j, i, k, ("core",))
 
-    def from_core(self, cond, x, y, z):
-        f = self.p.block(x, y, z, 1 - self.p.c)
-
-        @pl.when(cond)
-        def _():
-            for half in (0, 1):
-                self.wait(self.out.at[f, half], (half, f))
-
     def end(self):
         p = self.p
-        if not self.by_seq:
-            for k in range(p.Z):
-                for j in range(p.X):
-                    for i in range(p.Y):
-                        self.from_core(self.always, j, i, k)
-        self.sent()
-
-    def sent(self):
+        for k in range(p.Z):
+            for j in range(p.X):
+                for i in range(p.Y):
+                    f = p.block(j, i, k, 1 - p.c)
+                    for half in (0, 1):
+                        self.wait(self.out.at[f, half], (half, f))
         for cond, cp in self.started:
             @pl.when(cond)
             def _(cp=cp):
                 cp.wait_send()
 
 
+class PlaneGather(Gather):
+    def __init__(self, *a):
+        super().__init__(*a)
+        self.steps = self.p.Z + 1
+
+    @staticmethod
+    def semaphores(U, B):
+        dma = pltpu.SemaphoreType.DMA
+        return [dma((5, 1, U * B)), dma((1, U * B)), dma((1,))]
+
+    def where(self, half, x, y, z):
+        f = self.p.block(half, y, z, self.p.c)
+        return self.out.at[f], (0, f)
+
+    def step(self, n):
+        p = self.p
+        if n == 0:
+            cp = pltpu.make_async_copy(self.src.at[p.x], self.out.at[p.me], self.local_sem.at[0])
+            cp.start()
+            self.send(self.always, self.src.at[1 - p.x], self.out.at[p.me], (0, p.me), 4, p.x_peer)
+            cp.wait()
+            self.along(self.always, p.x, p.x, p.y, p.z, ("up", "down", "y", "core"))
+            self.arrive(self.always, 1 - p.x, p.x, p.y, p.z, ("up", "down", "y", "core"))
+            return
+        if n < p.Z:
+            for half in (0, 1):
+                for cond, k, on in self.zs(n):
+                    self.arrive(cond, half, p.x, p.y, k, on + ("y", "core"))
+        for half in (0, 1):
+            for cond, k, _ in self.zs(n - 1):
+                for i in p.others("y"):
+                    self.arrive(cond, half, p.x, i, k, ("core",))
+
+    def end(self):
+        p = self.p
+        for k in range(p.Z):
+            for i in range(p.Y):
+                for half in (0, 1):
+                    f = p.block(half, i, k, 1 - p.c)
+                    self.wait(self.out.at[f], (0, f))
+        for cond, cp in self.started:
+            @pl.when(cond)
+            def _(cp=cp):
+                cp.wait_send()
+
+
 class Spread:
     def __init__(self, p, same, src, out, send_sem, recv_sem):
         self.p, self.same, self.src, self.out = p, same, src, out
@@ -241,53 +267,53 @@
     @staticmethod
     def semaphores(U, B):
         dma = pltpu.SemaphoreType.DMA
-        return [dma((2, U * B // 2)), dma((U * B,))]
-
-    def part(self, q):
-        return self.src if self.same else self.src.at[q]
+        return [dma((2, 2 * B)), dma((U * B,))]
+
+    def part(self, r):
+        return self.src if self.same else self.src.at[r]
 
     def out_to(self, o):
         p = self.p
-        q = lax.rem(p.q + o, p.Q)
-        return remote(self.part(q), self.out.at[p.me], self.send_sem.at[0, q], self.recv_sem.at[p.me], p.chip_dev(q))
-
-    def across(self, q):
-        f = self.p.at(q, self.p.c)
-        return remote(self.out.at[f], self.out.at[f], self.send_sem.at[1, q], self.recv_sem.at[f], self.p.core_peer)
+        r = lax.rem(p.r + o, 2 * p.B)
+        return remote(self.part(r), self.out.at[p.me], self.send_sem.at[0, r], self.recv_sem.at[p.me], p.plane_dev(r))
+
+    def across(self, r):
+        f = self.p.at(r, self.p.x)
+        return remote(self.out.at[f], self.out.at[f], self.send_sem.at[1, r], self.recv_sem.at[f], self.p.x_peer)
 
     def arrive(self, f):
-        remote(self.out.at[f], self.out.at[f], self.send_sem.at[0, 0], self.recv_sem.at[f], self.p.core_peer).wait_recv()
+        remote(self.out.at[f], self.out.at[f], self.send_sem.at[0, 0], self.recv_sem.at[f], self.p.x_peer).wait_recv()
 
     def begin(self):
         p = self.p
 
-        @pl.loop(1, p.Q)
+        @pl.loop(1, 2 * p.B)
         def _(o):
             self.out_to(o).start()
 
-        cp = pltpu.make_async_copy(self.part(p.q), self.out.at[p.me], self.send_sem.at[0, p.q])
+        cp = pltpu.make_async_copy(self.part(p.r), self.out.at[p.me], self.send_sem.at[0, p.r])
         cp.start()
         cp.wait()
-        self.across(p.q).start()
+        self.across(p.r).start()
 
     def middle(self):
         p = self.p
 
-        @pl.loop(1, p.Q)
+        @pl.loop(1, 2 * p.B)
         def _(o):
-            q = lax.rem(p.q + o, p.Q)
-            self.arrive(p.at(q, p.c))
-            self.across(q).start()
+            r = lax.rem(p.r + o, 2 * p.B)
+            self.arrive(p.at(r, p.x))
+            self.across(r).start()
 
     def end(self):
         p = self.p
 
-        @pl.loop(0, p.Q)
-        def _(q):
-            self.arrive(p.at(q, 1 - p.c))
-            self.across(q).wait_send()
-
-        @pl.loop(1, p.Q)
+        @pl.loop(0, 2 * p.B)
+        def _(r):
+            self.arrive(p.at(r, 1 - p.x))
+            self.across(r).wait_send()
+
+        @pl.loop(1, 2 * p.B)
         def _(o):
             self.out_to(o).wait_send()
 
@@ -296,31 +322,30 @@
     return [pl.BlockSpec(memory_space=pl.ANY)] * n
 
 
-def gather_kernel(U, B, by_seq, src, out, *sems):
+def gather_kernel(U, B, src, out, *sems):
     p = Place(U, B)
     p.barrier("chain")
-    g = Gather(p, by_seq, src, out, *sems)
+    g = Gather(p, src, out, *sems)
     for n in range(g.steps):
         g.step(n)
     g.end()
 
 
-def gather_blocks(v, U, B, by_seq, cid):
-    shape = (U * B,) + (v.shape[1:] if by_seq else v.shape)
+def gather_blocks(v, U, B, cid):
     return pl.pallas_call(
-        functools.partial(gather_kernel, U, B, by_seq),
-        out_shape=jax.ShapeDtypeStruct(shape, v.dtype),
+        functools.partial(gather_kernel, U, B),
+        out_shape=jax.ShapeDtypeStruct((U * B,) + v.shape, v.dtype),
         in_specs=any_specs(1),
         out_specs=any_specs(1)[0],
-        scratch_shapes=Gather.semaphores(U, B, by_seq),
+        scratch_shapes=Gather.semaphores(U, B),
         compiler_params=pltpu.CompilerParams(collective_id=cid, has_side_effects=True),
     )(v)
 
 
 def front_kernel(U, B, tok, small, weights, tok_out, small_out, weights_out, *sems):
     p = Place(U, B)
-    p.barrier("all")
-    g = Gather(p, True, tok, tok_out, *sems[:3])
+    p.barrier("plane")
+    g = PlaneGather(p, tok, tok_out, *sems[:3])
     s = Spread(p, True, small, small_out, *sems[3:5])
     w = Spread(p, False, weights, weights_out, *sems[5:7])
     s.begin()
@@ -348,7 +373,7 @@
         ],
         in_specs=any_specs(3),
         out_specs=any_specs(3),
-        scratch_shapes=Gather.semaphores(U, B, True) + Spread.semaphores(U, B) * 2,
+        scratch_shapes=PlaneGather.semaphores(U, B) + Spread.semaphores(U, B) * 2,
         compiler_params=pltpu.CompilerParams(collective_id=cid, has_side_effects=True),
     )(tok, small, weights)
 
@@ -388,8 +413,8 @@
 
 
 class Scatter:
-    def __init__(self, p, by_seq, acc, rc, rx0, rx1, ry0, ry1, rz, fin, loc, cs, cr, xs, xr, ys, yr, zs, zr):
-        self.p, self.by_seq = p, by_seq
+    def __init__(self, p, acc, rc, rx0, rx1, ry0, ry1, rz, fin, loc, cs, cr, xs, xr, ys, yr, zs, zr):
+        self.p = p
         self.acc, self.rc, self.rx, self.ry, self.rz, self.fin = acc, rc, (rx0, rx1), (ry0, ry1), rz, fin
         self.loc, self.cs, self.cr = loc, cs, cr
         self.xs, self.xr, self.ys, self.yr, self.zs, self.zr = xs, xr, ys, yr, zs, zr
@@ -399,13 +424,13 @@
         self.local = True
 
     @staticmethod
-    def scratch(U, B, by_seq, rows, D, t):
+    def scratch(U, B, rows, D, t):
         X, Y, Z, Q = U // 2, 2, B // 2, U * B // 2
         dma = pltpu.SemaphoreType.DMA
         x, y = max(X - 1, 1), Y - 1
         return [
             pltpu.VMEM((Q, 2, rows, D), t),
-            pltpu.VMEM((1, 1, 16, 128) if by_seq else (Q, 2, rows, D), t),
+            pltpu.VMEM((Q, 2, rows, D), t),
             pltpu.VMEM((x, Z * Y, rows, D), t),
             pltpu.VMEM((x, Z, rows, D), t),
             pltpu.VMEM((y, Z, rows, D), t),
@@ -433,57 +458,30 @@
     def got(self, ref, sem):
         remote(ref, ref, sem, sem, self.p.core_peer).wait_recv()
 
-    def pieces(self, k):
-        p = self.p
-        ox, oy = p.others("x"), p.others("y")
-        return (
-            [(0, j, i, k) for j in ox for i in range(p.Y)] + [(1, j, i, k) for i in oy for j in range(p.X)],
-            [(0, p.x, i, k) for i in oy] + [(1, j, p.y, k) for j in ox],
-            [(0, p.x, p.y, k), (1, p.x, p.y, k)],
-        )
-
     def load(self, src):
         p = self.p
         for k in self.order:
-            for some in self.pieces(k):
-                for h, j, i, _ in some:
-                    q = p.chip(j, i, k)
-                    if self.by_seq:
-                        mine = src.at[p.block(j, i, k, h)]
-                    else:
-                        self.across(src.at[p.block(j, i, k, 1 - p.c), h], q, h)
-                        mine = src.at[p.block(j, i, k, p.c), h]
-                    pltpu.make_async_copy(mine, self.acc.at[q, h], self.loc.at[q, h]).start()
+            for j in p.others("x") + [p.x]:
+                for i in range(p.Y):
+                    for h in (0, 1):
+                        q = p.chip(j, i, k)
+                        cp = self.across(src.at[p.block(j, i, k, 1 - p.c), h], q, h)
+                        cp.start()
+                        self.started.append(cp)
+                        self.keep(src.at[p.block(j, i, k, p.c), h], q, h).start()
+
+    def keep(self, src, q, h):
+        return pltpu.make_async_copy(src, self.acc.at[q, h], self.loc.at[q, h])
 
     def across(self, src, q, h):
-        self.start(src, self.rc.at[q, h], self.cs.at[q, h], self.cr.at[q, h], self.p.core_peer)
+        return remote(src, self.rc.at[q, h], self.cs.at[q, h], self.cr.at[q, h], self.p.core_peer)
 
     def ready(self, h, j, i, k):
         q = self.p.chip(j, i, k)
         if self.local:
-            pltpu.make_async_copy(self.acc.at[q, h], self.acc.at[q, h], self.loc.at[q, h]).wait()
-        if self.by_seq:
-            return []
+            self.keep(self.acc.at[q, h], q, h).wait()
         self.got(self.rc.at[q, h], self.cr.at[q, h])
         return [self.rc.at[q, h]]
-
-    def add(self, dst, srcs, f32_out=None):
-        if not srcs and f32_out is None:
-            return
-        step = 16
-
-        def one(n, _):
-            r = pl.ds(pl.multiple_of(n * step, step), step)
-            t = dst[r, :].astype(jnp.float32)
-            for s in srcs:
-                t = t + s[r, :].astype(jnp.float32)
-            if f32_out is None:
-                dst[r, :] = t.astype(dst.dtype)
-            else:
-                f32_out[r, :] = t
-            return 0
-
-        lax.fori_loop(0, dst.shape[0] // step, one, 0)
 
     def send_x(self, h, q, j, s):
         p = self.p
@@ -511,132 +509,249 @@
             out.append(self.ry[h].at[o, s])
         return out
 
-    def step(self, n):
+    def last(self, n, h, q, extra):
+        p = self.p
+        k = self.order[n]
+        if n < p.Z - 1:
+            add(self.acc.at[q, h], extra)
+            self.start(self.acc.at[q, h], self.rz.at[h, p.z], self.zs.at[h, k], self.zr.at[h, p.z],
+                       p.dev(p.x, p.y, k, p.c))
+        else:
+            for a in p.others("z"):
+                self.got(self.rz.at[h, a], self.zr.at[h, a])
+                extra.append(self.rz.at[h, a])
+            add(self.acc.at[q, h], extra, self.fin.at[h])
+
+    def first(self, n, j):
+        p = self.p
+        k = self.order[n]
+        if j is not p.x:
+            for i in range(p.Y):
+                q = p.chip(j, i, k)
+                add(self.acc.at[q, 0], self.ready(0, j, i, k))
+                self.send_x(0, q, j, k * p.Y + i)
+        for i in p.others("y"):
+            q = p.chip(j, i, k)
+            add(self.acc.at[q, 1], self.ready(1, j, i, k))
+            self.send_y(1, q, i, k * p.X + j)
+
+    def rest(self, n):
         p = self.p
         X, Y, Z = p.X, p.Y, p.Z
-        if n < Z:
-            k = self.order[n]
-            for h, j, i, _ in self.pieces(k)[0]:
-                q = p.chip(j, i, k)
-                self.add(self.acc.at[q, h], self.ready(h, j, i, k))
-                if h == 0:
-                    self.send_x(0, q, j, k * Y + i)
-                else:
-                    self.send_y(1, q, i, k * X + j)
         if 1 <= n <= Z:
             k = self.order[n - 1]
-            for h, j, i, _ in self.pieces(k)[1]:
-                q = p.chip(j, i, k)
-                extra = self.ready(h, j, i, k)
-                if h == 0:
-                    self.add(self.acc.at[q, 0], extra + self.from_x(0, k * Y + i))
-                    self.send_y(0, q, i, k)
-                else:
-                    self.add(self.acc.at[q, 1], extra + self.from_y(1, k * X + j))
-                    self.send_x(1, q, j, k)
+            for i in p.others("y"):
+                q = p.chip(p.x, i, k)
+                add(self.acc.at[q, 0], self.ready(0, p.x, i, k) + self.from_x(0, k * Y + i))
+                self.send_y(0, q, i, k)
+            for j in p.others("x"):
+                q = p.chip(j, p.y, k)
+                add(self.acc.at[q, 1], self.ready(1, j, p.y, k) + self.from_y(1, k * X + j))
+                self.send_x(1, q, j, k)
         if n >= 2:
             k = self.order[n - 2]
-            for h, j, i, _ in self.pieces(k)[2]:
-                q = p.chip(j, i, k)
-                extra = self.ready(h, j, i, k)
-                if h == 0:
-                    extra = extra + self.from_x(0, k * Y + i) + self.from_y(0, k)
-                else:
-                    extra = extra + self.from_y(1, k * X + j) + self.from_x(1, k)
-                if n - 2 < Z - 1:
-                    self.add(self.acc.at[q, h], extra)
-                    self.start(self.acc.at[q, h], self.rz.at[h, p.z], self.zs.at[h, k], self.zr.at[h, p.z],
-                               p.dev(p.x, p.y, k, p.c))
-                else:
-                    for a in p.others("z"):
-                        self.got(self.rz.at[h, a], self.zr.at[h, a])
-                        extra.append(self.rz.at[h, a])
-                    self.add(self.acc.at[q, h], extra, self.fin.at[h])
+            q = p.chip(p.x, p.y, k)
+            self.last(n - 2, 0, q, self.ready(0, p.x, p.y, k) + self.from_x(0, k * Y + p.y) + self.from_y(0, k))
+            self.last(n - 2, 1, q, self.ready(1, p.x, p.y, k) + self.from_y(1, k * X + p.x) + self.from_x(1, k))
+
+    def step(self, n):
+        if n < self.p.Z:
+            for j in self.p.others("x") + [self.p.x]:
+                self.first(n, j)
+        self.rest(n)
 
     def sent(self):
         for cp in self.started:
             cp.wait_send()
 
 
-def give(p, by_seq, fin, out, sems):
-    if by_seq:
-        away = remote(fin.at[1 - p.c], out.at[p.c], sems.at[0], sems.at[1], p.core_peer)
-        away.start()
-        cp = pltpu.make_async_copy(fin.at[p.c], out.at[p.c], sems.at[2])
-        cp.start()
-        cp.wait()
-        remote(out.at[1 - p.c], out.at[1 - p.c], sems.at[0], sems.at[1], p.core_peer).wait_recv()
-        away.wait_send()
-    else:
-        cp = pltpu.make_async_copy(fin, out, sems.at[2])
-        cp.start()
-        cp.wait()
-
-
-def scatter_kernel(U, B, by_seq, src, out, *scratch):
+def add(dst, srcs, f32_out=None):
+    step = 16
+
+    def one(n, _):
+        r = pl.ds(pl.multiple_of(n * step, step), step)
+        t = dst[r, :].astype(jnp.float32)
+        for s in srcs:
+            t = t + s[r, :].astype(jnp.float32)
+        if f32_out is None:
+            dst[r, :] = t.astype(dst.dtype)
+        else:
+            f32_out[r, :] = t
+        return 0
+
+    lax.fori_loop(0, dst.shape[0] // step, one, 0)
+
+
+class PlaneScatter(Scatter):
+    def __init__(self, p, acc, rc, ry, rz, fin, loc, cs, cr, ys, yr, zs, zr):
+        self.p = p
+        self.acc, self.rc, self.rz, self.fin, self.ry = acc, rc, rz, fin, (ry.at[0], ry.at[1])
+        self.loc, self.cs, self.cr = loc, cs, cr
+        self.ys, self.yr, self.zs, self.zr = ys, yr, zs, zr
+        self.order = p.others("z") + [p.z]
+        self.steps = p.Z + 1
+        self.started = []
+        self.local = True
+
+    @staticmethod
+    def scratch(U, B, rows, D, t):
+        Y, Z = 2, B // 2
+        dma = pltpu.SemaphoreType.DMA
+        return [
+            pltpu.VMEM((B, 2, rows, D), t),
+            pltpu.VMEM((B, 2, rows, D), t),
+            pltpu.VMEM((2, Y - 1, Z, rows, D), t),
+            pltpu.VMEM((2, Z, rows, D), t),
+            pltpu.VMEM((2, rows, D), jnp.float32),
+            dma((B, 2)),
+            dma((B, 2)),
+            dma((B, 2)),
+            dma((2, Y - 1, Z)),
+            dma((2, Y - 1, Z)),
+            dma((2, Z)),
+            dma((2, Z)),
+        ]
+
+    SCRATCH = 12
+
+    def load(self, src):
+        p = self.p
+        for k in self.order:
+            for i in p.others("y") + [p.y]:
+                for h in (0, 1):
+                    q = p.chip(0, i, k)
+                    cp = self.across(src.at[p.block(h, i, k, 1 - p.c)], q, h)
+                    cp.start()
+                    self.started.append(cp)
+                    self.keep(src.at[p.block(h, i, k, p.c)], q, h).start()
+
+    def step(self, n):
+        p = self.p
+        if n < p.Z:
+            k = self.order[n]
+            for i in p.others("y"):
+                q = p.chip(0, i, k)
+                for h in (0, 1):
+                    add(self.acc.at[q, h], self.ready(h, 0, i, k))
+                    self.send_y(h, q, i, k)
+        if n >= 1:
+            k = self.order[n - 1]
+            q = p.chip(0, p.y, k)
+            for h in (0, 1):
+                self.last(n - 1, h, q, self.ready(h, 0, p.y, k) + self.from_y(h, k))
+
+
+def keep_sum(fin, out, sem):
+    cp = pltpu.make_async_copy(fin, out, sem)
+    cp.start()
+    cp.wait()
+
+
+class Combine:
+    def __init__(self, s, rows_in, hot_in, cols, rows_buf, hot_buf, stage, sems):
+        self.s, self.p = s, s.p
+        self.rows_in, self.hot_in, self.cols = rows_in, hot_in, cols
+        self.rows_buf, self.hot_buf, self.stage, self.sems = rows_buf, hot_buf, stage, sems
+        self.sent = []
+        s.local = False
+
+    def loads(self, j, k):
+        g = j * self.p.Z + k
+        RB = self.rows_buf.shape[1]
+        rows = pl.ds(pl.multiple_of(g * RB, RB), RB)
+        return (
+            pltpu.make_async_copy(self.rows_in.at[:, rows, self.cols], self.rows_buf, self.sems.at[0]),
+            pltpu.make_async_copy(self.hot_in.at[g], self.hot_buf, self.sems.at[1]),
+        )
+
+    def fetch(self, j, k):
+        for cp in self.loads(j, k):
+            cp.start()
+
+    def make(self, j, k):
+        p, s = self.p, self.s
+        for cp in self.loads(j, k):
+            cp.wait()
+        for cp in self.sent:
+            cp.wait_send()
+        self.sent.clear()
+        experts, RB, D = self.rows_buf.shape
+        KB = self.hot_buf.shape[1]
+        cut = min(D, 512)
+
+        for n in range(0, D, cut):
+            t = lax.dot_general(self.hot_buf[...], self.rows_buf[:, :, n:n + cut].reshape(experts * RB, cut),
+                                (((0,), (0,)), ((), ())), preferred_element_type=jnp.float32)
+            self.stage[:, :, :, n:n + cut] = t.astype(self.stage.dtype).reshape(self.stage.shape[:3] + (cut,))
+        kept = []
+        for i in range(p.Y):
+            for h in (0, 1):
+                q = p.chip(j, i, k)
+                cp = s.across(self.stage.at[(1 - p.c) * p.Y + i, h], q, h)
+                cp.start()
+                self.sent.append(cp)
+                cp = s.keep(self.stage.at[p.c * p.Y + i, h], q, h)
+                cp.start()
+                kept.append(cp)
+        for cp in kept:
+            cp.wait()
+
+    def end(self):
+        for cp in self.sent:
+            cp.wait_send()
+
+
+def pair_kernel(U, B, cols, a, b, hot, out_a, out_b, *scratch):
     p = Place(U, B)
     p.barrier("lines")
-    s = Scatter(p, by_seq, *scratch[:Scatter.SCRATCH])
-    s.load(src)
-    for n in range(s.steps):
-        s.step(n)
-    give(p, by_seq, s.fin, out, scratch[-1])
-    s.sent()
-
-
-def in_parts(call, v, F, D):
-    parts = max(1, F * D // 65536)
-    w = D // parts
-    return jnp.concatenate([call(v[..., n * w:(n + 1) * w]) for n in range(parts)], axis=-1)
-
-
-def scatter_blocks(v, U, B, by_seq, cid):
-    def call(m):
-        rows, D = m.shape[-2:]
+    k = Scatter.SCRATCH
+    work = [Scatter(p, *scratch[k * i:k * (i + 1)]) for i in range(2)]
+    feed = [Combine(s, m, hot, cols, *scratch[2 * k:2 * k + 4]) for s, m in zip(work, (a, b))]
+    feed[1].sent = feed[0].sent
+    xs = p.others("x") + [p.x]
+    todo = [(f, j, z) for z in work[0].order for f in feed for j in xs]
+    todo[0][0].fetch(*todo[0][1:])
+    at = 0
+    for n in range(work[0].steps):
+        for s in work:
+            if n < p.Z:
+                for x in xs:
+                    f, j, z = todo[at]
+                    f.make(j, z)
+                    at += 1
+                    if at < len(todo):
+                        todo[at][0].fetch(*todo[at][1:])
+                    s.first(n, x)
+            s.rest(n)
+    feed[0].end()
+    for s, out in zip(work, (out_a, out_b)):
+        keep_sum(s.fin, out, scratch[-1].at[0])
+        s.sent()
+
+
+def scatter_pair(a, b, hot, rows, U, B, cid):
+    F = U * B
+    experts, _, D = a.shape
+    G, n, KB = hot.shape
+    RB = n // experts
+    parts = max(1, F // 32)
+    D = D // parts
+    dma = pltpu.SemaphoreType.DMA
+
+    def call(c):
         return pl.pallas_call(
-            functools.partial(scatter_kernel, U, B, by_seq),
-            out_shape=jax.ShapeDtypeStruct((2, rows, D), jnp.float32),
-            in_specs=any_specs(1),
-            out_specs=any_specs(1)[0],
-            scratch_shapes=Scatter.scratch(U, B, by_seq, rows, D, m.dtype) + [pltpu.SemaphoreType.DMA((3,))],
+            functools.partial(pair_kernel, U, B, pl.ds(c * D, D)),
+            out_shape=[jax.ShapeDtypeStruct((2, rows, D), jnp.float32)] * 2,
+            in_specs=any_specs(3),
+            out_specs=any_specs(2),
+            scratch_shapes=Scatter.scratch(U, B, rows, D, a.dtype) * 2 + [
+                pltpu.VMEM((experts, RB, D), a.dtype), pltpu.VMEM((n, KB), hot.dtype),
+                pltpu.VMEM((4, 2, rows, D), a.dtype), dma((2,)), dma((1,))],
             compiler_params=pltpu.CompilerParams(
-                collective_id=cid, has_side_effects=True, vmem_limit_bytes=58 * 2**20),
-        )(m)
-
-    return in_parts(call, v, U * B, v.shape[-1])
-
-
-def pair_kernel(U, B, n, *refs):
-    p = Place(U, B)
-    p.barrier("lines")
-    srcs, outs, scratch = refs[:n], refs[n:2 * n], refs[2 * n:]
-    work = [Scatter(p, False, *scratch[Scatter.SCRATCH * i:Scatter.SCRATCH * (i + 1)]) for i in range(n)]
-    for s, src in zip(work, srcs):
-        s.load(src)
-    for k in range(work[0].steps):
-        for s in work:
-            s.step(k)
-    for i, s in enumerate(work):
-        give(p, False, s.fin, outs[i], scratch[-1])
-        s.sent()
-
-
-def scatter_pair(a, b, U, B, cid):
-    def call(v, w):
-        rows, D = v.shape[-2:]
-        return pl.pallas_call(
-            functools.partial(pair_kernel, U, B, 2),
-            out_shape=[jax.ShapeDtypeStruct((2, rows, D), jnp.float32)] * 2,
-            in_specs=any_specs(2),
-            out_specs=any_specs(2),
-            scratch_shapes=Scatter.scratch(U, B, False, rows, D, v.dtype) * 2 + [pltpu.SemaphoreType.DMA((3,))],
-            compiler_params=pltpu.CompilerParams(
-                collective_id=cid, has_side_effects=True, vmem_limit_bytes=60 * 2**20),
-        )(v, w)
-
-    parts = max(1, U * B // 32)
-    w = a.shape[-1] // parts
-    got = [call(a[..., n * w:(n + 1) * w], b[..., n * w:(n + 1) * w]) for n in range(parts)]
+                collective_id=cid, has_side_effects=True, vmem_limit_bytes=62 * 2**20),
+        )(a, b, hot)
+
+    got = [call(c) for c in range(parts)]
     return tuple(jnp.concatenate([g[i] for g in got], axis=-1) for i in range(2))
 
 
@@ -647,91 +762,102 @@
 
     @staticmethod
     def scratch(U, B, rows, w, t):
-        X, Q = U // 2, U * B // 2
         dma = pltpu.SemaphoreType.DMA
-        return [pltpu.VMEM((Q, rows, w), t), pltpu.VMEM((Q, rows, w), t),
-                dma((X,)), dma((X + Q,)), dma((X + Q,))]
+        return [pltpu.VMEM((2 * B, rows, w), t), pltpu.VMEM((2 * B, rows, w), t),
+                dma((1,)), dma((1 + 2 * B,)), dma((1 + 2 * B,))]
 
     SCRATCH = 5
 
-    def across(self, j):
-        p = self.p
-        part = self.rc.at[pl.ds(j * p.B, p.B)]
-        return remote(self.src.at[j, 1 - p.c], part, self.send.at[j], self.recv.at[j], p.core_peer)
-
-    def own(self, j):
-        p = self.p
-        return pltpu.make_async_copy(self.src.at[j, p.c], self.acc.at[pl.ds(j * p.B, p.B)], self.local.at[j])
+    def across(self):
+        p = self.p
+        return remote(self.src.at[1 - p.x], self.rc, self.send.at[0], self.recv.at[0], p.x_peer)
+
+    def own(self):
+        return pltpu.make_async_copy(self.src.at[self.p.x], self.acc, self.local.at[0])
 
     def away(self, o):
         p = self.p
-        q = lax.rem(p.q + o, p.Q)
-        return remote(self.acc.at[q], self.out.at[p.q], self.send.at[p.X + q], self.recv.at[p.X + p.q], p.chip_dev(q))
+        r = lax.rem(p.r + o, 2 * p.B)
+        return remote(self.acc.at[r], self.out.at[p.r], self.send.at[1 + r], self.recv.at[1 + p.r], p.plane_dev(r))
 
     def begin(self):
-        for j in range(self.p.X):
-            self.across(j).start()
-            self.own(j).start()
+        self.across().start()
+        self.own().start()
 
     def middle(self):
         p = self.p
-        for j in range(p.X):
-            self.own(j).wait()
-            self.across(j).wait_recv()
-
-        @pl.loop(0, p.Q)
-        def _(q):
-            t = self.acc[q].astype(jnp.float32) + self.rc[q].astype(jnp.float32)
-            self.acc[q] = t.astype(self.acc.dtype)
-
-        @pl.loop(1, p.Q)
+        self.own().wait()
+        self.across().wait_recv()
+
+        @pl.loop(0, 2 * p.B)
+        def _(r):
+            t = self.acc[r].astype(jnp.float32) + self.rc[r].astype(jnp.float32)
+            self.acc[r] = t.astype(self.acc.dtype)
+
+        @pl.loop(1, 2 * p.B)
         def _(o):
             self.away(o).start()
 
-        cp = pltpu.make_async_copy(self.acc.at[p.q], self.out.at[p.q], self.local.at[0])
+        cp = pltpu.make_async_copy(self.acc.at[p.r], self.out.at[p.r], self.local.at[0])
         cp.start()
         cp.wait()
 
     def end(self):
         p = self.p
-        for j in range(p.X):
-            self.across(j).wait_send()
-
-        @pl.loop(1, p.Q)
+        self.across().wait_send()
+
+        @pl.loop(1, 2 * p.B)
         def _(o):
-            q = lax.rem(p.q + o, p.Q)
-            part = self.out.at[q]
-            remote(part, part, self.send.at[0], self.recv.at[p.X + q], p.core_peer).wait_recv()
+            r = lax.rem(p.r + o, 2 * p.B)
+            part = self.out.at[r]
+            remote(part, part, self.send.at[0], self.recv.at[1 + r], p.x_peer).wait_recv()
             self.away(o).wait_send()
 
 
 def finish_kernel(U, B, more, *refs):
     p = Place(U, B)
-    p.barrier("all")
+    p.barrier("plane")
     n = 4 if more else 3
-    srcs, outs, scratch = refs[:n], refs[n:2 * n], refs[2 * n:]
-    k = Scatter.SCRATCH
-    work = [Scatter(p, True, *scratch[:k])]
+    srcs, outs, scratch = refs[:n], refs[n:2 * n + 1], refs[2 * n + 1:]
+    at = PlaneScatter.SCRATCH
+    work = [PlaneScatter(p, *scratch[:at])]
     if more:
-        work.append(Scatter(p, False, *scratch[k:2 * k]))
-    ex, at = [], k * len(work)
+        work.append(Scatter(p, *scratch[at:at + Scatter.SCRATCH]))
+        at += Scatter.SCRATCH
+    ex = []
     for i in range(2):
         ex.append(PairExchange(p, srcs[i], outs[i], *scratch[at:at + PairExchange.SCRATCH]))
         at += PairExchange.SCRATCH
+    stage, sems = scratch[at:]
+    for s, src in zip(work, srcs[2:]):
+        s.load(src)
     for e in ex:
         e.begin()
-    for s, src in zip(work, srcs[2:]):
-        s.load(src)
     work[0].step(0)
     for e in ex:
         e.middle()
     for s in work[1:]:
         s.step(0)
-    for j in range(1, p.Z + 2):
+    for j in range(1, p.Z + 1):
         for s in work:
             s.step(j)
-    for s, out, by_seq in zip(work, outs[2:], (True, False)):
-        give(p, by_seq, s.fin, out, scratch[-1])
+    fin = work[0].fin
+    rows = fin.shape[1]
+
+    def one(m, _):
+        r = pl.ds(pl.multiple_of(m * 16, 16), 16)
+        stage[r, :] = fin[1 - p.x, r, :].astype(stage.dtype)
+        return 0
+
+    lax.fori_loop(0, rows // 16, one, 0)
+    away = remote(stage, outs[3], sems.at[0], sems.at[1], p.x_peer)
+    away.start()
+    keep_sum(fin.at[p.x], outs[2], sems.at[2])
+    if more:
+        work[1].step(p.Z + 1)
+        keep_sum(work[1].fin, outs[4], sems.at[2])
+    away.wait_recv()
+    away.wait_send()
     for s in work:
         s.sent()
     for e in ex:
@@ -739,37 +865,37 @@
 
 
 def finish(weights, small, hidden, out, U, B, cid):
-    X, F, Q = U // 2, U * B, U * B // 2
+    F = U * B
     parts = max(1, F // 32)
-    rows, D = hidden.shape[-2:]
-    D = D // parts
+    D = hidden.shape[-1] // parts
     sds, f32 = jax.ShapeDtypeStruct, jnp.float32
 
-    def call(w, s, h, o):
-        args = [w.reshape((X, 2, B) + w.shape[1:]), s.reshape((X, 2, B) + s.shape[1:]), h]
-        shapes = [sds((Q,) + w.shape[1:], w.dtype), sds((Q,) + s.shape[1:], s.dtype), sds((2,) + h.shape[1:], f32)]
-        scratch = Scatter.scratch(U, B, True, h.shape[1], h.shape[2], h.dtype)
+    def call(h, o, cid):
+        args = [m.reshape((2, 2 * B) + m.shape[1:]) for m in (weights, small)] + [h]
+        shapes = [sds((2 * B,) + m.shape[1:], m.dtype) for m in (weights, small)]
+        shapes += [sds(h.shape[1:], f32), sds(h.shape[1:], h.dtype)]
+        scratch = PlaneScatter.scratch(U, B, h.shape[1], h.shape[2], h.dtype)
         if o is not None:
             args.append(o)
             shapes.append(sds(o.shape[1:], f32))
-            scratch += Scatter.scratch(U, B, False, o.shape[2], o.shape[3], o.dtype)
-        for m in (w, s):
+            scratch += Scatter.scratch(U, B, o.shape[2], o.shape[3], o.dtype)
+        for m in (weights, small):
             scratch += PairExchange.scratch(U, B, m.shape[1], m.shape[2], m.dtype)
         return pl.pallas_call(
             functools.partial(finish_kernel, U, B, o is not None),
             out_shape=shapes,
             in_specs=any_specs(len(args)),
-            out_specs=any_specs(len(args)),
-            scratch_shapes=scratch + [pltpu.SemaphoreType.DMA((3,))],
+            out_specs=any_specs(len(shapes)),
+            scratch_shapes=scratch + [pltpu.VMEM(h.shape[1:], h.dtype), pltpu.SemaphoreType.DMA((3,))],
             compiler_params=pltpu.CompilerParams(
-                collective_id=cid, has_side_effects=True, vmem_limit_bytes=60 * 2**20),
+                collective_id=cid, has_side_effects=True, vmem_limit_bytes=62 * 2**20),
         )(*args)
 
     if parts == 1:
-        return call(weights, small, hidden, out)
-    w, s, h = call(weights, small, hidden[..., :D], None)
-    rest = [scatter_blocks(hidden[..., n * D:(n + 1) * D], U, B, True, cid + 1) for n in range(1, parts)]
-    return w, s, jnp.concatenate([h] + rest, axis=-1), scatter_by_permutes(out, U, B)
+        return call(hidden, out, cid)
+    got = [call(hidden[..., n * D:(n + 1) * D], None, cid) for n in range(parts)]
+    own, other = (jnp.concatenate([g[i] for g in got], axis=-1) for i in (2, 3))
+    return got[0][0], got[0][1], own, other, scatter_by_permutes(out, U, B)
 
 
 def scatter_by_permutes(v, U, B):
@@ -1063,33 +1189,6 @@
     )(x, pg, rg, wg, wu, wd)
 
 
-def combine_kernel(hot_ref, y_ref, dx_ref, py_ref, pdx_ref):
-    hot = hot_ref[0]
-    rows, KB = hot.shape
-    D = y_ref.shape[2]
-    cut = min(D, 512)
-    for src, dst in ((y_ref, py_ref), (dx_ref, pdx_ref)):
-        for n in range(0, D, cut):
-            t = dot(hot, src[:, :, n:n + cut].reshape(rows, cut), 0, 0)
-            dst[:, :, :, :, :, n:n + cut] = t.astype(dst.dtype).reshape(dst.shape[:-1] + (cut,))
-
-
-def combine(hot, y, dx, shape):
-    G, rows, KB = hot.shape
-    experts, D = y.shape[0], y.shape[2]
-    RB = rows // experts
-    part = pl.BlockSpec((experts, RB, D), lambda g: (0, g, 0))
-    out = group_spec(shape, shape[2])
-    return pl.pallas_call(
-        combine_kernel,
-        grid=(G,),
-        in_specs=[pl.BlockSpec((1, rows, KB), lambda g: (g, 0, 0)), part, part],
-        out_specs=[out, out],
-        out_shape=[jax.ShapeDtypeStruct(shape, jnp.bfloat16)] * 2,
-        compiler_params=pltpu.CompilerParams(vmem_limit_bytes=58 * 2**20),
-    )(hot, y, dx)
-
-
 def body(tokens, w_query, w_key, w_value, w_out, attn_gain, ffn_gain, qk_gain,
          expert_gate, expert_up, expert_down, routes, gates, order, cotangent):
     f32, bf16 = jnp.float32, jnp.bfloat16
@@ -1104,9 +1203,9 @@
     top_count = routes.shape[-1]
     local_experts = expert_gate.shape[0]
     E = local_experts * B
-    chips = F // 2
-    R = chips // H
-    first_copy = lax.rem((u // 2) * B + b, R) == 0
+    R = 2 * B // H
+    x_here = u // 2
+    first_copy = lax.rem((u % 2) * B + b, R) == 0
 
     tok = tokens.transpose(1, 0, 2)
     cot = cotangent.transpose(1, 0, 2)
@@ -1126,7 +1225,7 @@
     small = jnp.pad(small, (0, -small.shape[0] % 1024)).reshape(-1, 128)
     heads_w = jnp.stack([w_query, w_key, w_value]).reshape(3, W, H, HD).transpose(2, 1, 0, 3).reshape(H, W, 3 * HD)
     if R > 1:
-        heads_w = heads_w[np.arange(chips) // R]
+        heads_w = heads_w[np.arange(2 * B) // R]
     seq_tok, table, head_w = front(tok, small, heads_w, U, B, 1)
     seq_tok, head_w = seq_tok.reshape(L, D), head_w.reshape(D, 3 * HD)
     out_w = lax.all_gather(w_out, AXES, axis=0, tiled=True)
@@ -1167,7 +1266,7 @@
     att_rows = exchange(att.reshape(F, positions, HD), U, B, 6)
 
     def from_heads(m):
-        m = m.reshape(U // 2, 2, B, positions, HD).transpose(1, 3, 0, 2, 4)
+        m = m.reshape(2, 2 * B, positions, HD).transpose(0, 2, 1, 3)
         return m.reshape(2, positions, H, R, HD)[:, :, :, 0].reshape(T, H * HD)
 
     attended = from_heads(att_rows)
@@ -1175,13 +1274,11 @@
     normed_full, ffn_back = jax.vjp(rms_norm, residual, ffn_g)
     normed = normed_full.astype(bf16).reshape(2, positions, D)
 
-    normed_all = gather_blocks(normed, U, B, False, 2)
+    normed_all = gather_blocks(normed, U, B, 2)
     shape = groups + (T, D)
     x, pair_grad, hot, row_gate = dispatch(val, gate_of, normed_all.reshape(shape), cot_all.reshape(shape), RB)
     y, dx, gate_grad, up_grad, down_grad = expert_layer(x, pair_grad, row_gate, expert_gate, expert_up, expert_down)
-    mixed_part, normed_part = combine(hot, y, dx, shape)
-    blocks = (F, 2, positions, D)
-    mixed_sum, normed_grad = scatter_pair(mixed_part.reshape(blocks), normed_part.reshape(blocks), U, B, 3)
+    normed_grad, mixed_sum = scatter_pair(dx, y, hot, positions, U, B, 3)
     mixed = (residual + mixed_sum.reshape(T, D)).reshape(2, positions, D).transpose(1, 0, 2).astype(bf16)
     normed_grad = normed_grad.reshape(T, D)
 
@@ -1189,8 +1286,8 @@
     residual_grad = cot.reshape(T, D).astype(f32) + residual_norm_grad
     attn_out_grad = residual_grad.astype(bf16)
     att_grad = dot(attn_out_grad, out_w, 1, 1).astype(bf16)
-    att_grad = jnp.repeat(att_grad.reshape(2, positions, H, HD).transpose(2, 0, 1, 3), R, axis=0)
-    att_grad = att_grad.reshape(U // 2, B, 2, positions, HD).transpose(0, 2, 1, 3, 4).reshape(F, positions, HD)
+    att_grad = jnp.repeat(att_grad.reshape(2, positions, H, HD).transpose(0, 2, 1, 3), R, axis=1)
+    att_grad = att_grad.reshape(F, positions, HD)
     do = exchange(att_grad, U, B, 6).reshape(L, HD)
     out_part = dot(attended, attn_out_grad, 0, 0).astype(bf16)
     out_part = out_part.reshape(F, 2, W // 2, D)
@@ -1204,8 +1301,10 @@
         [attn_gain_part[0].reshape(F, W), ffn_gain_part.reshape(F, W),
          qk_part[0].reshape(F, nq), qk_part[1].reshape(F, nq)], axis=1)
     small = jnp.pad(small, ((0, 0), (0, -small.shape[1] % 1024))).reshape(F, -1, 128)
-    weight_grad, small, hidden_grad, out_grad = finish(
+    weight_grad, small, own, other, out_grad = finish(
         weight_part, small, hidden_part.reshape(F, positions, D), out_part, U, B, 4)
+    other = other.astype(f32)
+    hidden_grad = jnp.where(x_here == 0, jnp.stack([own, other]), jnp.stack([other, own]))
     small = jnp.sum(small, axis=0).reshape(-1)
     weight_grad = weight_grad.reshape(H, R, W, 3 * HD).astype(f32).sum(axis=1)
     weight_grad = weight_grad.transpose(1, 0, 2).reshape(W, H, 3, HD)

time: 859 us -> 798 us (0.929)
  Pallas kernels: 762 us -> 700 us
    pallas_call x3 -> x2, Pallas kernels: 288 us -> 263 us  [the longest x1 157 us: call(): pl.pallas_call(functools.partial(pair_kernel, U, B, pl.ds(c * D, D)), out...]
    pallas_call x1, Pallas kernels: 133 us -> 114 us  [call(): pl.pallas_call(functools.partial(finish_kernel, U, B, o is not None), out...]
    pallas_call x1, Pallas kernels: 125 us -> 113 us  [front(): pl.pallas_call(functools.partial(front_kernel, U, B), out_shape=[jax.Shap...]
  transfers between devices with their start and end apart: 2 -> 2, of which waited for: 0 -> 0; matrix products, arithmetic and copies ran while one was open for 4% -> 5% of each run, Pallas kernels for 32% -> 33%
where the time goes in v3:
time: 798 us; the launch traced here: 793 us
  Pallas kernels  700 us (88%)
  local copies, waits for them, and re-layouts  38 us (5%)
  other arithmetic  26.4 us (3%)
  between operations  14.8 us (2%)
  matrix products  13.3 us (2%)
    pallas_call x1, Pallas kernels, call(): pl.pallas_call(functools.partial(pair_kernel, U, B, pl.ds(c * D, D)), out...  157 us
    pallas_call x1, Pallas kernels, call(): pl.pallas_call(functools.partial(finish_kernel, U, B, o is not None), out...  114 us
    pallas_call x1, Pallas kernels, front(): pl.pallas_call(functools.partial(front_kernel, U, B), out_shape=[jax.Shap...  113 us
    pallas_call x1, Pallas kernels, gather_blocks(): pl.pallas_call(functools.partial(gather_kernel, U, B), out_shape=jax.Shap...  107 us
    pallas_call x1, Pallas kernels, expert_layer(): pl.pallas_call(expert_kernel, grid=(x.shape[0], rows // step), in_specs=[...  70.6 us
    pallas_call x2, Pallas kernels, exchange(): pl.pallas_call(functools.partial(exchange_kernel, U, B), out_shape=jax.Sh...  38.7 us
    pallas_call x1, Pallas kernels, dispatch(): pl.pallas_call(dispatch_kernel, grid=(G,), in_specs=[one, one, group_spec...  36.6 us
    pallas_call x1, Pallas kernels, head_back(): pl.pallas_call(head_back_kernel, grid=(n // bm,), in_specs=[head] * 7 + [...  20.4 us
  transfers between devices with their start and end apart: 2, of which 0 were waited for; matrix products, arithmetic and copies ran while one was open for 5% of the time, Pallas kernels for 33%

profile of v3, /device:TPU:0, one launch (start us, length us, event | category | flops | bytes accessed | tf_op | source)
XLA Modules:
  0.0 793.2 jit_solution(1263236391331079486)
XLA Ops:
  8.0 2.0 copy.143
  10.5 1.3 reduce.29
  12.1 0.8 copy.80
  13.9 1.0 copy.100
  15.4 1.0 copy.101
  17.0 1.0 copy.102
  18.5 1.8 maximum_bitcast_fusion
  20.3 1.7 reshape.230.weights
  21.9 1.0 convert_reduce_fusion
  23.7 1.3 copy_bitcast_fusion.5
  25.1 112.6 %shard_map.247 = (bf16[32,64,2048]{2,1,0:T(8,128)(2,1)}, f32[32,24,128]{2,1,0:T(8,128)}, bf16[32,64,384]{2,1,0:T(8,128)(2,1)}) custom-call(bf16[2,64,2048]{2,1,0:T(8,128)(2,1)} %get-tuple-element.95.tok, f32[24,128]{1,0:T(8,128)} %pad_bitcast_fusion.small, bf16[16,64,384]{2,1,0:T(8,128)(2,1)} %reshape.230.weights), custom_call_target="tpu_custom_call" | custom-call | tf_op jit(solution)/shard_map/pallas_call | solution.py:367
  137.7 1.1 copy.142
  143.9 3.7 fusion.15
  147.6 1.9 pad_maximum_fusion
  149.5 13.3 %shard_map.248 = (bf16[2048,128]{1,0:T(8,128)(2,1)}, bf16[2048,128]{1,0:T(8,128)(2,1)}, bf16[2048,128]{1,0:T(8,128)(2,1)}, bf16[128,2048]{1,0:T(8,128)(2,1)}, bf...) custom-call(bf16[2048,2048]{1,0:T(8,128)(2,1)} %bitcast.147, f32[1,2048]{1,0:T(1,128)} %reshape.233.gain_ref, ...), custom_call_target="tpu_custom_call" | custom-call | tf_op jit(solution)/shard_map/pallas_call | solution.py:1033
  162.9 12.6 %shard_map.249 = (bf16[2048,128]{1,0:T(8,128)(2,1)}, f32[1,2048]{1,0:T(1,128)}) custom-call(bf16[2048,128]{1,0:T(8,128)(2,1)} %get-tuple-element.50.q_ref, bf16[2048,128]{1,0:T(8,128)(2,1)} %get-tuple-element.51.k_ref, bf16[128,2048]{1,0:T(8,128)(2,1)} %get-tuple-element.52.vt_ref), custom_call_target="tpu_custom_call" | custom-call | tf_op jit(solution)/shard_map/pallas_call | solution.py:955
  175.5 19.8 %shard_map.250 = bf16[32,64,128]{2,1,0:T(8,128)(2,1)} custom-call(bf16[32,64,128]{2,1,0:T(8,128)(2,1)} %bitcast.186), custom_call_target="tpu_custom_call" | custom-call | tf_op jit(solution)/shard_map/pallas_call | solution.py:405
  195.2 1.4 copy.86
  196.7 4.8 multiply_reduce_fusion.3
  201.5 1.1 multiply_convert_fusion
  202.6 106.8 %shard_map.251 = bf16[32,2,64,2048]{3,2,1,0:T(8,128)(2,1)} custom-call(bf16[2,64,2048]{2,1,0:T(8,128)(2,1)} %bitcast.162), custom_call_target="tpu_custom_call" | custom-call | tf_op jit(solution)/shard_map/pallas_call | solution.py:335
  309.4 36.6 %shard_map.252 = (bf16[8,640,2048]{2,1,0:T(8,128)(2,1)}, bf16[8,640,2048]{2,1,0:T(8,128)(2,1)}, bf16[8,640,512]{2,1,0:T(8,128)(2,1)}, f32[8,640,128]{2,1,0:T(8,128)}) custom-call(s32[8,8,512]{2,1,0:T(8,128)} %bitcast.177, f32[8,8,512]{2,1,0:T(8,128)} %bitcast.176, bf16[2,2,4,2,128,2048]{5,4,3,2,1,0:T(8,128)(2,1)} %bitcast.143, ...), custom_call_target="tpu_custom_call" | custom-call | tf_op jit(solution)/shard_map/pallas_call | solution.py:1133
  346.0 70.6 %shard_map.253 = (bf16[8,640,2048]{2,1,0:T(8,128)(2,1)}, bf16[8,640,2048]{2,1,0:T(8,128)(2,1)}, f32[8,2048,256]{2,1,0:T(8,128)}, f32[8,2048,256]{2,1,0:T(8,128)}, f32[8,256,2048]{2,1,0:T(8,128)}) custom-call(bf16[8,640,2048]{2,1,0:T(8,128)(2,1)} %get-tuple-element.54.x_ref, bf16[8,640,2048]{2,1,0:T(8,128)(2,1)} %get-tuple-element.55.pg_ref, ...), custom_call_target="tpu_custom_call" | custom-call | tf_op jit(solution)/shard_map/pallas_call | solution.py:1182
  416.6 156.7 %shard_map.254 = (f32[2,64,2048]{2,1,0:T(8,128)}, f32[2,64,2048]{2,1,0:T(8,128)}) custom-call(bf16[8,640,2048]{2,1,0:T(8,128)(2,1)} %get-tuple-element.57.a, bf16[8,640,2048]{2,1,0:T(8,128)(2,1)} %get-tuple-element.58.b, bf16[8,640,512]{2,1,0:T(8,128)(2,1)} %get-tuple-element.59.hot), custom_call_target="tpu_custom_call" | custom-call | tf_op jit(solution)/shard_map/pallas_call | solution.py:742
  573.3 1.5 fusion.7
  574.8 2.4 fusion.1
  577.2 1.3 copy.141
  578.5 5.6 convolution_convert_fusion
  584.1 2.9 fusion
  587.2 0.9 copy.95
  588.1 18.9 %shard_map.255 = bf16[32,64,128]{2,1,0:T(8,128)(2,1)} custom-call(bf16[32,64,128]{2,1,0:T(8,128)(2,1)} %bitcast.165), custom_call_target="tpu_custom_call" | custom-call | tf_op jit(solution)/shard_map/pallas_call | solution.py:405
  607.1 17.7 %shard_map.256 = (f32[2048,128]{1,0:T(8,128)}, f32[2048,128]{1,0:T(8,128)}, f32[2048,128]{1,0:T(8,128)}) custom-call(bf16[2048,128]{1,0:T(8,128)(2,1)} %get-tuple-element.50.q_ref, bf16[2048,128]{1,0:T(8,128)(2,1)} %bitcast.159, f32[1,2048]{1,0:T(1,128)} %get-tuple-element.62.lse_ref, bf16[2048,128]{1,0:T(8,128)(2,1)} %get-tuple-element.51.k_ref, ...), custom_call_target="tpu_custom_call" | custom-call | tf_op jit(solution)/shard_map/pallas_call | solution.py:990
  624.8 20.4 %shard_map.257 = (bf16[2048,2048]{1,0:T(8,128)(2,1)}, f32[2048,384]{1,0:T(8,128)}, f32[8,128]{1,0:T(8,128)}, f32[8,2048]{1,0:T(8,128)}) custom-call(f32[2048,128]{1,0:T(8,128)} %get-tuple-element.65.dq_ref, f32[2048,128]{1,0:T(8,128)} %get-tuple-element.66.dk_ref, f32[2048,128]{1,0:T(8,128)} %get-tuple-element.67.dv_ref, ...), custom_call_target="tpu_custom_call" | custom-call | tf_op jit(solution)/shard_map/pallas_call | solution.py:1085
  645.2 3.2 convert_element_type.122
  649.2 0.9 slice_reduce_fusion.3
  651.1 113.9 %shard_map.258 = (bf16[16,64,384]{2,1,0:T(8,128)(2,1)}, f32[16,8,128]{2,1,0:T(8,128)}, f32[64,2048]{1,0:T(8,128)}, bf16[64,2048]{1,0:T(8,128)(2,1)}, f32[2,32,2048]{2,1,0:T(8,128)}) custom-call(bf16[2,16,64,384]{3,2,1,0:T(8,128)(2,1)} %bitcast.153, f32[2,16,8,128]{3,2,1,0:T(8,128)} %bitcast.178, bf16[32,64,2048]{2,1,0:T(8,128)(2,1)} %bitcast.152, ...), custom_call_target="tpu_custom_call" | custom-call | tf_op jit(solution)/shard_map/pallas_call | solution.py:884
  765.0 0.9 reduce_sum.97
  767.1 1.0 bitcast_convert_fusion
  768.1 1.7 multiply_reduce_fusion
  770.5 1.8 copy.137
  772.2 1.3 convert_bitcast_fusion
  773.5 2.1 copy.97
  775.6 2.7 reshape.261
  778.3 4.1 slice_reduce_fusion
  782.4 1.0 copy.138
  783.4 1.0 copy.139
  784.4 1.0 copy.140
  785.3 0.8 copy.145
  (86 shorter events, 13.7 us)
Async XLA Ops:
  7.2 15.8 %copy-start.6 = (bf16[2,4]{1,0:T(2,128)(2,1)S(1)}, bf16[2,4]{1,0:T(2,128)(2,1)}, u32[]{:S(2)}) copy-start(bf16[2,4]{1,0:T(2,128)(2,1)} %param.23) | copy-start | bytes 52
  7.2 15.8 %copy-start.8 = (bf16[64]{0:T(256)(128)(2,1)S(1)}, bf16[64]{0:T(256)(128)(2,1)}, u32[]{:S(2)}) copy-start(bf16[64]{0:T(256)(128)(2,1)} %param.22) | copy-start | bytes 388
  7.2 15.8 %copy-start.7 = (bf16[64]{0:T(256)(128)(2,1)S(1)}, bf16[64]{0:T(256)(128)(2,1)}, u32[]{:S(2)}) copy-start(bf16[64]{0:T(256)(128)(2,1)} %param.21) | copy-start | bytes 388
  7.2 16.5 %copy-start.1 = (bf16[64,2,2048]{2,1,0:T(2,128)(2,1)S(1)}, bf16[64,2,2048]{2,1,0:T(2,128)(2,1)}, u32[]{:S(2)}) copy-start(bf16[64,2,2048]{2,1,0:T(2,128)(2,1)} %param.16) | copy-start | bytes 1572868
  7.2 189.4 %all-gather.4.cloned.1.call-start = ((), (), s32[]{:S(2)}) async-start(), calls=%async_computation | async-start | bytes 8650752 | tf_op jit(solution)/shard_map/all_gather | solution.py:1231
  8.0 301.4 %all-gather.6.cloned.1.call-start = ((), (), s32[]{:S(2)}) async-start(), calls=%async_computation.1 | async-start | bytes 17301504 | tf_op jit(solution)/shard_map/all_gather | solution.py:1232
  16.9 125.6 %copy-start.5 = (s32[2,2,4,2]{3,2,1,0:T(4,128)S(1)}, s32[2,2,4,2]{3,2,1,0:T(4,128)}, u32[]{:S(2)}) copy-start(s32[2,2,4,2]{3,2,1,0:T(4,128)} %constant.66) | copy-start | bytes 388
  149.5 47.1 %copy-start.3 = (f32[2,64,2048]{2,1,0:T(8,128)S(1)}, f32[2,64,2048]{2,1,0:T(8,128)}, u32[]{:S(2)}) copy-start(f32[2,64,2048]{2,1,0:T(8,128)} %get-tuple-element.96) | copy-start | bytes 3145732
  201.5 371.8 %copy-start = (f32[128,2048]{1,0:T(8,128)}, f32[128,2048]{1,0:T(8,128)S(1)}, u32[]{:S(2)}) copy-start(f32[128,2048]{1,0:T(8,128)S(1)} %get-tuple-element.111) | copy-start | bytes 3145732
  577.2 7.0 slice-start
  578.5 5.6 slice-start.1
  651.1 117.0 %copy-start.2 = (bf16[64,2,2048]{2,1,0:T(2,128)(2,1)S(1)}, bf16[64,2,2048]{2,1,0:T(2,128)(2,1)}, u32[]{:S(2)}) copy-start(bf16[64,2,2048]{2,1,0:T(2,128)(2,1)} %param.16) | copy-start | bytes 1572868
  770.5 14.9 %copy-start.4 = (f32[2,32,2048]{2,1,0:T(8,128)S(1)}, f32[2,32,2048]{2,1,0:T(8,128)}, u32[]{:S(2)}) copy-start(f32[2,32,2048]{2,1,0:T(8,128)} %get-tuple-element.77) | copy-start | bytes 1572868
Sparse Core Ops, SparseCore 0:
  11.0 107.9 all-gather.3
  122.1 128.7 all-gather.5

commit v4 on v3

--- a/solution.py
+++ b/solution.py
@@ -107,8 +107,8 @@
 
 
 class Gather:
-    def __init__(self, p, src, out, send_sem, recv_sem, local_sem):
-        self.p, self.src, self.out = p, src, out
+    def __init__(self, p, src, out, send_sem, recv_sem, local_sem, like=(0, 1)):
+        self.p, self.src, self.out, self.like = p, src, out, like
         self.send_sem, self.recv_sem, self.local_sem = send_sem, recv_sem, local_sem
         self.steps = p.Z + 2
         self.started = []
@@ -184,20 +184,26 @@
                     self.arrive(cond, half, p.x, p.y, k, on + ("y", "x", "core"))
         if n <= p.Z:
             for cond, k, _ in self.zs(n - 1):
-                for j in p.others("y"):
-                    self.arrive(cond, 0, p.x, j, k, ("x", "core"))
-                for j in p.others("x"):
-                    self.arrive(cond, 1, j, p.y, k, ("y", "core"))
+                for half, way in enumerate(self.like):
+                    if way == 0:
+                        for i in p.others("y"):
+                            self.arrive(cond, half, p.x, i, k, ("x", "core"))
+                    else:
+                        for j in p.others("x"):
+                            self.arrive(cond, half, j, p.y, k, ("y", "core"))
         if n >= 2:
             for cond, k, _ in self.zs(n - 2):
-                for j in p.others("x"):
-                    self.arrive(cond, 0, j, p.y, k, ("core",))
-                for i in p.others("y"):
-                    self.arrive(cond, 1, p.x, i, k, ("core",))
-                for j in p.others("x"):
-                    for i in p.others("y"):
-                        self.arrive(cond, 0, j, i, k, ("core",))
-                        self.arrive(cond, 1, j, i, k, ("core",))
+                for half, way in enumerate(self.like):
+                    if way == 0:
+                        for j in p.others("x"):
+                            self.arrive(cond, half, j, p.y, k, ("core",))
+                    else:
+                        for i in p.others("y"):
+                            self.arrive(cond, half, p.x, i, k, ("core",))
+                for half in (0, 1):
+                    for j in p.others("x"):
+                        for i in p.others("y"):
+                            self.arrive(cond, half, j, i, k, ("core",))
 
     def end(self):
         p = self.p
@@ -322,24 +328,48 @@
     return [pl.BlockSpec(memory_space=pl.ANY)] * n
 
 
-def gather_kernel(U, B, src, out, *sems):
+def gather_kernel(U, B, experts, RB, src, val, gate, out, hot_out, rg_out, send, recv, local, hot, rg, store):
     p = Place(U, B)
     p.barrier("chain")
-    g = Gather(p, src, out, *sems)
+    g = Gather(p, src, out, send, recv, local)
+    G, _, KB = val.shape
+    per = -(-G // (g.steps - 2))
+    at = lax.broadcasted_iota(jnp.int32, (RB, KB), 0)
+    saves = [pltpu.make_async_copy(hot, hot_out, store.at[0]), pltpu.make_async_copy(rg, rg_out, store.at[1])]
     for n in range(g.steps):
         g.step(n)
+
+        @pl.loop(min(n * per, G), min((n + 1) * per, G))
+        def _(m):
+            for e in range(experts):
+                hit = at == val[m, e:e + 1, :]
+                hot[m, e * RB:(e + 1) * RB, :] = jnp.where(hit, 1.0, 0.0).astype(hot.dtype)
+                w = jnp.sum(jnp.where(hit, gate[m, e:e + 1, :], 0.0), axis=1, keepdims=True)
+                rg[e, pl.ds(pl.multiple_of(m * RB, RB), RB), :] = jnp.broadcast_to(w, (RB, 128))
+
+        if n == g.steps - 2:
+            for cp in saves:
+                cp.start()
     g.end()
-
-
-def gather_blocks(v, U, B, cid):
+    for cp in saves:
+        cp.wait()
+
+
+def gather_blocks(v, val, gate, RB, U, B, cid):
+    G, experts, KB = val.shape
+    sds = jax.ShapeDtypeStruct
+    vmem = pl.BlockSpec(memory_space=pltpu.VMEM)
+    hot, rg = sds((G, experts * RB, KB), jnp.bfloat16), sds((experts, G * RB, 128), jnp.float32)
     return pl.pallas_call(
-        functools.partial(gather_kernel, U, B),
-        out_shape=jax.ShapeDtypeStruct((U * B,) + v.shape, v.dtype),
-        in_specs=any_specs(1),
-        out_specs=any_specs(1)[0],
-        scratch_shapes=Gather.semaphores(U, B),
-        compiler_params=pltpu.CompilerParams(collective_id=cid, has_side_effects=True),
-    )(v)
+        functools.partial(gather_kernel, U, B, experts, RB),
+        out_shape=[sds((U * B,) + v.shape, v.dtype), hot, rg],
+        in_specs=any_specs(1) + [vmem, vmem],
+        out_specs=any_specs(3),
+        scratch_shapes=Gather.semaphores(U, B) + [
+            pltpu.VMEM(hot.shape, hot.dtype), pltpu.VMEM(rg.shape, rg.dtype), pltpu.SemaphoreType.DMA((2,))],
+        compiler_params=pltpu.CompilerParams(
+            collective_id=cid, has_side_effects=True, vmem_limit_bytes=32 * 2**20),
+    )(v, val, gate)
 
 
 def front_kernel(U, B, tok, small, weights, tok_out, small_out, weights_out, *sems):
@@ -413,8 +443,8 @@
 
 
 class Scatter:
-    def __init__(self, p, acc, rc, rx0, rx1, ry0, ry1, rz, fin, loc, cs, cr, xs, xr, ys, yr, zs, zr):
-        self.p = p
+    def __init__(self, p, acc, rc, rx0, rx1, ry0, ry1, rz, fin, loc, cs, cr, xs, xr, ys, yr, zs, zr, like=(0, 1)):
+        self.p, self.like = p, like
         self.acc, self.rc, self.rx, self.ry, self.rz, self.fin = acc, rc, (rx0, rx1), (ry0, ry1), rz, fin
         self.loc, self.cs, self.cr = loc, cs, cr
         self.xs, self.xr, self.ys, self.yr, self.zs, self.zr = xs, xr, ys, yr, zs, zr
@@ -424,7 +454,7 @@
         self.local = True
 
     @staticmethod
-    def scratch(U, B, rows, D, t):
+    def scratch(U, B, rows, D, t, like=(0, 1)):
         X, Y, Z, Q = U // 2, 2, B // 2, U * B // 2
         dma = pltpu.SemaphoreType.DMA
         x, y = max(X - 1, 1), Y - 1
@@ -432,9 +462,9 @@
             pltpu.VMEM((Q, 2, rows, D), t),
             pltpu.VMEM((Q, 2, rows, D), t),
             pltpu.VMEM((x, Z * Y, rows, D), t),
-            pltpu.VMEM((x, Z, rows, D), t),
+            pltpu.VMEM((x, Z if like[1] else Z * Y, rows, D), t),
             pltpu.VMEM((y, Z, rows, D), t),
-            pltpu.VMEM((y, Z * X, rows, D), t),
+            pltpu.VMEM((y, Z * X if like[1] else Z, rows, D), t),
             pltpu.VMEM((2, Z, rows, D), t),
             pltpu.VMEM((2, rows, D), jnp.float32),
             dma((Q, 2)),
@@ -525,34 +555,44 @@
     def first(self, n, j):
         p = self.p
         k = self.order[n]
-        if j is not p.x:
-            for i in range(p.Y):
-                q = p.chip(j, i, k)
-                add(self.acc.at[q, 0], self.ready(0, j, i, k))
-                self.send_x(0, q, j, k * p.Y + i)
-        for i in p.others("y"):
-            q = p.chip(j, i, k)
-            add(self.acc.at[q, 1], self.ready(1, j, i, k))
-            self.send_y(1, q, i, k * p.X + j)
+        for h, way in enumerate(self.like):
+            if way == 0 and j is not p.x:
+                for i in range(p.Y):
+                    q = p.chip(j, i, k)
+                    add(self.acc.at[q, h], self.ready(h, j, i, k))
+                    self.send_x(h, q, j, k * p.Y + i)
+            if way == 1:
+                for i in p.others("y"):
+                    q = p.chip(j, i, k)
+                    add(self.acc.at[q, h], self.ready(h, j, i, k))
+                    self.send_y(h, q, i, k * p.X + j)
 
     def rest(self, n):
         p = self.p
         X, Y, Z = p.X, p.Y, p.Z
         if 1 <= n <= Z:
             k = self.order[n - 1]
-            for i in p.others("y"):
-                q = p.chip(p.x, i, k)
-                add(self.acc.at[q, 0], self.ready(0, p.x, i, k) + self.from_x(0, k * Y + i))
-                self.send_y(0, q, i, k)
-            for j in p.others("x"):
-                q = p.chip(j, p.y, k)
-                add(self.acc.at[q, 1], self.ready(1, j, p.y, k) + self.from_y(1, k * X + j))
-                self.send_x(1, q, j, k)
+            for h, way in enumerate(self.like):
+                if way == 0:
+                    for i in p.others("y"):
+                        q = p.chip(p.x, i, k)
+                        add(self.acc.at[q, h], self.ready(h, p.x, i, k) + self.from_x(h, k * Y + i))
+                        self.send_y(h, q, i, k)
+                else:
+                    for j in p.others("x"):
+                        q = p.chip(j, p.y, k)
+                        add(self.acc.at[q, h], self.ready(h, j, p.y, k) + self.from_y(h, k * X + j))
+                        self.send_x(h, q, j, k)
         if n >= 2:
             k = self.order[n - 2]
             q = p.chip(p.x, p.y, k)
-            self.last(n - 2, 0, q, self.ready(0, p.x, p.y, k) + self.from_x(0, k * Y + p.y) + self.from_y(0, k))
-            self.last(n - 2, 1, q, self.ready(1, p.x, p.y, k) + self.from_y(1, k * X + p.x) + self.from_x(1, k))
+            for h, way in enumerate(self.like):
+                extra = self.ready(h, p.x, p.y, k)
+                if way == 0:
+                    extra = extra + self.from_x(h, k * Y + p.y) + self.from_y(h, k)
+                else:
+                    extra = extra + self.from_y(h, k * X + p.x) + self.from_x(h, k)
+                self.last(n - 2, h, q, extra)
 
     def step(self, n):
         if n < self.p.Z:
@@ -822,7 +862,7 @@
     at = PlaneScatter.SCRATCH
     work = [PlaneScatter(p, *scratch[:at])]
     if more:
-        work.append(Scatter(p, *scratch[at:at + Scatter.SCRATCH]))
+        work.append(Scatter(p, *scratch[at:at + Scatter.SCRATCH], like=(0, 0)))
         at += Scatter.SCRATCH
     ex = []
     for i in range(2):
@@ -878,7 +918,7 @@
         if o is not None:
             args.append(o)
             shapes.append(sds(o.shape[1:], f32))
-            scratch += Scatter.scratch(U, B, o.shape[2], o.shape[3], o.dtype)
+            scratch += Scatter.scratch(U, B, o.shape[2], o.shape[3], o.dtype, (0, 0))
         for m in (weights, small):
             scratch += PairExchange.scratch(U, B, m.shape[1], m.shape[2], m.dtype)
         return pl.pallas_call(
@@ -939,30 +979,58 @@
     return lax.dot_general(a, b, (((ca,), (cb,)), ((), ())), preferred_element_type=jnp.float32)
 
 
-def attend_kernel(scale, q_ref, k_ref, vt_ref, o_ref, lse_ref):
-    s = dot(k_ref[...], q_ref[...], 1, 1) * scale
-    top = jnp.max(s, axis=0, keepdims=True)
-    e = jnp.exp(s - top)
-    total = jnp.sum(e, axis=0, keepdims=True)
-    o = dot(vt_ref[...], e.astype(jnp.bfloat16), 1, 0) / total
-    o_ref[...] = o.T.astype(o_ref.dtype)
-    lse_ref[...] = top + jnp.log(total)
-
-
-def attend(q, k, vt):
+def attend_kernel(U, B, bq, scale, q_ref, k_ref, vt_ref, out_ref, lse_ref, rows_ref, send, recv):
+    p = Place(U, B)
+    p.barrier("every")
+    per = bq // rows_ref.shape[1]
+    n = q_ref.shape[0] // bq
+
+    def away(f):
+        return remote(rows_ref.at[f], out_ref.at[p.me], send.at[f], recv.at[p.me], p.flat_dev(f))
+
+    @pl.loop(0, n)
+    def _(t):
+        i = lax.rem(t + lax.div(p.me, per), n)
+        rows = pl.ds(pl.multiple_of(i * bq, bq), bq)
+        s = dot(k_ref[...], q_ref[rows, :], 1, 1) * scale
+        top = jnp.max(s, axis=0, keepdims=True)
+        e = jnp.exp(s - top)
+        total = jnp.sum(e, axis=0, keepdims=True)
+        o = dot(vt_ref[...], e.astype(jnp.bfloat16), 1, 0) / total
+        lse_ref[:, rows] = top + jnp.log(total)
+        rows_ref[pl.ds(i * per, per)] = o.T.astype(rows_ref.dtype).reshape((per,) + rows_ref.shape[1:])
+        for d in range(per):
+            f = i * per + d
+
+            @pl.when(f != p.me)
+            def _():
+                away(f).start()
+
+    cp = pltpu.make_async_copy(rows_ref.at[p.me], out_ref.at[p.me], recv.at[p.me])
+    cp.start()
+    cp.wait()
+
+    @pl.loop(1, p.F)
+    def _(o):
+        f = lax.rem(p.me + o, p.F)
+        remote(out_ref.at[f], out_ref.at[f], send.at[f], recv.at[f], p.flat_dev(f)).wait_recv()
+        away(f).wait_send()
+
+
+def attend(q, k, vt, positions, U, B, cid):
     n = q.shape[0]
+    F = U * B
     bq = 256 if n <= 2048 else 128
+    vmem = pl.BlockSpec(memory_space=pltpu.VMEM)
+    dma = pltpu.SemaphoreType.DMA
     return pl.pallas_call(
-        functools.partial(attend_kernel, 1.0 / math.sqrt(HD)),
-        grid=(n // bq,),
-        in_specs=[
-            pl.BlockSpec((bq, HD), lambda i: (i, 0)),
-            pl.BlockSpec((n, HD), lambda i: (0, 0)),
-            pl.BlockSpec((HD, n), lambda i: (0, 0)),
-        ],
-        out_specs=[pl.BlockSpec((bq, HD), lambda i: (i, 0)), pl.BlockSpec((1, bq), lambda i: (0, i))],
-        out_shape=[jax.ShapeDtypeStruct((n, HD), jnp.bfloat16), jax.ShapeDtypeStruct((1, n), jnp.float32)],
-        compiler_params=pltpu.CompilerParams(vmem_limit_bytes=58 * 2**20),
+        functools.partial(attend_kernel, U, B, bq, 1.0 / math.sqrt(HD)),
+        in_specs=[vmem] * 3,
+        out_specs=any_specs(1) + [vmem],
+        out_shape=[jax.ShapeDtypeStruct((F, positions, HD), jnp.bfloat16), jax.ShapeDtypeStruct((1, n), jnp.float32)],
+        scratch_shapes=[pltpu.VMEM((F, positions, HD), jnp.bfloat16), dma((F,)), dma((F,))],
+        compiler_params=pltpu.CompilerParams(
+            collective_id=cid, has_side_effects=True, vmem_limit_bytes=40 * 2**20),
     )(q, k, vt)
 
 
@@ -1044,7 +1112,7 @@
 
 
 def head_back_kernel(dq_ref, dk_ref, dv_ref, rq_ref, rk_ref, cos_ref, sin_ref, qk_ref, tok_ref, gain_ref, w_ref,
-                     part_ref, dw_ref, dg_ref, da_ref):
+                     part_ref, dwout_ref, dg_ref, da_ref, dw_ref):
     f32, bf16 = jnp.float32, jnp.bfloat16
 
     @pl.when(pl.program_id(0) == 0)
@@ -1075,6 +1143,10 @@
         da_ref[0:1, n:n + cut] += jnp.sum(part * norm[:, n:n + cut], axis=0, keepdims=True)
         dw_ref[n:n + cut, :] += dot(hidden[:, n:n + cut], grad, 0, 0)
 
+    @pl.when(pl.program_id(0) == pl.num_programs(0) - 1)
+    def _():
+        dwout_ref[...] = dw_ref[...].astype(bf16)
+
 
 def head_back(dq, dk, dv, rq, rk, cosine, sine, qk, tok, gain, w):
     n, D = tok.shape
@@ -1091,31 +1163,26 @@
         out_specs=[
             pl.BlockSpec((bm, D), row), pl.BlockSpec((D, 3 * HD), whole), pl.BlockSpec((8, HD), whole),
             pl.BlockSpec((8, D), whole)],
-        out_shape=[sds((n, D), jnp.bfloat16), sds((D, 3 * HD), jnp.float32), sds((8, HD), jnp.float32),
+        out_shape=[sds((n, D), jnp.bfloat16), sds((D, 3 * HD), jnp.bfloat16), sds((8, HD), jnp.float32),
                    sds((8, D), jnp.float32)],
+        scratch_shapes=[pltpu.VMEM((D, 3 * HD), jnp.float32)],
         compiler_params=pltpu.CompilerParams(vmem_limit_bytes=58 * 2**20),
     )(dq, dk, dv, rq, rk, cosine, sine, qk, tok, gain, w)
 
 
-def dispatch_kernel(val_ref, gate_ref, norm_ref, cot_ref, x_ref, pg_ref, hot_ref, rg_ref, rg_s):
-    f32, bf16 = jnp.float32, jnp.bfloat16
-    experts, KB = val_ref.shape[1:]
-    RB, D = x_ref.shape[1:]
-    at = lax.broadcasted_iota(jnp.int32, (RB, KB), 0)
-    for e in range(experts):
-        hit = at == val_ref[0, e:e + 1, :]
-        hot_ref[0, e * RB:(e + 1) * RB, :] = jnp.where(hit, 1.0, 0.0).astype(bf16)
-        weight = jnp.sum(jnp.where(hit, gate_ref[0, e:e + 1, :], 0.0), axis=1, keepdims=True)
-        rg_s[e * RB:(e + 1) * RB, :] = weight
-        rg_ref[e] = jnp.broadcast_to(weight, (RB, rg_ref.shape[2]))
+def dispatch_kernel(hot_ref, rg_ref, norm_ref, cot_ref, x_ref, pg_ref):
+    bf16 = jnp.bfloat16
+    experts, RB, D = x_ref.shape
+    hot = hot_ref[0]
+    KB = hot.shape[1]
+    weight = rg_ref[:, :, 0:1].reshape(experts * RB, 1)
     cut = min(D, 512)
-    hot = hot_ref[0]
     norm = norm_ref[...].reshape(KB, D)
     cot = cot_ref[...].reshape(KB, D)
     for n in range(0, D, cut):
         x = dot(hot, norm[:, n:n + cut], 1, 0).astype(bf16)
         x_ref[:, :, n:n + cut] = x.reshape(experts, RB, cut)
-        g = (dot(hot, cot[:, n:n + cut], 1, 0) * rg_s[...]).astype(bf16)
+        g = (dot(hot, cot[:, n:n + cut], 1, 0) * weight).astype(bf16)
         pg_ref[:, :, n:n + cut] = g.reshape(experts, RB, cut)
 
 
@@ -1124,23 +1191,20 @@
     return pl.BlockSpec((1, two, 1, Y, T, D), lambda g: (g // Z, 0, g % Z, 0, 0, 0))
 
 
-def dispatch(val, gate, normed, cot, RB):
-    G, experts, KB = val.shape
-    D, Z = normed.shape[-1], normed.shape[2]
-    one = pl.BlockSpec((1, experts, KB), lambda g: (g, 0, 0))
+def dispatch(hot, rg, normed, cot):
+    G, rows, KB = hot.shape
+    experts, D, Z = rg.shape[0], normed.shape[-1], normed.shape[2]
+    RB = rows // experts
     out = pl.BlockSpec((experts, RB, D), lambda g: (0, g, 0))
-    sds = jax.ShapeDtypeStruct
     return pl.pallas_call(
         dispatch_kernel,
         grid=(G,),
-        in_specs=[one, one, group_spec(normed.shape, Z), group_spec(cot.shape, Z)],
-        out_specs=[out, out, pl.BlockSpec((1, experts * RB, KB), lambda g: (g, 0, 0)),
-                   pl.BlockSpec((experts, RB, 128), lambda g: (0, g, 0))],
-        out_shape=[sds((experts, G * RB, D), jnp.bfloat16)] * 2 + [
-            sds((G, experts * RB, KB), jnp.bfloat16), sds((experts, G * RB, 128), jnp.float32)],
-        scratch_shapes=[pltpu.VMEM((experts * RB, 1), jnp.float32)],
+        in_specs=[pl.BlockSpec((1, rows, KB), lambda g: (g, 0, 0)), pl.BlockSpec((experts, RB, 128), lambda g: (0, g, 0)),
+                  group_spec(normed.shape, Z), group_spec(cot.shape, Z)],
+        out_specs=[out, out],
+        out_shape=[jax.ShapeDtypeStruct((experts, G * RB, D), jnp.bfloat16)] * 2,
         compiler_params=pltpu.CompilerParams(vmem_limit_bytes=58 * 2**20),
-    )(val, gate, normed, cot)
+    )(hot, rg, normed, cot)
 
 
 def expert_kernel(x_ref, pg_ref, rg_ref, wg_ref, wu_ref, wd_ref, y_ref, dx_ref, dwg_ref, dwu_ref, dwd_ref):
@@ -1187,6 +1251,34 @@
         out_shape=[sds(x.shape, x.dtype)] * 2 + [sds(a.shape, jnp.float32) for a in (wg, wu, wd)],
         compiler_params=pltpu.CompilerParams(vmem_limit_bytes=60 * 2**20),
     )(x, pg, rg, wg, wu, wd)
+
+
+def close_kernel(x_ref, w_ref, own_ref, other_ref, back_ref, tok_ref, gain_ref, q_ref, k_ref, v_ref, in_ref):
+    f32 = jnp.float32
+    for h in range(w_ref.shape[0]):
+        for n, ref in enumerate((q_ref, k_ref, v_ref)):
+            ref[:, h * HD:(h + 1) * HD] = w_ref[h, :, n * HD:(n + 1) * HD].astype(f32)
+    here = x_ref[0]
+    for s in (0, 1):
+        grad = jnp.where(here == s, own_ref[...], other_ref[...].astype(f32))
+        tok = tok_ref[s].astype(f32)
+        inv = lax.rsqrt(jnp.mean(tok * tok, axis=-1, keepdims=True) + EPSILON)
+        norm = tok * inv
+        m = grad * gain_ref[...]
+        in_ref[s] = back_ref[s] + inv * (m - norm * jnp.mean(m * norm, axis=-1, keepdims=True))
+
+
+def close(here, weight_grad, own, other, back, tok, gain):
+    heads, W, _ = weight_grad.shape
+    vmem = pl.BlockSpec(memory_space=pltpu.VMEM)
+    sds = jax.ShapeDtypeStruct
+    return pl.pallas_call(
+        close_kernel,
+        in_specs=[pl.BlockSpec(memory_space=pltpu.SMEM)] + [vmem] * 6,
+        out_specs=[vmem] * 4,
+        out_shape=[sds((W, heads * HD), jnp.float32)] * 3 + [sds(tok.shape, jnp.float32)],
+        compiler_params=pltpu.CompilerParams(vmem_limit_bytes=32 * 2**20),
+    )(here, weight_grad, own, other, back, tok, gain)
 
 
 def body(tokens, w_query, w_key, w_value, w_out, attn_gain, ffn_gain, qk_gain,
@@ -1256,14 +1348,12 @@
 
     val, gate_of = by_group(val), by_group(gate_of)
 
-    half = HD // 2
-    inverse = ROPE_BASE ** (-2.0 * jnp.arange(half).astype(f32) / HD)
-    angles = jnp.arange(L).astype(f32)[:, None] * inverse[None, :]
-    cosine = jnp.concatenate([jnp.cos(angles)] * 2, axis=1)
-    sine = jnp.concatenate([-jnp.sin(angles), jnp.sin(angles)], axis=1)
+    inverse = (ROPE_BASE ** (-2.0 * np.arange(HD // 2) / HD)).astype(np.float32)
+    angles = np.arange(L).astype(np.float32)[:, None] * inverse[None, :]
+    cosine = jnp.asarray(np.concatenate([np.cos(angles)] * 2, axis=1).astype(np.float32))
+    sine = jnp.asarray(np.concatenate([-np.sin(angles), np.sin(angles)], axis=1).astype(np.float32))
     q, k, v, kt, vt, raw_q, raw_k = project(seq_tok, attn_g, head_w, qk_g, cosine, sine)
-    att, lse = attend(q, k, vt)
-    att_rows = exchange(att.reshape(F, positions, HD), U, B, 6)
+    att_rows, lse = attend(q, k, vt, positions, U, B, 5)
 
     def from_heads(m):
         m = m.reshape(2, 2 * B, positions, HD).transpose(0, 2, 1, 3)
@@ -1274,9 +1364,9 @@
     normed_full, ffn_back = jax.vjp(rms_norm, residual, ffn_g)
     normed = normed_full.astype(bf16).reshape(2, positions, D)
 
-    normed_all = gather_blocks(normed, U, B, 2)
+    normed_all, hot, row_gate = gather_blocks(normed, val, gate_of, RB, U, B, 2)
     shape = groups + (T, D)
-    x, pair_grad, hot, row_gate = dispatch(val, gate_of, normed_all.reshape(shape), cot_all.reshape(shape), RB)
+    x, pair_grad = dispatch(hot, row_gate, normed_all.reshape(shape), cot_all.reshape(shape))
     y, dx, gate_grad, up_grad, down_grad = expert_layer(x, pair_grad, row_gate, expert_gate, expert_up, expert_down)
     normed_grad, mixed_sum = scatter_pair(dx, y, hot, positions, U, B, 3)
     mixed = (residual + mixed_sum.reshape(T, D)).reshape(2, positions, D).transpose(1, 0, 2).astype(bf16)
@@ -1296,25 +1386,20 @@
         dq, dk, dv = (jnp.where(first_copy, m, 0.0) for m in (dq, dk, dv))
     hidden_part, weight_part, qk_part, attn_gain_part = head_back(
         dq, dk, dv, raw_q, raw_k, cosine, sine, qk_g, seq_tok, attn_g, head_w)
-    weight_part = weight_part.astype(bf16).reshape(F, W, 3 * HD)
+    weight_part = weight_part.reshape(F, W, 3 * HD)
     small = jnp.concatenate(
         [attn_gain_part[0].reshape(F, W), ffn_gain_part.reshape(F, W),
          qk_part[0].reshape(F, nq), qk_part[1].reshape(F, nq)], axis=1)
     small = jnp.pad(small, ((0, 0), (0, -small.shape[1] % 1024))).reshape(F, -1, 128)
     weight_grad, small, own, other, out_grad = finish(
         weight_part, small, hidden_part.reshape(F, positions, D), out_part, U, B, 4)
-    other = other.astype(f32)
-    hidden_grad = jnp.where(x_here == 0, jnp.stack([own, other]), jnp.stack([other, own]))
     small = jnp.sum(small, axis=0).reshape(-1)
-    weight_grad = weight_grad.reshape(H, R, W, 3 * HD).astype(f32).sum(axis=1)
-    weight_grad = weight_grad.transpose(1, 0, 2).reshape(W, H, 3, HD)
-    query_grad, key_grad, value_grad = (weight_grad[:, :, n].reshape(W, H * HD) for n in range(3))
-    hidden_grad, out_grad = hidden_grad.reshape(T, D), out_grad.reshape(W, D)
-    inv = lax.rsqrt(jnp.mean(rows_f * rows_f, axis=-1, keepdims=True) + EPSILON)
-    norm = rows_f * inv
-    m = hidden_grad * attn_g
-    token_grad = inv * (m - norm * jnp.mean(m * norm, axis=-1, keepdims=True))
-    input_grad = (residual_grad + token_grad).reshape(2, positions, D).transpose(1, 0, 2)
+    if R > 1:
+        weight_grad = weight_grad.reshape(H, R, W, 3 * HD).astype(f32).sum(axis=1)
+    query_grad, key_grad, value_grad, input_grad = close(
+        x_here.reshape(1), weight_grad, own, other, residual_grad.reshape(2, positions, D), tok, attn_g)
+    input_grad = input_grad.transpose(1, 0, 2)
+    out_grad = out_grad.reshape(W, D)
     return (
         mixed, input_grad, query_grad, key_grad, value_grad, out_grad,
         small[:W], small[W:2 * W], small[2 * W:2 * W + 2 * nq].reshape(2, nq),

time: 798 us -> 782 us (0.980)
  other arithmetic: 26.4 us -> 10.5 us
    pallas_call x3 -> x4, Pallas kernels: 156 us -> 178 us  [the longest x1 109 us: gather_blocks(): pl.pallas_call(functools.partial(gather_kernel, U, B, experts, RB), out_s...]
    pallas_call x2 -> x1, Pallas kernels: 38.7 us -> 17.1 us  [exchange(): pl.pallas_call(functools.partial(exchange_kernel, U, B), out_shape=jax.Sh...]
    unnamed x36 -> x55, local copies, waits for them, and re-layouts: 11.4 us -> 22.5 us
  transfers between devices with their start and end apart: 2 -> 2, of which waited for: 0 -> 0; matrix products, arithmetic and copies ran while one was open for 5% -> 3% of each run, Pallas kernels for 33% -> 34%
where the time goes in v4:
time: 782 us; the launch traced here: 777 us
  Pallas kernels  701 us (90%)
  local copies, waits for them, and re-layouts  36 us (5%)
  between operations  14.9 us (2%)
  matrix products  13.4 us (2%)
  other arithmetic  10.5 us (1%)
    pallas_call x1, Pallas kernels, call(): pl.pallas_call(functools.partial(pair_kernel, U, B, pl.ds(c * D, D)), out...  159 us
    pallas_call x1, Pallas kernels, call(): pl.pallas_call(functools.partial(finish_kernel, U, B, o is not None), out...  114 us
    pallas_call x1, Pallas kernels, front(): pl.pallas_call(functools.partial(front_kernel, U, B), out_shape=[jax.Shap...  112 us
    pallas_call x1, Pallas kernels, gather_blocks(): pl.pallas_call(functools.partial(gather_kernel, U, B, experts, RB), out_s...  109 us
    pallas_call x1, Pallas kernels, expert_layer(): pl.pallas_call(expert_kernel, grid=(x.shape[0], rows // step), in_specs=[...  70.7 us
    pallas_call x1, Pallas kernels, dispatch(): pl.pallas_call(dispatch_kernel, grid=(G,), in_specs=[pl.BlockSpec((1, row...  36.3 us
    pallas_call x1, Pallas kernels, attend(): pl.pallas_call(functools.partial(attend_kernel, U, B, bq, 1.0 / math.sqrt...  31.2 us
    unnamed x55, local copies, waits for them, and re-layouts  22.5 us
  transfers between devices with their start and end apart: 2, of which 0 were waited for; matrix products, arithmetic and copies ran while one was open for 3% of the time, Pallas kernels for 34%

profile of v4, /device:TPU:0, one launch (start us, length us, event | category | flops | bytes accessed | tf_op | source)
XLA Modules:
  0.0 776.9 jit_solution(15548254097707555827)
XLA Ops:
  7.3 0.7 all-gather.4.cloned.1.call-update
  8.0 2.0 copy.122
  10.5 1.3 reduce.15
  12.1 0.8 copy.77
  13.0 0.8 copy.79
  13.9 1.0 copy.96
  15.4 1.0 copy.97
  17.0 1.0 copy.98
  18.5 1.8 maximum_bitcast_fusion
  20.3 1.8 reshape.167.weights
  22.0 1.0 copy.121
  23.0 1.0 convert_reduce_fusion
  24.2 0.6 pad_bitcast_fusion.small
  24.8 111.5 %shard_map.265 = (bf16[32,64,2048]{2,1,0:T(8,128)(2,1)}, f32[32,24,128]{2,1,0:T(8,128)}, bf16[32,64,384]{2,1,0:T(8,128)(2,1)}) custom-call(bf16[2,64,2048]{2,1,0:T(8,128)(2,1)} %bitcast.106, f32[24,128]{1,0:T(8,128)} %pad_bitcast_fusion.small, bf16[16,64,384]{2,1,0:T(8,128)(2,1)} %reshape.167.weights), custom_call_target="tpu_custom_call" | custom-call | tf_op jit(solution)/shard_map/pallas_call | solution.py:397
  136.3 1.1 copy.120
  137.8 0.7 reshape.170.gain_ref
  140.8 13.1 %shard_map.266 = (bf16[2048,128]{1,0:T(8,128)(2,1)}, bf16[2048,128]{1,0:T(8,128)(2,1)}, bf16[2048,128]{1,0:T(8,128)(2,1)}, bf16[128,2048]{1,0:T(8,128)(2,1)}, bf...) custom-call(bf16[2048,2048]{1,0:T(8,128)(2,1)} %bitcast.117, f32[1,2048]{1,0:T(1,128)} %reshape.170.gain_ref, ...), custom_call_target="tpu_custom_call" | custom-call | tf_op jit(solution)/shard_map/pallas_call | solution.py:1101
  153.9 1.0 copy-done.3
  155.0 1.1 copy-done.4
  156.1 1.0 copy-done.6
  157.1 31.2 %shard_map.267 = (bf16[32,64,128]{2,1,0:T(8,128)(2,1)S(1)}, f32[1,2048]{1,0:T(1,128)S(1)}) custom-call(bf16[2048,128]{1,0:T(8,128)(2,1)S(1)} %copy-done.3, bf16[2048,128]{1,0:T(8,128)(2,1)S(1)} %copy-done.4, bf16[128,2048]{1,0:T(8,128)(2,1)S(1)} %copy-done.6), custom_call_target="tpu_custom_call" | custom-call | tf_op jit(solution)/shard_map/pallas_call | solution.py:1026
  188.8 4.9 multiply_reduce_fusion.1
  193.9 108.5 %shard_map.268 = (bf16[32,2,64,2048]{3,2,1,0:T(8,128)(2,1)}, bf16[8,640,512]{2,1,0:T(8,128)(2,1)S(1)}, f32[8,640,128]{2,1,0:T(8,128)S(1)}) custom-call(bf16[2,64,2048]{2,1,0:T(8,128)(2,1)S(1)} %bitcast.109, s32[8,8,512]{2,1,0:T(8,128)S(1)} %bitcast.113, f32[8,8,512]{2,1,0:T(8,128)S(1)} %bitcast.112), custom_call_target="tpu_custom_call" | custom-call | tf_op jit(solution)/shard_map/pallas_call | solution.py:363
  302.5 2.3 copy-done
  304.8 1.5 copy-done.1
  306.3 36.3 %shard_map.269 = (bf16[8,640,2048]{2,1,0:T(8,128)(2,1)}, bf16[8,640,2048]{2,1,0:T(8,128)(2,1)}) custom-call(bf16[8,640,512]{2,1,0:T(8,128)(2,1)} %copy-done, f32[8,640,128]{2,1,0:T(8,128)} %copy-done.1, bf16[2,2,4,2,128,2048]{5,4,3,2,1,0:T(8,128)(2,1)} %bitcast.120, bf16[2,2,4,2,128,2048]{5,4,3,2,1,0:T(8,128)(2,1)} %bitcast.119), custom_call_target="tpu_custom_call" | custom-call | tf_op jit(solution)/shard_map/pallas_call | solution.py:1199
  342.6 70.7 %shard_map.270 = (bf16[8,640,2048]{2,1,0:T(8,128)(2,1)}, bf16[8,640,2048]{2,1,0:T(8,128)(2,1)}, f32[8,2048,256]{2,1,0:T(8,128)}, f32[8,2048,256]{2,1,0:T(8,128)}, f32[8,256,2048]{2,1,0:T(8,128)}) custom-call(bf16[8,640,2048]{2,1,0:T(8,128)(2,1)} %get-tuple-element.62.x_ref, bf16[8,640,2048]{2,1,0:T(8,128)(2,1)} %get-tuple-element.63.pg_ref, ...), custom_call_target="tpu_custom_call" | custom-call | tf_op jit(solution)/shard_map/pallas_call | solution.py:1246
  413.4 158.9 %shard_map.271 = (f32[2,64,2048]{2,1,0:T(8,128)}, f32[2,64,2048]{2,1,0:T(8,128)}) custom-call(bf16[8,640,2048]{2,1,0:T(8,128)(2,1)} %get-tuple-element.64.a, bf16[8,640,2048]{2,1,0:T(8,128)(2,1)} %get-tuple-element.65.b, bf16[8,640,512]{2,1,0:T(8,128)(2,1)} %copy-done), custom_call_target="tpu_custom_call" | custom-call | tf_op jit(solution)/shard_map/pallas_call | solution.py:782
  572.3 1.5 fusion.4
  573.8 2.4 fusion.1
  576.2 1.3 copy.119
  577.6 5.6 convolution_convert_fusion
  583.2 2.9 fusion
  586.2 0.9 copy.92
  587.2 17.1 %shard_map.272 = bf16[32,64,128]{2,1,0:T(8,128)(2,1)} custom-call(bf16[32,64,128]{2,1,0:T(8,128)(2,1)} %bitcast.131), custom_call_target="tpu_custom_call" | custom-call | tf_op jit(solution)/shard_map/pallas_call | solution.py:435
  604.3 17.6 %shard_map.273 = (f32[2048,128]{1,0:T(8,128)}, f32[2048,128]{1,0:T(8,128)}, f32[2048,128]{1,0:T(8,128)}) custom-call(bf16[2048,128]{1,0:T(8,128)(2,1)} %get-tuple-element.55.q_ref, bf16[2048,128]{1,0:T(8,128)(2,1)} %bitcast.127, f32[1,2048]{1,0:T(1,128)} %copy-done.10, bf16[2048,128]{1,0:T(8,128)(2,1)} %get-tuple-element.56.k_ref, ...), custom_call_target="tpu_custom_call" | custom-call | tf_op jit(solution)/shard_map/pallas_call | solution.py:1058
  622.0 20.5 %shard_map.274 = (bf16[2048,2048]{1,0:T(8,128)(2,1)}, bf16[2048,384]{1,0:T(8,128)(2,1)}, f32[8,128]{1,0:T(8,128)}, f32[8,2048]{1,0:T(8,128)}) custom-call(f32[2048,128]{1,0:T(8,128)} %get-tuple-element.71.dq_ref, f32[2048,128]{1,0:T(8,128)} %get-tuple-element.72.dk_ref, f32[2048,128]{1,0:T(8,128)} %get-tuple-element.73.dv_ref, ...), custom_call_target="tpu_custom_call" | custom-call | tf_op jit(solution)/shard_map/pallas_call | solution.py:1157
  642.5 0.8 slice_reduce_fusion.2
  643.3 0.9 slice_reduce_fusion
  644.5 0.7 copy.102
  645.2 114.2 %shard_map.275 = (bf16[16,64,384]{2,1,0:T(8,128)(2,1)}, f32[16,8,128]{2,1,0:T(8,128)}, f32[64,2048]{1,0:T(8,128)}, bf16[64,2048]{1,0:T(8,128)(2,1)}, f32[2,32,2048]{2,1,0:T(8,128)}) custom-call(bf16[2,16,64,384]{3,2,1,0:T(8,128)(2,1)} %bitcast.132, f32[2,16,8,128]{3,2,1,0:T(8,128)} %bitcast.139, bf16[32,64,2048]{2,1,0:T(8,128)(2,1)} %bitcast.123, ...), custom_call_target="tpu_custom_call" | custom-call | tf_op jit(solution)/shard_map/pallas_call | solution.py:924
  759.4 1.1 copy-done.5
  760.5 1.0 copy-done.7
  761.6 0.9 copy-done.8
  762.5 1.5 shard_map.276
  764.0 1.8 copy.93
  765.8 0.9 reduce_sum.73
  767.9 1.9 copy.124
  (85 shorter events, 7.7 us)
Async XLA Ops:
  7.2 14.9 %copy-start.14 = (bf16[64,2,2048]{2,1,0:T(2,128)(2,1)S(1)}, bf16[64,2,2048]{2,1,0:T(2,128)(2,1)}, u32[]{:S(2)}) copy-start(bf16[64,2,2048]{2,1,0:T(2,128)(2,1)} %param.18) | copy-start | bytes 1572868
  7.2 16.8 %copy-start.16 = (bf16[2,4]{1,0:T(2,128)(2,1)S(1)}, bf16[2,4]{1,0:T(2,128)(2,1)}, u32[]{:S(2)}) copy-start(bf16[2,4]{1,0:T(2,128)(2,1)} %param.25) | copy-start | bytes 52
  7.2 16.9 %copy-start.18 = (bf16[64]{0:T(256)(128)(2,1)S(1)}, bf16[64]{0:T(256)(128)(2,1)}, u32[]{:S(2)}) copy-start(bf16[64]{0:T(256)(128)(2,1)} %param.24) | copy-start | bytes 388
  7.2 16.9 %copy-start.17 = (bf16[64]{0:T(256)(128)(2,1)S(1)}, bf16[64]{0:T(256)(128)(2,1)}, u32[]{:S(2)}) copy-start(bf16[64]{0:T(256)(128)(2,1)} %param.23) | copy-start | bytes 388
  7.2 181.6 %all-gather.4.cloned.1.call-start = ((), (), s32[]{:S(2)}) async-start(), calls=%async_computation | async-start | bytes 8650752 | tf_op jit(solution)/shard_map/all_gather | solution.py:1323
  8.0 298.4 %all-gather.6.cloned.1.call-start = ((), (), s32[]{:S(2)}) async-start(), calls=%async_computation.1 | async-start | bytes 17301504 | tf_op jit(solution)/shard_map/all_gather | solution.py:1324
  14.9 125.2 %copy-start.15 = (s32[2,2,4,2]{3,2,1,0:T(4,128)S(1)}, s32[2,2,4,2]{3,2,1,0:T(4,128)}, u32[]{:S(2)}) copy-start(s32[2,2,4,2]{3,2,1,0:T(4,128)} %constant.63) | copy-start | bytes 388
  139.4 49.4 %copy-start.2 = (bf16[64,2,2048]{2,0,1:T(8,128)(2,1)S(1)}, bf16[64,2,2048]{2,0,1:T(8,128)(2,1)}, u32[]{:S(2)}) copy-start(bf16[64,2,2048]{2,0,1:T(8,128)(2,1)} %copy.121) | copy-start | bytes 1572868
  153.9 1.0 copy-start.3
  155.0 1.1 copy-start.4
  156.1 1.0 copy-start.6
  188.4 5.3 copy-start.10
  188.7 5.2 copy-start.12
  193.7 378.6 %copy-start.11 = (f32[128,2048]{1,0:T(8,128)}, f32[128,2048]{1,0:T(8,128)S(1)}, u32[]{:S(2)}) copy-start(f32[128,2048]{1,0:T(8,128)S(1)} %get-tuple-element.161) | copy-start | bytes 3145732
  302.5 2.3 copy-start
  304.8 1.5 copy-start.1
  572.3 5.3 copy-start.13
  576.2 7.0 slice-start
  577.6 5.6 slice-start.1
  645.2 114.2 %copy-start.9 = (f32[1,2048]{1,0:T(1,128)S(1)}, f32[1,2048]{1,0:T(1,128)}, u32[]{:S(2)}) copy-start(f32[1,2048]{1,0:T(1,128)} %reshape.170.gain_ref) | copy-start | bytes 24580
  759.4 1.1 copy-start.5
  760.5 1.0 copy-start.7
  761.5 0.9 copy-start.8
Sparse Core Ops, SparseCore 0:
  11.0 108.4 all-gather.3
  122.6 157.8 all-gather.5

commit v5 on v4

--- a/solution.py
+++ b/solution.py
@@ -53,6 +53,16 @@
         n = {"x": self.X, "y": self.Y, "z": self.Z}[axis]
         i = {"x": self.x, "y": self.y, "z": self.z}[axis]
         return [lax.rem(i + o, n) for o in range(1, n)]
+
+    def far_first(self):
+        table = [sorted((k for k in range(self.Z) if k != z), key=lambda k: (-abs(k - z), -k)) for z in range(self.Z)]
+        out = []
+        for n in range(self.Z - 1):
+            k = 0
+            for z in range(self.Z):
+                k = k + jnp.where(self.z == z, table[z][n], 0)
+            out.append(k)
+        return out + [self.z]
 
     def barrier(self, reach):
         sem = pltpu.get_barrier_semaphore()
@@ -266,40 +276,39 @@
 
 
 class Spread:
-    def __init__(self, p, same, src, out, send_sem, recv_sem):
-        self.p, self.same, self.src, self.out = p, same, src, out
-        self.send_sem, self.recv_sem = send_sem, recv_sem
+    def __init__(self, p, parts, out, send_sem, recv_sem, over_sem):
+        self.p, self.parts, self.out = p, parts, out
+        self.send_sem, self.recv_sem, self.over_sem = send_sem, recv_sem, over_sem
 
     @staticmethod
-    def semaphores(U, B):
+    def semaphores(U, B, n):
         dma = pltpu.SemaphoreType.DMA
-        return [dma((2, 2 * B)), dma((U * B,))]
-
-    def part(self, r):
-        return self.src if self.same else self.src.at[r]
+        return [dma((n, 2 * B)), dma((n, 2 * B)), dma((2, 2 * B))]
 
     def out_to(self, o):
         p = self.p
         r = lax.rem(p.r + o, 2 * p.B)
-        return remote(self.part(r), self.out.at[p.me], self.send_sem.at[0, r], self.recv_sem.at[p.me], p.plane_dev(r))
+        return [remote(src, self.out.at[(p.me,) + at], self.send_sem.at[n, r], self.recv_sem.at[n, p.r], p.plane_dev(r))
+                for n, (src, at) in enumerate(self.parts(r))]
 
     def across(self, r):
         f = self.p.at(r, self.p.x)
-        return remote(self.out.at[f], self.out.at[f], self.send_sem.at[1, r], self.recv_sem.at[f], self.p.x_peer)
-
-    def arrive(self, f):
-        remote(self.out.at[f], self.out.at[f], self.send_sem.at[0, 0], self.recv_sem.at[f], self.p.x_peer).wait_recv()
+        return remote(self.out.at[f], self.out.at[f], self.over_sem.at[0, r], self.over_sem.at[1, r], self.p.x_peer)
 
     def begin(self):
         p = self.p
 
         @pl.loop(1, 2 * p.B)
         def _(o):
-            self.out_to(o).start()
-
-        cp = pltpu.make_async_copy(self.part(p.r), self.out.at[p.me], self.send_sem.at[0, p.r])
-        cp.start()
-        cp.wait()
+            for cp in self.out_to(o):
+                cp.start()
+
+        mine = [pltpu.make_async_copy(src, self.out.at[(p.me,) + at], self.send_sem.at[n, p.r])
+                for n, (src, at) in enumerate(self.parts(p.r))]
+        for cp in mine:
+            cp.start()
+        for cp in mine:
+            cp.wait()
         self.across(p.r).start()
 
     def middle(self):
@@ -308,7 +317,9 @@
         @pl.loop(1, 2 * p.B)
         def _(o):
             r = lax.rem(p.r + o, 2 * p.B)
-            self.arrive(p.at(r, p.x))
+            for n, (_, at) in enumerate(self.parts(r)):
+                ref = self.out.at[(p.at(r, p.x),) + at]
+                remote(ref, ref, self.send_sem.at[n, 0], self.recv_sem.at[n, r], p.x_peer).wait_recv()
             self.across(r).start()
 
     def end(self):
@@ -316,12 +327,14 @@
 
         @pl.loop(0, 2 * p.B)
         def _(r):
-            self.arrive(p.at(r, 1 - p.x))
+            f = p.at(r, 1 - p.x)
+            remote(self.out.at[f], self.out.at[f], self.over_sem.at[0, 0], self.over_sem.at[1, r], p.x_peer).wait_recv()
             self.across(r).wait_send()
 
         @pl.loop(1, 2 * p.B)
         def _(o):
-            self.out_to(o).wait_send()
+            for cp in self.out_to(o):
+                cp.wait_send()
 
 
 def any_specs(n):
@@ -372,12 +385,19 @@
     )(v, val, gate)
 
 
-def front_kernel(U, B, tok, small, weights, tok_out, small_out, weights_out, *sems):
+def front_kernel(U, B, width, copies, tok, small, wq, wk, wv, tok_out, small_out, weights_out, *sems):
     p = Place(U, B)
     p.barrier("plane")
     g = PlaneGather(p, tok, tok_out, *sems[:3])
-    s = Spread(p, True, small, small_out, *sems[3:5])
-    w = Spread(p, False, weights, weights_out, *sems[5:7])
+    s = Spread(p, lambda r: [(small, ())], small_out, *sems[3:6])
+    every = slice(None)
+
+    def columns(r):
+        h = lax.div(r, copies)
+        cols = pl.ds(pl.multiple_of(h * width, width), width)
+        return [(m.at[:, cols], (every, slice(n * width, (n + 1) * width))) for n, m in enumerate((wq, wk, wv))]
+
+    w = Spread(p, columns, weights_out, *sems[6:9])
     s.begin()
     g.step(0)
     w.begin()
@@ -385,76 +405,39 @@
         g.step(n)
         if n == 1:
             s.middle()
-        if n == 2:
             w.middle()
     s.end()
     w.end()
     g.end()
 
 
-def front(tok, small, weights, U, B, cid):
+def front(tok, small, weights, width, copies, U, B, cid):
     F = U * B
+    rows = weights[0].shape[0]
+    shapes = [((F,) + tok.shape[1:], tok.dtype), ((F,) + small.shape, small.dtype), ((F, rows, 3 * width), weights[0].dtype)]
     return pl.pallas_call(
-        functools.partial(front_kernel, U, B),
-        out_shape=[
-            jax.ShapeDtypeStruct((F,) + tok.shape[1:], tok.dtype),
-            jax.ShapeDtypeStruct((F,) + small.shape, small.dtype),
-            jax.ShapeDtypeStruct((F,) + weights.shape[1:], weights.dtype),
-        ],
-        in_specs=any_specs(3),
+        functools.partial(front_kernel, U, B, width, copies),
+        out_shape=[jax.ShapeDtypeStruct(*m) for m in shapes],
+        in_specs=any_specs(5),
         out_specs=any_specs(3),
-        scratch_shapes=PlaneGather.semaphores(U, B) + Spread.semaphores(U, B) * 2,
+        scratch_shapes=PlaneGather.semaphores(U, B) + Spread.semaphores(U, B, 1) + Spread.semaphores(U, B, 3),
         compiler_params=pltpu.CompilerParams(collective_id=cid, has_side_effects=True),
-    )(tok, small, weights)
-
-
-def exchange_kernel(U, B, src, out, send_sem, recv_sem):
-    p = Place(U, B)
-    p.barrier("every")
-
-    def copy(o):
-        f = lax.rem(p.me + o, p.F)
-        return f, remote(src.at[f], out.at[p.me], send_sem.at[f], recv_sem.at[p.me], p.flat_dev(f))
-
-    @pl.loop(1, p.F)
-    def _(o):
-        copy(o)[1].start()
-
-    cp = pltpu.make_async_copy(src.at[p.me], out.at[p.me], recv_sem.at[p.me])
-    cp.start()
-    cp.wait()
-
-    @pl.loop(1, p.F)
-    def _(o):
-        f, cp = copy(o)
-        remote(out.at[f], out.at[f], send_sem.at[f], recv_sem.at[f], p.flat_dev(f)).wait_recv()
-        cp.wait_send()
-
-
-def exchange(v, U, B, cid):
-    return pl.pallas_call(
-        functools.partial(exchange_kernel, U, B),
-        out_shape=jax.ShapeDtypeStruct(v.shape, v.dtype),
-        in_specs=any_specs(1),
-        out_specs=any_specs(1)[0],
-        scratch_shapes=[pltpu.SemaphoreType.DMA((U * B,))] * 2,
-        compiler_params=pltpu.CompilerParams(collective_id=cid, has_side_effects=True),
-    )(v)
+    )(tok, small, *weights)
 
 
 class Scatter:
-    def __init__(self, p, acc, rc, rx0, rx1, ry0, ry1, rz, fin, loc, cs, cr, xs, xr, ys, yr, zs, zr, like=(0, 1)):
-        self.p, self.like = p, like
+    def __init__(self, p, acc, rc, rx0, rx1, ry0, ry1, rz, fin, loc, cs, cr, xs, xr, ys, yr, zs, zr, like=(0, 1), chain=False):
+        self.p, self.like, self.chain = p, like, chain
         self.acc, self.rc, self.rx, self.ry, self.rz, self.fin = acc, rc, (rx0, rx1), (ry0, ry1), rz, fin
         self.loc, self.cs, self.cr = loc, cs, cr
         self.xs, self.xr, self.ys, self.yr, self.zs, self.zr = xs, xr, ys, yr, zs, zr
-        self.order = p.others("z") + [p.z]
+        self.order = p.far_first() if chain else p.others("z") + [p.z]
         self.steps = p.Z + 2
-        self.started = []
+        self.started, self.maybe = [], []
         self.local = True
 
     @staticmethod
-    def scratch(U, B, rows, D, t, like=(0, 1)):
+    def scratch(U, B, rows, D, t, like=(0, 1), chain=False):
         X, Y, Z, Q = U // 2, 2, B // 2, U * B // 2
         dma = pltpu.SemaphoreType.DMA
         x, y = max(X - 1, 1), Y - 1
@@ -465,7 +448,7 @@
             pltpu.VMEM((x, Z if like[1] else Z * Y, rows, D), t),
             pltpu.VMEM((y, Z, rows, D), t),
             pltpu.VMEM((y, Z * X if like[1] else Z, rows, D), t),
-            pltpu.VMEM((2, Z, rows, D), t),
+            pltpu.VMEM((2, 2, Z, rows, D) if chain else (2, Z, rows, D), t),
             pltpu.VMEM((2, rows, D), jnp.float32),
             dma((Q, 2)),
             dma((Q, 2)),
@@ -475,7 +458,7 @@
             dma((2, y, Z * X)),
             dma((2, y, Z * X)),
             dma((2, Z)),
-            dma((2, Z)),
+            dma((2, 2, Z) if chain else (2, Z)),
         ]
 
     SCRATCH = 17
@@ -539,8 +522,33 @@
             out.append(self.ry[h].at[o, s])
         return out
 
+    def along_z(self, n, h, q, extra):
+        p = self.p
+        k = self.order[n]
+        here = self.acc.at[q, h]
+        add(here, extra)
+        for way, cond in enumerate(((k >= p.z) & (p.z > 0), (k <= p.z) & (p.z < p.Z - 1))):
+            @pl.when(cond)
+            def _(way=way):
+                self.got(self.rz.at[way, h, k], self.zr.at[way, h, k])
+                add(here, [self.rz.at[way, h, k]])
+        if n == p.Z - 1:
+            add(here, [], self.fin.at[h])
+            return
+        for way, cond, z in ((0, k > p.z, p.z + 1), (1, k < p.z, p.z - 1)):
+            cp = remote(here, self.rz.at[way, h, k], self.zs.at[h, k], self.zr.at[way, h, k], p.dev(p.x, p.y, z, p.c))
+
+            @pl.when(cond)
+            def _(cp=cp):
+                cp.start()
+
+            self.maybe.append((cond, cp))
+
     def last(self, n, h, q, extra):
         p = self.p
+        if self.chain:
+            self.along_z(n, h, q, extra)
+            return
         k = self.order[n]
         if n < p.Z - 1:
             add(self.acc.at[q, h], extra)
@@ -603,6 +611,10 @@
     def sent(self):
         for cp in self.started:
             cp.wait_send()
+        for cond, cp in self.maybe:
+            @pl.when(cond)
+            def _(cp=cp):
+                cp.wait_send()
 
 
 def add(dst, srcs, f32_out=None):
@@ -628,9 +640,10 @@
         self.acc, self.rc, self.rz, self.fin, self.ry = acc, rc, rz, fin, (ry.at[0], ry.at[1])
         self.loc, self.cs, self.cr = loc, cs, cr
         self.ys, self.yr, self.zs, self.zr = ys, yr, zs, zr
-        self.order = p.others("z") + [p.z]
+        self.chain = True
+        self.order = p.far_first()
         self.steps = p.Z + 1
-        self.started = []
+        self.started, self.maybe = [], []
         self.local = True
 
     @staticmethod
@@ -641,7 +654,7 @@
             pltpu.VMEM((B, 2, rows, D), t),
             pltpu.VMEM((B, 2, rows, D), t),
             pltpu.VMEM((2, Y - 1, Z, rows, D), t),
-            pltpu.VMEM((2, Z, rows, D), t),
+            pltpu.VMEM((2, 2, Z, rows, D), t),
             pltpu.VMEM((2, rows, D), jnp.float32),
             dma((B, 2)),
             dma((B, 2)),
@@ -649,7 +662,7 @@
             dma((2, Y - 1, Z)),
             dma((2, Y - 1, Z)),
             dma((2, Z)),
-            dma((2, Z)),
+            dma((2, 2, Z)),
         ]
 
     SCRATCH = 12
@@ -719,22 +732,32 @@
         KB = self.hot_buf.shape[1]
         cut = min(D, 512)
 
-        for n in range(0, D, cut):
-            t = lax.dot_general(self.hot_buf[...], self.rows_buf[:, :, n:n + cut].reshape(experts * RB, cut),
-                                (((0,), (0,)), ((), ())), preferred_element_type=jnp.float32)
-            self.stage[:, :, :, n:n + cut] = t.astype(self.stage.dtype).reshape(self.stage.shape[:3] + (cut,))
-        kept = []
+        half = KB // 2
+        t = s.acc.shape[2]
+
+        def blocks(core, put):
+            hot = self.hot_buf[:, pl.ds(pl.multiple_of(core * half, half), half)]
+            for n in range(0, D, cut):
+                m = lax.dot_general(hot, self.rows_buf[:, :, n:n + cut].reshape(experts * RB, cut),
+                                    (((0,), (0,)), ((), ())), preferred_element_type=jnp.float32).astype(s.acc.dtype)
+                for i in range(p.Y):
+                    for h in (0, 1):
+                        at = (i * 2 + h) * t
+                        put(i, h, n, m[at:at + t])
+
+        def away(i, h, n, m):
+            self.stage[i, h, :, n:n + cut] = m
+
+        def own(i, h, n, m):
+            s.acc[p.chip(j, i, k), h, :, n:n + cut] = m
+
+        blocks(1 - p.c, away)
         for i in range(p.Y):
             for h in (0, 1):
-                q = p.chip(j, i, k)
-                cp = s.across(self.stage.at[(1 - p.c) * p.Y + i, h], q, h)
+                cp = s.across(self.stage.at[i, h], p.chip(j, i, k), h)
                 cp.start()
                 self.sent.append(cp)
-                cp = s.keep(self.stage.at[p.c * p.Y + i, h], q, h)
-                cp.start()
-                kept.append(cp)
-        for cp in kept:
-            cp.wait()
+        blocks(p.c, own)
 
     def end(self):
         for cp in self.sent:
@@ -786,7 +809,7 @@
             out_specs=any_specs(2),
             scratch_shapes=Scatter.scratch(U, B, rows, D, a.dtype) * 2 + [
                 pltpu.VMEM((experts, RB, D), a.dtype), pltpu.VMEM((n, KB), hot.dtype),
-                pltpu.VMEM((4, 2, rows, D), a.dtype), dma((2,)), dma((1,))],
+                pltpu.VMEM((2, 2, rows, D), a.dtype), dma((2,)), dma((1,))],
             compiler_params=pltpu.CompilerParams(
                 collective_id=cid, has_side_effects=True, vmem_limit_bytes=62 * 2**20),
         )(a, b, hot)
@@ -862,7 +885,7 @@
     at = PlaneScatter.SCRATCH
     work = [PlaneScatter(p, *scratch[:at])]
     if more:
-        work.append(Scatter(p, *scratch[at:at + Scatter.SCRATCH], like=(0, 0)))
+        work.append(Scatter(p, *scratch[at:at + Scatter.SCRATCH], like=(0, 0), chain=True))
         at += Scatter.SCRATCH
     ex = []
     for i in range(2):
@@ -918,7 +941,7 @@
         if o is not None:
             args.append(o)
             shapes.append(sds(o.shape[1:], f32))
-            scratch += Scatter.scratch(U, B, o.shape[2], o.shape[3], o.dtype, (0, 0))
+            scratch += Scatter.scratch(U, B, o.shape[2], o.shape[3], o.dtype, (0, 0), True)
         for m in (weights, small):
             scratch += PairExchange.scratch(U, B, m.shape[1], m.shape[2], m.dtype)
         return pl.pallas_call(
@@ -1034,42 +1057,66 @@
     )(q, k, vt)
 
 
-def attend_back_kernel(scale, q_ref, do_ref, lse_ref, k_ref, kt_ref, v_ref, dq_ref, dk_ref, dv_ref):
-    @pl.when(pl.program_id(0) == 0)
-    def _():
-        dk_ref[...] = jnp.zeros_like(dk_ref)
-        dv_ref[...] = jnp.zeros_like(dv_ref)
-
-    p = jnp.exp(dot(k_ref[...], q_ref[...], 1, 1) * scale - lse_ref[...])
-    dp = dot(v_ref[...], do_ref[...], 1, 1)
-    delta = jnp.sum(p * dp, axis=0, keepdims=True)
-    ds = (p * (dp - delta)).astype(jnp.bfloat16)
-    dv_ref[...] += dot(p.astype(jnp.bfloat16), do_ref[...], 1, 0)
-    dk_ref[...] += dot(ds, q_ref[...], 1, 0) * scale
-    dq_ref[...] = (dot(kt_ref[...], ds, 1, 0) * scale).T
-
-
-def attend_back(q, do, lse, k, kt, v):
+def attend_back_kernel(U, B, bq, scale, src_ref, q_ref, lse_ref, k_ref, kt_ref, v_ref,
+                       dq_ref, dk_ref, dv_ref, do_ref, send, recv, local):
+    p = Place(U, B)
+    p.barrier("every")
+    per = bq // do_ref.shape[1]
+    n = q_ref.shape[0] // bq
+
+    def away(f):
+        return remote(src_ref.at[f], do_ref.at[p.me], send.at[f], recv.at[p.me], p.flat_dev(f))
+
+    @pl.loop(1, p.F)
+    def _(o):
+        away(lax.rem(p.me + o, p.F)).start()
+
+    cp = pltpu.make_async_copy(src_ref.at[p.me], do_ref.at[p.me], local.at[0])
+    cp.start()
+    dk_ref[...] = jnp.zeros_like(dk_ref)
+    dv_ref[...] = jnp.zeros_like(dv_ref)
+    cp.wait()
+
+    @pl.loop(0, n)
+    def _(t):
+        i = lax.rem(n - t + lax.div(p.me, per), n)
+        rows = pl.ds(pl.multiple_of(i * bq, bq), bq)
+        e = jnp.exp(dot(k_ref[...], q_ref[rows, :], 1, 1) * scale - lse_ref[:, rows])
+        for d in range(per):
+            f = i * per + d
+
+            @pl.when(f != p.me)
+            def _():
+                remote(do_ref.at[f], do_ref.at[f], send.at[f], recv.at[f], p.flat_dev(f)).wait_recv()
+
+        do = do_ref[pl.ds(i * per, per)].reshape(bq, HD)
+        dp = dot(v_ref[...], do, 1, 1)
+        delta = jnp.sum(e * dp, axis=0, keepdims=True)
+        ds = (e * (dp - delta)).astype(jnp.bfloat16)
+        dv_ref[...] += dot(e.astype(jnp.bfloat16), do, 1, 0)
+        dk_ref[...] += dot(ds, q_ref[rows, :], 1, 0) * scale
+        dq_ref[rows, :] = (dot(kt_ref[...], ds, 1, 0) * scale).T
+
+    @pl.loop(1, p.F)
+    def _(o):
+        away(lax.rem(p.me + o, p.F)).wait_send()
+
+
+def attend_back(grads, q, lse, k, kt, v, U, B, cid):
     n = q.shape[0]
+    F = U * B
     bq = 256 if n <= 2048 else 128
-    row = lambda i: (i, 0)
-    whole = lambda i: (0, 0)
-    f32 = jax.ShapeDtypeStruct((n, HD), jnp.float32)
+    vmem = pl.BlockSpec(memory_space=pltpu.VMEM)
+    dma = pltpu.SemaphoreType.DMA
     return pl.pallas_call(
-        functools.partial(attend_back_kernel, 1.0 / math.sqrt(HD)),
-        grid=(n // bq,),
-        in_specs=[
-            pl.BlockSpec((bq, HD), row),
-            pl.BlockSpec((bq, HD), row),
-            pl.BlockSpec((1, bq), lambda i: (0, i)),
-            pl.BlockSpec((n, HD), whole),
-            pl.BlockSpec((HD, n), whole),
-            pl.BlockSpec((n, HD), whole),
-        ],
-        out_specs=[pl.BlockSpec((bq, HD), row), pl.BlockSpec((n, HD), whole), pl.BlockSpec((n, HD), whole)],
-        out_shape=[f32, f32, f32],
-        compiler_params=pltpu.CompilerParams(vmem_limit_bytes=58 * 2**20),
-    )(q, do, lse, k, kt, v)
+        functools.partial(attend_back_kernel, U, B, bq, 1.0 / math.sqrt(HD)),
+        in_specs=any_specs(1) + [vmem] * 5,
+        out_specs=[vmem] * 3,
+        out_shape=[jax.ShapeDtypeStruct((n, HD), jnp.float32)] * 3,
+        scratch_shapes=[pltpu.VMEM(grads.shape, grads.dtype), dma((F,)), dma((F,)), dma((1,))],
+        compiler_params=pltpu.CompilerParams(
+            collective_id=cid, has_side_effects=True, vmem_limit_bytes=58 * 2**20),
+    )(grads, q, lse, k, kt, v)
 
 
 def turn(v, cosine, sine):
@@ -1093,7 +1140,7 @@
 
 def project(tok, gain, w, qk, cosine, sine):
     n, D = tok.shape
-    bm = 256
+    bm = 512
     row, whole = (lambda i: (i, 0)), (lambda i: (0, 0))
     head, across = pl.BlockSpec((bm, HD), row), pl.BlockSpec((HD, bm), lambda i: (0, i))
     sds = jax.ShapeDtypeStruct
@@ -1132,6 +1179,7 @@
         grads.append((r * (m - norm * jnp.mean(m * norm, axis=-1, keepdims=True))).astype(bf16))
     grads.append(dv_ref[...].astype(bf16))
     grad = jnp.concatenate(grads, axis=1)
+    across = grad.T
     tok = tok_ref[...].astype(f32)
     norm = tok * lax.rsqrt(jnp.mean(tok * tok, axis=-1, keepdims=True) + EPSILON)
     hidden = (norm * gain_ref[...]).astype(bf16)
@@ -1141,11 +1189,12 @@
         part = dot(grad, w_ref[n:n + cut, :], 1, 1)
         part_ref[:, n:n + cut] = part.astype(bf16)
         da_ref[0:1, n:n + cut] += jnp.sum(part * norm[:, n:n + cut], axis=0, keepdims=True)
-        dw_ref[n:n + cut, :] += dot(hidden[:, n:n + cut], grad, 0, 0)
+        dw_ref[:, n:n + cut] += dot(across, hidden[:, n:n + cut], 1, 0)
 
     @pl.when(pl.program_id(0) == pl.num_programs(0) - 1)
     def _():
-        dwout_ref[...] = dw_ref[...].astype(bf16)
+        for n in range(0, D, cut):
+            dwout_ref[n:n + cut, :] = dw_ref[:, n:n + cut].T.astype(bf16)
 
 
 def head_back(dq, dk, dv, rq, rk, cosine, sine, qk, tok, gain, w):
@@ -1165,7 +1214,7 @@
             pl.BlockSpec((8, D), whole)],
         out_shape=[sds((n, D), jnp.bfloat16), sds((D, 3 * HD), jnp.bfloat16), sds((8, HD), jnp.float32),
                    sds((8, D), jnp.float32)],
-        scratch_shapes=[pltpu.VMEM((D, 3 * HD), jnp.float32)],
+        scratch_shapes=[pltpu.VMEM((3 * HD, D), jnp.float32)],
         compiler_params=pltpu.CompilerParams(vmem_limit_bytes=58 * 2**20),
     )(dq, dk, dv, rq, rk, cosine, sine, qk, tok, gain, w)
 
@@ -1203,7 +1252,7 @@
                   group_spec(normed.shape, Z), group_spec(cot.shape, Z)],
         out_specs=[out, out],
         out_shape=[jax.ShapeDtypeStruct((experts, G * RB, D), jnp.bfloat16)] * 2,
-        compiler_params=pltpu.CompilerParams(vmem_limit_bytes=58 * 2**20),
+        compiler_params=pltpu.CompilerParams(vmem_limit_bytes=62 * 2**20),
     )(hot, rg, normed, cot)
 
 
@@ -1218,11 +1267,13 @@
     back = dot(pg, wd_ref[0], 1, 1)
     dgate = (back * up * sigma * (1.0 + gate * (1.0 - sigma))).astype(bf16)
     dup = (back * silu).astype(bf16)
-    cut = min(D, 512)
+    cut = min(D, 1024)
     weight = rg_ref[0, :, 0:1]
+    both = jnp.concatenate([dgate, dup], axis=1)
+    ff = dgate.shape[1]
     first = pl.program_id(1) == 0
 
-    def gather_in(ref, ix, value):
+    def put(ref, ix, value):
         if pl.num_programs(1) == 1:
             ref[ix] = value
         else:
@@ -1232,9 +1283,10 @@
         c = slice(n, n + cut)
         y_ref[0, :, c] = (dot(inner, wd_ref[0, :, c], 1, 0) * weight).astype(bf16)
         dx_ref[0, :, c] = (dot(dgate, wg_ref[0, c, :], 1, 1) + dot(dup, wu_ref[0, c, :], 1, 1)).astype(bf16)
-        gather_in(dwg_ref, (0, c, slice(None)), dot(x_ref[0, :, c], dgate, 0, 0))
-        gather_in(dwu_ref, (0, c, slice(None)), dot(x_ref[0, :, c], dup, 0, 0))
-        gather_in(dwd_ref, (0, slice(None), c), dot(inner, pg_ref[0, :, c], 0, 0))
+        d = dot(x_ref[0, :, c], both, 0, 0)
+        put(dwg_ref, (0, c, slice(None)), d[:, :ff])
+        put(dwu_ref, (0, c, slice(None)), d[:, ff:])
+        put(dwd_ref, (0, slice(None), c), dot(inner, pg_ref[0, :, c], 0, 0))
 
 
 def expert_layer(x, pg, rg, wg, wu, wd):
@@ -1249,8 +1301,53 @@
         in_specs=[some(a) for a in (x, pg, rg)] + [whole(a) for a in (wg, wu, wd)],
         out_specs=[some(a) for a in (x, x)] + [whole(a) for a in (wg, wu, wd)],
         out_shape=[sds(x.shape, x.dtype)] * 2 + [sds(a.shape, jnp.float32) for a in (wg, wu, wd)],
-        compiler_params=pltpu.CompilerParams(vmem_limit_bytes=60 * 2**20),
+        compiler_params=pltpu.CompilerParams(vmem_limit_bytes=62 * 2**20),
     )(x, pg, rg, wg, wu, wd)
+
+
+def middle_kernel(res_ref, gain_ref, grad_ref, cot_ref, att_ref, w_ref, back_ref, gain_out_ref, heads_ref, part_ref, low_ref):
+    f32, bf16 = jnp.float32, jnp.bfloat16
+
+    @pl.when(pl.program_id(0) == 0)
+    def _():
+        u = res_ref[...]
+        r = lax.rsqrt(jnp.mean(u * u, axis=-1, keepdims=True) + EPSILON)
+        norm = u * r
+        w = grad_ref[...]
+        gain_out_ref[...] = jnp.broadcast_to(jnp.sum(w * norm, axis=0, keepdims=True), gain_out_ref.shape)
+        m = w * gain_ref[...]
+        back = cot_ref[...].astype(f32) + r * (m - norm * jnp.mean(m * norm, axis=-1, keepdims=True))
+        back_ref[...] = back
+        low_ref[...] = back.astype(bf16)
+
+    low = low_ref[...]
+    seqs, heads, positions, _ = heads_ref.shape
+    grad = dot(low, w_ref[...], 1, 1).astype(bf16)
+    for s in range(seqs):
+        for h in range(heads):
+            heads_ref[s, h] = grad[s * positions:(s + 1) * positions, h * HD:(h + 1) * HD]
+    part_ref[...] = dot(att_ref[...], low, 0, 0).astype(bf16)
+
+
+def middle(residual, gain, normed_grad, cot, attended, out_w, seqs):
+    T, D = residual.shape
+    features = attended.shape[1]
+    cut = 512
+    whole = lambda n: (0, 0)
+    sds, f32, bf16 = jax.ShapeDtypeStruct, jnp.float32, jnp.bfloat16
+    full = pl.BlockSpec((T, D), whole)
+    rows = pl.BlockSpec((cut, D), lambda n: (n, 0))
+    return pl.pallas_call(
+        middle_kernel,
+        grid=(features // cut,),
+        in_specs=[full, pl.BlockSpec((1, D), whole), full, full, pl.BlockSpec((T, cut), lambda n: (0, n)), rows],
+        out_specs=[full, pl.BlockSpec((8, D), whole),
+                   pl.BlockSpec((seqs, cut // HD, T // seqs, HD), lambda n: (0, n, 0, 0)), rows],
+        out_shape=[sds((T, D), f32), sds((8, D), f32), sds((seqs, features // HD, T // seqs, HD), bf16),
+                   sds((features, D), bf16)],
+        scratch_shapes=[pltpu.VMEM((T, D), bf16)],
+        compiler_params=pltpu.CompilerParams(vmem_limit_bytes=58 * 2**20),
+    )(residual, gain, normed_grad, cot, attended, out_w)
 
 
 def close_kernel(x_ref, w_ref, own_ref, other_ref, back_ref, tok_ref, gain_ref, q_ref, k_ref, v_ref, in_ref):
@@ -1315,10 +1412,7 @@
         [slot, gates.transpose(1, 0, 2).reshape(-1)]
         + [g.astype(f32) for g in (attn_gain, ffn_gain, qk_gain[0], qk_gain[1])])
     small = jnp.pad(small, (0, -small.shape[0] % 1024)).reshape(-1, 128)
-    heads_w = jnp.stack([w_query, w_key, w_value]).reshape(3, W, H, HD).transpose(2, 1, 0, 3).reshape(H, W, 3 * HD)
-    if R > 1:
-        heads_w = heads_w[np.arange(2 * B) // R]
-    seq_tok, table, head_w = front(tok, small, heads_w, U, B, 1)
+    seq_tok, table, head_w = front(tok, small, (w_query, w_key, w_value), HD, R, U, B, 1)
     seq_tok, head_w = seq_tok.reshape(L, D), head_w.reshape(D, 3 * HD)
     out_w = lax.all_gather(w_out, AXES, axis=0, tiled=True)
     cot_all = lax.all_gather(cot, AXES, axis=0)
@@ -1361,34 +1455,30 @@
 
     attended = from_heads(att_rows)
     residual = rows_f + jnp.dot(attended, out_w, preferred_element_type=f32)
-    normed_full, ffn_back = jax.vjp(rms_norm, residual, ffn_g)
-    normed = normed_full.astype(bf16).reshape(2, positions, D)
+    normed = rms_norm(residual, ffn_g).astype(bf16).reshape(2, positions, D)
 
     normed_all, hot, row_gate = gather_blocks(normed, val, gate_of, RB, U, B, 2)
     shape = groups + (T, D)
-    x, pair_grad = dispatch(hot, row_gate, normed_all.reshape(shape), cot_all.reshape(shape))
-    y, dx, gate_grad, up_grad, down_grad = expert_layer(x, pair_grad, row_gate, expert_gate, expert_up, expert_down)
+    normed_all, cot_all = normed_all.reshape(shape), cot_all.reshape(shape)
+    weights = (expert_gate, expert_up, expert_down)
+    x, pair_grad = dispatch(hot, row_gate, normed_all, cot_all)
+    y, dx, gate_grad, up_grad, down_grad = expert_layer(x, pair_grad, row_gate, *weights)
     normed_grad, mixed_sum = scatter_pair(dx, y, hot, positions, U, B, 3)
     mixed = (residual + mixed_sum.reshape(T, D)).reshape(2, positions, D).transpose(1, 0, 2).astype(bf16)
     normed_grad = normed_grad.reshape(T, D)
 
-    residual_norm_grad, ffn_gain_part = ffn_back(normed_grad)
-    residual_grad = cot.reshape(T, D).astype(f32) + residual_norm_grad
-    attn_out_grad = residual_grad.astype(bf16)
-    att_grad = dot(attn_out_grad, out_w, 1, 1).astype(bf16)
-    att_grad = jnp.repeat(att_grad.reshape(2, positions, H, HD).transpose(0, 2, 1, 3), R, axis=1)
-    att_grad = att_grad.reshape(F, positions, HD)
-    do = exchange(att_grad, U, B, 6).reshape(L, HD)
-    out_part = dot(attended, attn_out_grad, 0, 0).astype(bf16)
+    residual_grad, ffn_gain_part, att_grad, out_part = middle(
+        residual, ffn_g, normed_grad, cot.reshape(T, D), attended, out_w, seqs)
+    att_grad = jnp.repeat(att_grad, R, axis=1).reshape(F, positions, HD)
     out_part = out_part.reshape(F, 2, W // 2, D)
-    dq, dk, dv = attend_back(q, do, lse, k, kt, v)
+    dq, dk, dv = attend_back(att_grad, q, lse, k, kt, v, U, B, 6)
     if R > 1:
         dq, dk, dv = (jnp.where(first_copy, m, 0.0) for m in (dq, dk, dv))
     hidden_part, weight_part, qk_part, attn_gain_part = head_back(
         dq, dk, dv, raw_q, raw_k, cosine, sine, qk_g, seq_tok, attn_g, head_w)
     weight_part = weight_part.reshape(F, W, 3 * HD)
     small = jnp.concatenate(
-        [attn_gain_part[0].reshape(F, W), ffn_gain_part.reshape(F, W),
+        [attn_gain_part[0].reshape(F, W), ffn_gain_part[0].reshape(F, W),
          qk_part[0].reshape(F, nq), qk_part[1].reshape(F, nq)], axis=1)
     small = jnp.pad(small, ((0, 0), (0, -small.shape[1] % 1024))).reshape(F, -1, 128)
     weight_grad, small, own, other, out_grad = finish(

time: 782 us -> 760 us (0.972)
  Pallas kernels: 701 us -> 692 us
  matrix products: 13.4 us -> 4.77 us
    pallas_call x1, Pallas kernels: 114 us -> 102 us  [call(): pl.pallas_call(functools.partial(finish_kernel, U, B, o is not None), out...]
    dot_general x2 -> x0, matrix products: 8.51 us -> none  [dot(): lax.dot_general(a, b, (((ca,), (cb,)), ((), ())), preferred_element_type=...]
    unnamed x55 -> x38, local copies, waits for them, and re-layouts: 22.5 us -> 21.3 us
  transfers between devices with their start and end apart: 2 -> 2, of which waited for: 0 -> 0; matrix products, arithmetic and copies ran while one was open for 3% -> 3% of each run, Pallas kernels for 34% -> 35%
where the time goes in v5:
time: 760 us; the launch traced here: 752 us
  Pallas kernels  692 us (91%)
  local copies, waits for them, and re-layouts  32.6 us (4%)
  between operations  14.9 us (2%)
    pallas_call x1, Pallas kernels, call(): pl.pallas_call(functools.partial(pair_kernel, U, B, pl.ds(c * D, D)), out...  158 us
    pallas_call x1, Pallas kernels, gather_blocks(): pl.pallas_call(functools.partial(gather_kernel, U, B, experts, RB), out_s...  109 us
    pallas_call x1, Pallas kernels, front(): pl.pallas_call(functools.partial(front_kernel, U, B, width, copies), out_...  108 us
    pallas_call x1, Pallas kernels, call(): pl.pallas_call(functools.partial(finish_kernel, U, B, o is not None), out...  102 us
    pallas_call x1, Pallas kernels, expert_layer(): pl.pallas_call(expert_kernel, grid=(x.shape[0], rows // step), in_specs=[...  66.4 us
    pallas_call x1, Pallas kernels, dispatch(): pl.pallas_call(dispatch_kernel, grid=(G,), in_specs=[pl.BlockSpec((1, row...  36.3 us
    pallas_call x1, Pallas kernels, attend(): pl.pallas_call(functools.partial(attend_kernel, U, B, bq, 1.0 / math.sqrt...  33.8 us
    pallas_call x1, Pallas kernels, attend_back(): pl.pallas_call(functools.partial(attend_back_kernel, U, B, bq, 1.0 / math...  31.6 us
  transfers between devices with their start and end apart: 2, of which 0 were waited for; matrix products, arithmetic and copies ran while one was open for 3% of the time, Pallas kernels for 35%

profile of v5, /device:TPU:0, one launch (start us, length us, event | category | flops | bytes accessed | tf_op | source)
XLA Modules:
  0.0 752.0 jit_solution(3984305678236708100)
XLA Ops:
  7.2 0.7 all-gather.4.cloned.1.call-update
  8.0 2.0 copy.98
  10.0 0.5 broadcast.77
  10.5 1.3 reduce.19
  12.1 0.8 copy.66
  13.0 0.8 copy.68
  13.9 2.0 copy.97
  15.9 1.0 convert_reduce_fusion
  16.9 0.7 bitcast_convert_fusion
  17.7 1.4 concatenate.6
  19.1 0.6 pad_bitcast_fusion.small
  19.7 108.4 %shard_map.265 = (bf16[32,64,2048]{2,1,0:T(8,128)(2,1)}, f32[32,24,128]{2,1,0:T(8,128)}, bf16[32,64,384]{2,1,0:T(8,128)(2,1)}) custom-call(bf16[2,64,2048]{2,1,0:T(8,128)(2,1)} %bitcast.75, f32[24,128]{1,0:T(8,128)} %pad_bitcast_fusion.small, bf16[64,2048]{1,0:T(8,128)(2,1)} %wq.1, bf16[64,2048]{1,0:T(8,128)(2,1)} %wk.1, bf16[64,2048]{1,0:T(8,128)(2,1)} %wv.1), custom_call_target="tpu_custom_call" | custom-call | tf_op jit(solution)/shard_map/pallas_call | solution.py:418
  128.1 1.1 copy.96
  129.2 0.7 reshape.155.gain_ref
  130.3 0.7 reshape.144.gain_ref
  132.7 0.6 pad_maximum_fusion.qk_ref
  133.3 13.4 %shard_map.266 = (bf16[2048,128]{1,0:T(8,128)(2,1)}, bf16[2048,128]{1,0:T(8,128)(2,1)}, bf16[2048,128]{1,0:T(8,128)(2,1)}, bf16[128,2048]{1,0:T(8,128)(2,1)}, bf...) custom-call(bf16[2048,2048]{1,0:T(8,128)(2,1)} %bitcast.84, f32[1,2048]{1,0:T(1,128)} %reshape.144.gain_ref, ...), custom_call_target="tpu_custom_call" | custom-call | tf_op jit(solution)/shard_map/pallas_call | solution.py:1148
  146.7 1.0 copy-done.3
  147.7 1.0 copy-done.4
  148.7 1.0 copy-done.7
  149.8 33.8 %shard_map.267 = (bf16[32,64,128]{2,1,0:T(8,128)(2,1)S(1)}, f32[1,2048]{1,0:T(1,128)S(1)}) custom-call(bf16[2048,128]{1,0:T(8,128)(2,1)S(1)} %copy-done.3, bf16[2048,128]{1,0:T(8,128)(2,1)S(1)} %copy-done.4, bf16[128,2048]{1,0:T(8,128)(2,1)S(1)} %copy-done.7), custom_call_target="tpu_custom_call" | custom-call | tf_op jit(solution)/shard_map/pallas_call | solution.py:1049
  183.6 0.3 copy.69
  183.9 0.9 copy.94
  184.9 4.8 multiply_reduce_fusion
  189.8 109.2 %shard_map.268 = (bf16[32,2,64,2048]{3,2,1,0:T(8,128)(2,1)}, bf16[8,640,512]{2,1,0:T(8,128)(2,1)S(1)}, f32[8,640,128]{2,1,0:T(8,128)S(1)}) custom-call(bf16[2,64,2048]{2,1,0:T(8,128)(2,1)S(1)} %bitcast.78, s32[8,8,512]{2,1,0:T(8,128)S(1)} %bitcast.83, f32[8,8,512]{2,1,0:T(8,128)S(1)} %bitcast.82), custom_call_target="tpu_custom_call" | custom-call | tf_op jit(solution)/shard_map/pallas_call | solution.py:376
  299.0 2.3 copy-done
  301.3 1.5 copy-done.1
  302.8 36.3 %shard_map.269 = (bf16[8,640,2048]{2,1,0:T(8,128)(2,1)}, bf16[8,640,2048]{2,1,0:T(8,128)(2,1)}) custom-call(bf16[8,640,512]{2,1,0:T(8,128)(2,1)} %copy-done, f32[8,640,128]{2,1,0:T(8,128)} %copy-done.1, bf16[2,2,4,2,128,2048]{5,4,3,2,1,0:T(8,128)(2,1)} %bitcast.87, bf16[2,2,4,2,128,2048]{5,4,3,2,1,0:T(8,128)(2,1)} %bitcast.86), custom_call_target="tpu_custom_call" | custom-call | tf_op jit(solution)/shard_map/pallas_call | solution.py:1248
  339.2 66.4 %shard_map.270 = (bf16[8,640,2048]{2,1,0:T(8,128)(2,1)}, bf16[8,640,2048]{2,1,0:T(8,128)(2,1)}, f32[8,2048,256]{2,1,0:T(8,128)}, f32[8,2048,256]{2,1,0:T(8,128)}, f32[8,256,2048]{2,1,0:T(8,128)}) custom-call(bf16[8,640,2048]{2,1,0:T(8,128)(2,1)} %get-tuple-element.66.x_ref, bf16[8,640,2048]{2,1,0:T(8,128)(2,1)} %get-tuple-element.67.pg_ref, ...), custom_call_target="tpu_custom_call" | custom-call | tf_op jit(solution)/shard_map/pallas_call | solution.py:1298
  405.6 158.2 %shard_map.271 = (f32[2,64,2048]{2,1,0:T(8,128)}, f32[2,64,2048]{2,1,0:T(8,128)}) custom-call(bf16[8,640,2048]{2,1,0:T(8,128)(2,1)} %get-tuple-element.68.a, bf16[8,640,2048]{2,1,0:T(8,128)(2,1)} %get-tuple-element.69.b, bf16[8,640,512]{2,1,0:T(8,128)(2,1)} %copy-done), custom_call_target="tpu_custom_call" | custom-call | tf_op jit(solution)/shard_map/pallas_call | solution.py:805
  563.8 1.3 fusion.2
  565.2 1.3 copy.95
  566.5 11.5 %shard_map.272 = (f32[128,2048]{1,0:T(8,128)}, f32[8,2048]{1,0:T(8,128)}, bf16[2,16,64,128]{3,2,1,0:T(8,128)(2,1)}, bf16[2048,2048]{1,0:T(8,128)(2,1)}) custom-call(f32[128,2048]{1,0:T(8,128)} %copy-done.12, f32[1,2048]{1,0:T(1,128)} %reshape.155.gain_ref, f32[128,2048]{1,0:T(8,128)} %bitcast.103, bf16[128,2048]{1,0:T(8,128)(2,1)} %bitcast.95, ...), custom_call_target="tpu_custom_call" | custom-call | tf_op jit(solution)/shard_map/pallas_call | solution.py:1340
  578.0 31.6 %shard_map.273 = (f32[2048,128]{1,0:T(8,128)}, f32[2048,128]{1,0:T(8,128)}, f32[2048,128]{1,0:T(8,128)}) custom-call(bf16[32,64,128]{2,1,0:T(8,128)(2,1)} %bitcast.105, bf16[2048,128]{1,0:T(8,128)(2,1)} %get-tuple-element.59.q_ref, f32[1,2048]{1,0:T(1,128)} %copy-done.11, bf16[2048,128]{1,0:T(8,128)(2,1)} %get-tuple-element.60.k_ref, ...), custom_call_target="tpu_custom_call" | custom-call | tf_op jit(solution)/shard_map/pallas_call | solution.py:1111
  609.6 19.6 %shard_map.274 = (bf16[2048,2048]{1,0:T(8,128)(2,1)}, bf16[2048,384]{1,0:T(8,128)(2,1)}, f32[8,128]{1,0:T(8,128)}, f32[8,2048]{1,0:T(8,128)}) custom-call(f32[2048,128]{1,0:T(8,128)} %get-tuple-element.76.dq_ref, f32[2048,128]{1,0:T(8,128)} %get-tuple-element.77.dk_ref, f32[2048,128]{1,0:T(8,128)} %get-tuple-element.78.dv_ref, ...), custom_call_target="tpu_custom_call" | custom-call | tf_op jit(solution)/shard_map/pallas_call | solution.py:1206
  629.3 0.8 slice_reduce_fusion.3
  630.0 0.9 slice_reduce_fusion
  631.4 0.7 copy.83
  632.1 102.2 %shard_map.275 = (bf16[16,64,384]{2,1,0:T(8,128)(2,1)}, f32[16,8,128]{2,1,0:T(8,128)}, f32[64,2048]{1,0:T(8,128)}, bf16[64,2048]{1,0:T(8,128)(2,1)}, f32[2,32,2048]{2,1,0:T(8,128)}) custom-call(bf16[2,16,64,384]{3,2,1,0:T(8,128)(2,1)} %bitcast.99, f32[2,16,8,128]{3,2,1,0:T(8,128)} %bitcast.104, bf16[32,64,2048]{2,1,0:T(8,128)(2,1)} %bitcast.89, ...), custom_call_target="tpu_custom_call" | custom-call | tf_op jit(solution)/shard_map/pallas_call | solution.py:947
  734.3 1.1 copy-done.6
  735.4 1.0 copy-done.8
  736.5 0.9 copy-done.9
  737.4 1.5 shard_map.276
  738.9 1.8 copy.78
  740.7 0.9 reduce_sum.49
  741.7 0.6 fusion.9
  742.3 0.6 slice.70
  742.8 1.9 copy.100
  (58 shorter events, 3.3 us)
Async XLA Ops:
  7.2 125.4 %copy-start.13 = (s32[2,2,4,2]{3,2,1,0:T(4,128)S(1)}, s32[2,2,4,2]{3,2,1,0:T(4,128)}, u32[]{:S(2)}) copy-start(s32[2,2,4,2]{3,2,1,0:T(4,128)} %constant.60) | copy-start | bytes 388
  7.2 177.7 %all-gather.4.cloned.1.call-start = ((), (), s32[]{:S(2)}) async-start(), calls=%async_computation | async-start | bytes 8650752 | tf_op jit(solution)/shard_map/all_gather | solution.py:1417
  7.9 294.9 %all-gather.6.cloned.1.call-start = ((), (), s32[]{:S(2)}) async-start(), calls=%async_computation.1 | async-start | bytes 17301504 | tf_op jit(solution)/shard_map/all_gather | solution.py:1418
  132.5 52.4 %copy-start.2 = (bf16[64,2,2048]{2,0,1:T(8,128)(2,1)S(1)}, bf16[64,2,2048]{2,0,1:T(8,128)(2,1)}, u32[]{:S(2)}) copy-start(bf16[64,2,2048]{2,0,1:T(8,128)(2,1)} %copy.97) | copy-start | bytes 1572868
  146.6 1.0 copy-start.3
  147.7 1.0 copy-start.4
  148.7 1.0 copy-start.7
  183.6 6.1 copy-start.11
  189.6 374.2 %copy-start.12 = (f32[128,2048]{1,0:T(8,128)}, f32[128,2048]{1,0:T(8,128)S(1)}, u32[]{:S(2)}) copy-start(f32[128,2048]{1,0:T(8,128)S(1)} %get-tuple-element.165.res_ref) | copy-start | bytes 3145732
  299.0 2.3 copy-start
  301.3 1.5 copy-start.1
  632.1 102.2 %copy-start.5 = (f32[128,2048]{1,0:T(8,128)S(1)}, f32[128,2048]{1,0:T(8,128)}, u32[]{:S(2)}) copy-start(f32[128,2048]{1,0:T(8,128)} %get-tuple-element.90) | copy-start | bytes 3145732
  632.1 102.2 %copy-start.10 = (f32[1,2048]{1,0:T(1,128)S(1)}, f32[1,2048]{1,0:T(1,128)}, u32[]{:S(2)}) copy-start(f32[1,2048]{1,0:T(1,128)} %reshape.144.gain_ref) | copy-start | bytes 24580
  734.3 1.1 copy-start.6
  735.4 1.0 copy-start.8
  736.5 0.9 copy-start.9
Sparse Core Ops, SparseCore 0:
  11.0 109.7 all-gather.3
  123.9 153.8 all-gather.5

commit v6 on v5

--- a/solution.py
+++ b/solution.py
@@ -381,7 +381,7 @@
         scratch_shapes=Gather.semaphores(U, B) + [
             pltpu.VMEM(hot.shape, hot.dtype), pltpu.VMEM(rg.shape, rg.dtype), pltpu.SemaphoreType.DMA((2,))],
         compiler_params=pltpu.CompilerParams(
-            collective_id=cid, has_side_effects=True, vmem_limit_bytes=32 * 2**20),
+            collective_id=cid, has_side_effects=True, vmem_limit_bytes=62 * 2**20),
     )(v, val, gate)
 
 

time: 760 us -> 763 us (level)
    unnamed x38 -> x34, local copies, waits for them, and re-layouts: 21.3 us -> 17.7 us
  transfers between devices with their start and end apart: 2 -> 2, of which waited for: 0 -> 0; matrix products, arithmetic and copies ran while one was open for 3% -> 3% of each run, Pallas kernels for 35% -> 36%
where the time goes in v6:
time: 763 us; the launch traced here: 754 us
  Pallas kernels  696 us (91%)
  local copies, waits for them, and re-layouts  30.3 us (4%)
  between operations  14.9 us (2%)
  other arithmetic  7.88 us (1%)
    pallas_call x1, Pallas kernels, call(): pl.pallas_call(functools.partial(pair_kernel, U, B, pl.ds(c * D, D)), out...  158 us
    pallas_call x1, Pallas kernels, gather_blocks(): pl.pallas_call(functools.partial(gather_kernel, U, B, experts, RB), out_s...  114 us
    pallas_call x1, Pallas kernels, front(): pl.pallas_call(functools.partial(front_kernel, U, B, width, copies), out_...  108 us
    pallas_call x1, Pallas kernels, call(): pl.pallas_call(functools.partial(finish_kernel, U, B, o is not None), out...  103 us
    pallas_call x1, Pallas kernels, expert_layer(): pl.pallas_call(expert_kernel, grid=(x.shape[0], rows // step), in_specs=[...  66.4 us
    pallas_call x1, Pallas kernels, dispatch(): pl.pallas_call(dispatch_kernel, grid=(G,), in_specs=[pl.BlockSpec((1, row...  36.3 us
    pallas_call x1, Pallas kernels, attend(): pl.pallas_call(functools.partial(attend_kernel, U, B, bq, 1.0 / math.sqrt...  33.7 us
    pallas_call x1, Pallas kernels, attend_back(): pl.pallas_call(functools.partial(attend_back_kernel, U, B, bq, 1.0 / math...  31.1 us
  transfers between devices with their start and end apart: 2, of which 0 were waited for; matrix products, arithmetic and copies ran while one was open for 3% of the time, Pallas kernels for 36%

profile of v6, /device:TPU:0, one launch (start us, length us, event | category | flops | bytes accessed | tf_op | source)
XLA Modules:
  0.0 754.4 jit_solution(9278506016264064052)
XLA Ops:
  7.2 0.7 all-gather.4.cloned.1.call-update
  8.0 2.0 copy.98
  10.0 0.5 broadcast.77
  10.5 1.3 reduce.19
  12.1 0.8 copy.66
  13.0 0.8 copy.68
  13.9 2.0 copy.97
  15.9 1.0 convert_reduce_fusion
  16.9 0.7 bitcast_convert_fusion
  17.7 1.4 concatenate.6
  19.1 0.6 pad_bitcast_fusion.small
  19.7 108.4 %shard_map.265 = (bf16[32,64,2048]{2,1,0:T(8,128)(2,1)}, f32[32,24,128]{2,1,0:T(8,128)}, bf16[32,64,384]{2,1,0:T(8,128)(2,1)}) custom-call(bf16[2,64,2048]{2,1,0:T(8,128)(2,1)} %bitcast.75, f32[24,128]{1,0:T(8,128)} %pad_bitcast_fusion.small, bf16[64,2048]{1,0:T(8,128)(2,1)} %wq.1, bf16[64,2048]{1,0:T(8,128)(2,1)} %wk.1, bf16[64,2048]{1,0:T(8,128)(2,1)} %wv.1), custom_call_target="tpu_custom_call" | custom-call | tf_op jit(solution)/shard_map/pallas_call | solution.py:418
  128.1 1.1 copy.96
  129.2 0.7 reshape.155.gain_ref
  130.3 0.7 reshape.144.gain_ref
  132.2 0.7 copy.75
  133.3 0.7 copy.72
  134.0 0.6 pad_maximum_fusion.qk_ref
  134.5 13.4 %shard_map.266 = (bf16[2048,128]{1,0:T(8,128)(2,1)}, bf16[2048,128]{1,0:T(8,128)(2,1)}, bf16[2048,128]{1,0:T(8,128)(2,1)}, bf16[128,2048]{1,0:T(8,128)(2,1)}, bf...) custom-call(bf16[2048,2048]{1,0:T(8,128)(2,1)} %bitcast.81, f32[1,2048]{1,0:T(1,128)} %reshape.144.gain_ref, ...), custom_call_target="tpu_custom_call" | custom-call | tf_op jit(solution)/shard_map/pallas_call | solution.py:1148
  147.9 1.0 copy-done.1
  149.0 1.0 copy-done.2
  150.0 1.0 copy-done.5
  151.1 33.7 %shard_map.267 = (bf16[32,64,128]{2,1,0:T(8,128)(2,1)S(1)}, f32[1,2048]{1,0:T(1,128)S(1)}) custom-call(bf16[2048,128]{1,0:T(8,128)(2,1)S(1)} %copy-done.1, bf16[2048,128]{1,0:T(8,128)(2,1)S(1)} %copy-done.2, bf16[128,2048]{1,0:T(8,128)(2,1)S(1)} %copy-done.5), custom_call_target="tpu_custom_call" | custom-call | tf_op jit(solution)/shard_map/pallas_call | solution.py:1049
  185.4 0.9 copy.94
  186.4 4.8 multiply_reduce_fusion
  191.1 1.2 multiply_convert_fusion
  192.3 113.6 %shard_map.268 = (bf16[32,2,64,2048]{3,2,1,0:T(8,128)(2,1)}, bf16[8,640,512]{2,1,0:T(8,128)(2,1)}, f32[8,640,128]{2,1,0:T(8,128)}) custom-call(bf16[2,64,2048]{2,1,0:T(8,128)(2,1)} %bitcast.96, s32[8,8,512]{2,1,0:T(8,128)} %bitcast.109, f32[8,8,512]{2,1,0:T(8,128)} %bitcast.108), custom_call_target="tpu_custom_call" | custom-call | tf_op jit(solution)/shard_map/pallas_call | solution.py:376
  306.0 36.3 %shard_map.269 = (bf16[8,640,2048]{2,1,0:T(8,128)(2,1)}, bf16[8,640,2048]{2,1,0:T(8,128)(2,1)}) custom-call(bf16[8,640,512]{2,1,0:T(8,128)(2,1)} %get-tuple-element.63.hot_ref.hot, f32[8,640,128]{2,1,0:T(8,128)} %get-tuple-element.64.rg_ref, bf16[2,2,4,2,128,2048]{5,4,3,2,1,0:T(8,128)(2,1)} %bitcast.84, bf16[2,2,4,2,128,2048]{5,4,3,2,1,0:T(8,128)(2,1)} %bitcast.83), custom_call_target="tpu_custom_call" | custom-call | tf_op jit(solution)/shard_map/pallas_call | solution.py:1248
  342.3 66.4 %shard_map.270 = (bf16[8,640,2048]{2,1,0:T(8,128)(2,1)}, bf16[8,640,2048]{2,1,0:T(8,128)(2,1)}, f32[8,2048,256]{2,1,0:T(8,128)}, f32[8,2048,256]{2,1,0:T(8,128)}, f32[8,256,2048]{2,1,0:T(8,128)}) custom-call(bf16[8,640,2048]{2,1,0:T(8,128)(2,1)} %get-tuple-element.66.x_ref, bf16[8,640,2048]{2,1,0:T(8,128)(2,1)} %get-tuple-element.67.pg_ref, ...), custom_call_target="tpu_custom_call" | custom-call | tf_op jit(solution)/shard_map/pallas_call | solution.py:1298
  408.7 157.6 %shard_map.271 = (f32[2,64,2048]{2,1,0:T(8,128)}, f32[2,64,2048]{2,1,0:T(8,128)}) custom-call(bf16[8,640,2048]{2,1,0:T(8,128)(2,1)} %get-tuple-element.68.a, bf16[8,640,2048]{2,1,0:T(8,128)(2,1)} %get-tuple-element.69.b, bf16[8,640,512]{2,1,0:T(8,128)(2,1)} %get-tuple-element.63.hot_ref.hot), custom_call_target="tpu_custom_call" | custom-call | tf_op jit(solution)/shard_map/pallas_call | solution.py:805
  566.4 1.3 fusion.2
  567.7 1.3 copy.95
  569.0 11.5 %shard_map.272 = (f32[128,2048]{1,0:T(8,128)}, f32[8,2048]{1,0:T(8,128)}, bf16[2,16,64,128]{3,2,1,0:T(8,128)(2,1)}, bf16[2048,2048]{1,0:T(8,128)(2,1)}) custom-call(f32[128,2048]{1,0:T(8,128)} %copy-done.10, f32[1,2048]{1,0:T(1,128)} %reshape.155.gain_ref, f32[128,2048]{1,0:T(8,128)} %bitcast.101, bf16[128,2048]{1,0:T(8,128)(2,1)} %bitcast.92, ...), custom_call_target="tpu_custom_call" | custom-call | tf_op jit(solution)/shard_map/pallas_call | solution.py:1340
  580.5 31.1 %shard_map.273 = (f32[2048,128]{1,0:T(8,128)}, f32[2048,128]{1,0:T(8,128)}, f32[2048,128]{1,0:T(8,128)}) custom-call(bf16[32,64,128]{2,1,0:T(8,128)(2,1)} %bitcast.103, bf16[2048,128]{1,0:T(8,128)(2,1)} %get-tuple-element.59.q_ref, f32[1,2048]{1,0:T(1,128)} %copy-done.9, bf16[2048,128]{1,0:T(8,128)(2,1)} %get-tuple-element.60.k_ref, ...), custom_call_target="tpu_custom_call" | custom-call | tf_op jit(solution)/shard_map/pallas_call | solution.py:1111
  611.6 19.6 %shard_map.274 = (bf16[2048,2048]{1,0:T(8,128)(2,1)}, bf16[2048,384]{1,0:T(8,128)(2,1)}, f32[8,128]{1,0:T(8,128)}, f32[8,2048]{1,0:T(8,128)}) custom-call(f32[2048,128]{1,0:T(8,128)} %get-tuple-element.76.dq_ref, f32[2048,128]{1,0:T(8,128)} %get-tuple-element.77.dk_ref, f32[2048,128]{1,0:T(8,128)} %get-tuple-element.78.dv_ref, ...), custom_call_target="tpu_custom_call" | custom-call | tf_op jit(solution)/shard_map/pallas_call | solution.py:1206
  631.3 0.8 slice_reduce_fusion.3
  632.1 0.9 slice_reduce_fusion
  633.4 0.7 copy.83
  634.1 102.5 %shard_map.275 = (bf16[16,64,384]{2,1,0:T(8,128)(2,1)}, f32[16,8,128]{2,1,0:T(8,128)}, f32[64,2048]{1,0:T(8,128)}, bf16[64,2048]{1,0:T(8,128)(2,1)}, f32[2,32,2048]{2,1,0:T(8,128)}) custom-call(bf16[2,16,64,384]{3,2,1,0:T(8,128)(2,1)} %bitcast.97, f32[2,16,8,128]{3,2,1,0:T(8,128)} %bitcast.102, bf16[32,64,2048]{2,1,0:T(8,128)(2,1)} %bitcast.86, ...), custom_call_target="tpu_custom_call" | custom-call | tf_op jit(solution)/shard_map/pallas_call | solution.py:947
  736.7 1.1 copy-done.4
  737.8 1.0 copy-done.6
  738.8 0.9 copy-done.7
  739.8 1.5 shard_map.276
  741.3 1.8 copy.78
  743.1 0.9 reduce_sum.49
  744.1 0.6 fusion.9
  744.7 0.6 slice.70
  745.2 1.9 copy.100
  (54 shorter events, 3.7 us)
Async XLA Ops:
  7.2 126.0 %copy-start.11 = (s32[2,2,4,2]{3,2,1,0:T(4,128)S(1)}, s32[2,2,4,2]{3,2,1,0:T(4,128)}, u32[]{:S(2)}) copy-start(s32[2,2,4,2]{3,2,1,0:T(4,128)} %constant.60) | copy-start | bytes 388
  7.2 179.2 %all-gather.4.cloned.1.call-start = ((), (), s32[]{:S(2)}) async-start(), calls=%async_computation | async-start | bytes 8650752 | tf_op jit(solution)/shard_map/all_gather | solution.py:1417
  7.9 298.0 %all-gather.6.cloned.1.call-start = ((), (), s32[]{:S(2)}) async-start(), calls=%async_computation.1 | async-start | bytes 17301504 | tf_op jit(solution)/shard_map/all_gather | solution.py:1418
  133.1 53.2 %copy-start = (bf16[64,2,2048]{2,0,1:T(8,128)(2,1)S(1)}, bf16[64,2,2048]{2,0,1:T(8,128)(2,1)}, u32[]{:S(2)}) copy-start(bf16[64,2,2048]{2,0,1:T(8,128)(2,1)} %copy.97) | copy-start | bytes 1572868
  147.9 1.0 copy-start.1
  149.0 1.0 copy-start.2
  150.0 1.0 copy-start.5
  184.8 0.6 copy-start.9
  191.1 375.2 %copy-start.10 = (f32[128,2048]{1,0:T(8,128)}, f32[128,2048]{1,0:T(8,128)S(1)}, u32[]{:S(2)}) copy-start(f32[128,2048]{1,0:T(8,128)S(1)} %get-tuple-element.165.res_ref) | copy-start | bytes 3145732
  634.1 102.5 %copy-start.3 = (f32[128,2048]{1,0:T(8,128)S(1)}, f32[128,2048]{1,0:T(8,128)}, u32[]{:S(2)}) copy-start(f32[128,2048]{1,0:T(8,128)} %get-tuple-element.90) | copy-start | bytes 3145732
  634.1 102.6 %copy-start.8 = (f32[1,2048]{1,0:T(1,128)S(1)}, f32[1,2048]{1,0:T(1,128)}, u32[]{:S(2)}) copy-start(f32[1,2048]{1,0:T(1,128)} %reshape.144.gain_ref) | copy-start | bytes 24580
  736.7 1.1 copy-start.4
  737.8 1.0 copy-start.6
  738.8 0.9 copy-start.7
Sparse Core Ops, SparseCore 0:
  11.0 109.7 all-gather.3
  123.9 143.8 all-gather.5
